TPU v7x, 128 devices: a whole 4x4x4 slice. The times are simulated.
128 devices in a mesh: group: 16 (over y, x), local: 8 (over z, core).
Axes of the slice: x: 4, y: 4, z: 4, core: 2. Of those that a mesh axis runs over, the one named last changes fastest.
Arguments:
- grad_out: bfloat16 [2048, 7168], P('group', 'local'), may hold values from -6 to 6
- combine_weight: float32 [2048, 8], P('group'), may hold values from 0.1 to 1
- token_groups: int32 [2048, 4], P('group'), may hold values from 0 to 15, all different within a row; in each aligned block of 128 rows (0 to 127, 128 to 255, ...) at most 64 rows name the same one
- expert_pick: int32 [2048, 8], P('group'), may hold values from 0 to 11, as said below
- saved_gate: bfloat16 [48, 1024, 1024], P('group', None, 'local'), may hold values from -6 to 6
- saved_up: bfloat16 [48, 1024, 1024], P('group', None, 'local'), may hold values from -6 to 6
- w_gate: bfloat16 [48, 7168, 1024], P('group', None, 'local'), may hold values from -0.25 to 0.25
- w_up: bfloat16 [48, 7168, 1024], P('group', None, 'local'), may hold values from -0.1875 to 0.1875
- w_down: bfloat16 [48, 1024, 7168], P('group', 'local'), may hold values from -0.0625 to 0.0625
Outputs:
- grad_in: bfloat16 [2048, 7168], P('group', 'local')
Inputs may be any that keep to these rules, and one draw needn't show every extreme that they name: `token_groups`: each row names 4 different groups; within the rows of one index of group no group is named by more than 64 rows, a bound that some block reaches. `expert_pick`: each row names 8 different slots; slot v stands for expert v % 3 of the group token_groups[row, v // 3], and each of the row's 4 groups is named by at least one slot.
All inputs are finite; a program needn't handle non-finite values.
Results may differ from a plain program's by a relative error of at most 0.017.
Values may be sent and summed in bfloat16 or wider, within the bound.
No kernel may reach another device: no remote copies, remote signals or barrier semaphores. Data moves between devices by JAX's collectives and lax.ppermute only.
A program may use at most 128 MiB of HBM per device.

v0:
```python
import jax
import jax.numpy as jnp
from jax import lax
from jax.sharding import PartitionSpec as P

EXP_GRP = 3


def dispatch_tables(token_groups, expert_pick, combine_weight, group_count, slot_count):
    group_ids = jnp.arange(group_count, dtype=jnp.int32)
    member = jnp.any(token_groups[:, :, None] == group_ids[None, None, :], axis=1).astype(jnp.int32)
    slot_index = jnp.cumsum(member, axis=0) - member
    slot_ids = jnp.arange(slot_count, dtype=jnp.int32)
    routing_table = (
        (member.T[:, None, :] == 1) & (slot_index.T[:, None, :] == slot_ids[None, :, None])
    ).astype(jnp.float32)
    chosen = jnp.take_along_axis(token_groups, expert_pick // EXP_GRP, axis=1)
    within = expert_pick % EXP_GRP
    group_hot = (chosen[:, :, None] == group_ids[None, None, :]).astype(jnp.float32)
    expert_hot = (within[:, :, None] == jnp.arange(EXP_GRP, dtype=jnp.int32)[None, None, :]).astype(
        jnp.float32
    )
    spread = jnp.einsum(
        "tk,tkg,tkj->tgj", combine_weight, group_hot, expert_hot, precision=lax.Precision.HIGHEST
    )
    lane_weights = jnp.einsum(
        "gct,tgj->gcj", routing_table, spread, precision=lax.Precision.HIGHEST
    ).astype(jnp.bfloat16)
    return (routing_table, lane_weights)


def expert_grads(hidden_grad, lane_cols, saved_gate, saved_up):
    scaled = hidden_grad * lane_cols
    gate_value = saved_gate.astype(jnp.float32)
    up_value = saved_up.astype(jnp.float32)
    sigmoid_gate = jax.nn.sigmoid(gate_value)
    grad_gate = (
        scaled * up_value * sigmoid_gate * (1.0 + gate_value * (1.0 - sigmoid_gate))
    ).astype(jnp.bfloat16)
    grad_up = (scaled * gate_value * sigmoid_gate).astype(jnp.bfloat16)
    return (grad_gate, grad_up)


def on_device(
    grad_out, combine_weight, token_groups, expert_pick, saved_gate, saved_up, w_gate, w_up, w_down
):
    group_count = lax.axis_size("group")
    local_count = lax.axis_size("local")
    tok_rows = grad_out.shape[0]
    feat_width = grad_out.shape[1]
    slot_count = tok_rows // 2
    expert_count = w_gate.shape[0]
    hidden_count = w_gate.shape[2]
    row_total = group_count * slot_count
    routing_table, lane_weights = dispatch_tables(
        token_groups, expert_pick, combine_weight, group_count, slot_count
    )
    outgoing = jnp.einsum(
        "gct,td->gcd",
        routing_table.astype(jnp.bfloat16),
        grad_out,
        preferred_element_type=jnp.float32,
    ).astype(jnp.bfloat16)
    wide_feat = jnp.broadcast_to(
        outgoing[:, None], (group_count, local_count, slot_count, feat_width)
    )
    wide_feat = wide_feat.reshape(group_count * local_count, slot_count, feat_width)
    wide_lane = jnp.broadcast_to(
        lane_weights[:, None], (group_count, local_count, slot_count, EXP_GRP)
    )
    wide_lane = wide_lane.reshape(group_count * local_count, slot_count, EXP_GRP)
    arrived, arrived_lane = (
        lax.all_to_all(wide_feat, ("group", "local"), split_axis=0, concat_axis=0, tiled=True),
        lax.all_to_all(wide_lane, ("group", "local"), split_axis=0, concat_axis=0, tiled=True),
    )
    arrived = arrived.reshape(group_count, local_count, slot_count, feat_width)
    lane_rows = arrived_lane.reshape(group_count, local_count, slot_count, EXP_GRP)[:, 0]
    down_split = w_down.reshape(expert_count, hidden_count, local_count, feat_width)
    hidden_grad = jnp.einsum(
        "glcd,ehld->egch", arrived, down_split, preferred_element_type=jnp.float32
    )
    hidden_grad = hidden_grad.reshape(expert_count, row_total, hidden_count)
    lane_cols = jnp.transpose(lane_rows.reshape(row_total, EXP_GRP).astype(jnp.float32))[:, :, None]
    grad_gate, grad_up = expert_grads(hidden_grad, lane_cols, saved_gate, saved_up)
    flat_table = routing_table.reshape(row_total, tok_rows)
    gate_split = w_gate.reshape(expert_count, local_count, feat_width, hidden_count)
    up_split = w_up.reshape(expert_count, local_count, feat_width, hidden_count)
    gate_rows = grad_gate.reshape(expert_count, group_count, slot_count, hidden_count)
    up_rows = grad_up.reshape(expert_count, group_count, slot_count, hidden_count)
    partial_term = jnp.einsum(
        "egch,eldh->glcd", gate_rows, gate_split, preferred_element_type=jnp.float32
    )
    partial_term = partial_term + jnp.einsum(
        "egch,eldh->glcd", up_rows, up_split, preferred_element_type=jnp.float32
    )
    partial_term = partial_term.astype(jnp.bfloat16).reshape(
        group_count * local_count, slot_count, feat_width
    )
    returned = lax.all_to_all(
        partial_term, ("group", "local"), split_axis=0, concat_axis=0, tiled=True
    )
    summed = jnp.sum(
        returned.reshape(group_count, local_count, slot_count, feat_width),
        axis=1,
        dtype=jnp.float32,
    )
    summed = summed.reshape(row_total, feat_width)
    input_grad = jnp.einsum("rt,rd->td", flat_table, summed, precision=lax.Precision.HIGHEST)
    return input_grad.astype(jnp.bfloat16)


def solution(mesh):
    placed = (
        P("group", "local"),
        P("group", None),
        P("group", None),
        P("group", None),
        P("group", None, "local"),
        P("group", None, "local"),
        P("group", None, "local"),
        P("group", None, "local"),
        P("group", "local", None),
    )
    return jax.shard_map(
        on_device, mesh=mesh, in_specs=placed, out_specs=P("group", "local"), check_vma=False
    )
```

profile of v0, /device:TPU:0, one launch (start us, length us, event | category | flops | bytes accessed | tf_op | source)
XLA Modules:
  0.0 463.8 jit_solution(999303217798136392)
XLA Ops:
  0.0 0.8 fusion.36
  0.8 0.7 bitcast_or_fusion
  1.5 0.1 copy.75
  1.6 0.1 copy.80
  1.7 0.1 reshape.73
  1.8 8.7 %gather_fusion = s32[1024]{0:T(1024)S(1)} fusion(s32[128,4]{0,1:T(4,128)S(1)} %copy-done.2, s32[1024]{0:T(1024)S(1)} %reshape.73), kind=kCustom, calls=%fused_computation | custom fusion | bytes 16384 | tf_op jit(solution)/shard_map/jit(take_along_axis)/gather | solution.py:17
  10.5 0.1 reshape.76
  10.7 0.1 copy.83
  10.8 0.1 copy.82
  10.9 0.1 copy.84
  11.0 0.6 fusion.23
  11.6 0.1 copy.85
  11.8 0.1 copy.76
  11.9 0.2 reduce_window_sum.11
  12.1 0.5 convolution_convert_fusion.1
  12.6 0.7 broadcast_in_dim.10
  13.3 11.1 %all-to-all-start.1 = ((bf16[128,64,3]{1,2,0:T(4,128)(2,1)}), bf16[128,64,3]{1,2,0:T(4,128)(2,1)S(1)}, u32[]{:S(2)}, u32[]{:S(2)}) async-start(bf16[128,64,3]{1,2,0:T(4,128)(2,1)} %bitcast.13), calls=%async_computation.1 | async-start | bytes 262144 | tf_op jit(solution)/shard_map/all_to_all | solution.py:74
  24.5 0.6 convolution_convert_fusion
  25.1 9.0 %all-to-all-done.1 = bf16[128,64,3]{1,2,0:T(4,128)(2,1)S(1)} async-done(((bf16[128,64,3]{1,2,0:T(4,128)(2,1)}), bf16[128,64,3]{1,2,0:T(4,128)(2,1)S(1)}, u32[]{:S(2)}, u32[]{:S(2)}) %all-to-all-start.1) | async-done | bytes 49184 | tf_op jit(solution)/shard_map/all_to_all | solution.py:74
  34.1 6.1 %broadcast_in_dim.8 = bf16[16,8,64,896]{3,2,1,0:T(8,128)(2,1)} broadcast(bf16[16,64,896]{2,1,0:T(8,128)(2,1)S(1)} %convolution_convert_fusion), dimensions={0,2,3} | broadcast | bytes 16515072 | tf_op jit(solution)/shard_map/broadcast_in_dim | solution.py:64
  40.2 5.9 %all-to-all-start = ((bf16[128,64,896]{2,1,0:T(8,128)(2,1)}), bf16[128,64,896]{2,1,0:T(8,128)(2,1)}, u32[]{:S(2)}, u32[]{:S(2)}) async-start(bf16[128,64,896]{2,1,0:T(8,128)(2,1)} %bitcast.81), calls=%async_computation | async-start | bytes 29360128 | tf_op jit(solution)/shard_map/all_to_all | solution.py:73
  46.2 0.1 fusion.37
  46.3 0.1 reshape.72
  46.3 193.0 %all-to-all-done = bf16[128,64,896]{2,1,0:T(8,128)(2,1)} async-done(((bf16[128,64,896]{2,1,0:T(8,128)(2,1)}), bf16[128,64,896]{2,1,0:T(8,128)(2,1)}, u32[]{:S(2)}, u32[]{:S(2)}) %all-to-all-start) | async-done | bytes 14680096 | tf_op jit(solution)/shard_map/all_to_all | solution.py:73
  239.4 12.0 %fusion.16 = f32[3,16,64,128]{3,2,0,1:T(8,128)S(1)} fusion(bf16[16,8,64,896,1]{3,2,1,4,0:T(8,128)(2,1)} %bitcast.6, bf16[3,16,8,8,896]{4,3,2,1,0:T(8,128)(2,1)} %bitcast.93), kind=kOutput, calls=%fused_computation.25 | convolution fusion | flops 5637144576 | bytes 21757952 | tf_op jit(solution)/shard_map/glcd,ehld->egch/dot_general | solution.py:79
  251.4 0.1 copy.79
  251.6 1.8 fusion.15
  253.4 13.7 %fusion.4 = f32[16,64,8,896,1]{3,1,4,2,0:T(8,128)} fusion(bf16[3,8,896,128]{3,2,1,0:T(8,128)(2,1)S(1)} %bitcast.85, bf16[3,16,64,128,1]{3,2,1,0,4:T(8,128)(2,1)S(1)} %bitcast.89), kind=kOutput, calls=%fused_computation.8 | convolution fusion | flops 5637144576 | bytes 35651584 | tf_op jit(solution)/shard_map/egch,eldh->glcd/dot_general | solution.py:90
  267.1 13.1 %fusion = bf16[16,64,8,896]{3,1,2,0:T(8,128)(2,1)S(1)} fusion(f32[16,64,8,896,1]{3,1,4,2,0:T(8,128)} %fusion.4, bf16[3,8,896,128]{3,2,1,0:T(8,128)(2,1)S(1)} %bitcast.88, bf16[3,16,64,128,1]{3,2,1,0,4:T(8,128)(2,1)} %bitcast.90), kind=kOutput, calls=%fused_computation.3 | convolution fusion | flops 5651824640 | bytes 50331648 | tf_op jit(solution)/shard_map/egch,eldh->glcd/dot_general | solution.py:93
  280.2 178.3 %all_to_all.15 = bf16[128,64,896]{2,1,0:T(8,128)(2,1)S(1)} all-to-all(bf16[128,64,896]{2,1,0:T(8,128)(2,1)S(1)} %bitcast.82), channel_id=1, replica_groups=mesh['group'=16,'local'=8] {'group','local'}, dimensions={0} | all-to-all | bytes 29360128 | tf_op jit(solution)/shard_map/all_to_all | solution.py:99
  458.5 3.0 convert_reduce_fusion
  461.5 2.3 fusion.17
  (30 shorter events, 0.2 us)
Async XLA Ops:
  0.0 24.5 %copy-start = (bf16[128,896]{1,0:T(8,128)(2,1)S(1)}, bf16[128,896]{1,0:T(8,128)(2,1)}, u32[]{:S(2)}) copy-start(bf16[128,896]{1,0:T(8,128)(2,1)} %param.9) | copy-start | bytes 688132
  0.0 1.8 copy-start.2
  1.8 8.8 %copy-start.5 = (s32[128,8]{0,1:T(8,128)S(1)}, s32[128,8]{0,1:T(8,128)}, u32[]{:S(2)}) copy-start(s32[128,8]{0,1:T(8,128)} %param.12) | copy-start | bytes 12292
  1.8 9.1 %copy-start.6 = (f32[128,8]{0,1:T(8,128)S(1)}, f32[128,8]{0,1:T(8,128)}, u32[]{:S(2)}) copy-start(f32[128,8]{0,1:T(8,128)} %param.10) | copy-start | bytes 12292
  13.3 20.8 %all-to-all-start.1 = ((bf16[128,64,3]{1,2,0:T(4,128)(2,1)}), bf16[128,64,3]{1,2,0:T(4,128)(2,1)S(1)}, u32[]{:S(2)}, u32[]{:S(2)}) async-start(bf16[128,64,3]{1,2,0:T(4,128)(2,1)} %bitcast.13), calls=%async_computation.1 | async-start | bytes 262144 | tf_op jit(solution)/shard_map/all_to_all | solution.py:74
  40.2 199.2 %all-to-all-start = ((bf16[128,64,896]{2,1,0:T(8,128)(2,1)}), bf16[128,64,896]{2,1,0:T(8,128)(2,1)}, u32[]{:S(2)}, u32[]{:S(2)}) async-start(bf16[128,64,896]{2,1,0:T(8,128)(2,1)} %bitcast.81), calls=%async_computation | async-start | bytes 29360128 | tf_op jit(solution)/shard_map/all_to_all | solution.py:73
  239.4 14.0 %slice-start = ((s8[5505024]{0:T(1024)(128)(4,1)}), s8[4194304]{0:T(1024)(128)(4,1)S(1)}, s32[]{:S(2)}) async-start(s8[5505024]{0:T(1024)(128)(4,1)} %bitcast.83), calls=%async_computation.3 | async-start | bytes 8388608
  239.4 12.1 %copy-start.3 = (bf16[3,1024,128]{2,1,0:T(8,128)(2,1)S(1)}, bf16[3,1024,128]{2,1,0:T(8,128)(2,1)}, u32[]{:S(2)}) copy-start(bf16[3,1024,128]{2,1,0:T(8,128)(2,1)} %param.13) | copy-start | bytes 2359300
  239.4 12.1 %copy-start.4 = (bf16[3,1024,128]{2,1,0:T(8,128)(2,1)S(1)}, bf16[3,1024,128]{2,1,0:T(8,128)(2,1)}, u32[]{:S(2)}) copy-start(bf16[3,1024,128]{2,1,0:T(8,128)(2,1)} %param.14) | copy-start | bytes 2359300
  239.4 14.0 %slice-start.1 = ((s8[5505024]{0:T(1024)(128)(4,1)}), s8[1310720]{0:T(1024)(128)(4,1)S(1)}, s32[]{:S(2)}) async-start(s8[5505024]{0:T(1024)(128)(4,1)} %bitcast.83), calls=%async_computation.4 | async-start | bytes 2621440
  251.5 15.5 %slice-start.2 = ((s8[5505024]{0:T(1024)(128)(4,1)}), s8[4194304]{0:T(1024)(128)(4,1)S(1)}, s32[]{:S(2)}) async-start(s8[5505024]{0:T(1024)(128)(4,1)} %bitcast.86), calls=%async_computation.5 | async-start | bytes 8388608
  253.4 13.7 %slice-start.3 = ((s8[5505024]{0:T(1024)(128)(4,1)}), s8[1310720]{0:T(1024)(128)(4,1)S(1)}, s32[]{:S(2)}) async-start(s8[5505024]{0:T(1024)(128)(4,1)} %bitcast.86), calls=%async_computation.6 | async-start | bytes 2621440
  458.5 5.3 %copy-start.1 = (bf16[128,896]{1,0:T(8,128)(2,1)S(1)}, bf16[128,896]{1,0:T(8,128)(2,1)}, u32[]{:S(2)}) copy-start(bf16[128,896]{1,0:T(8,128)(2,1)} %param.9) | copy-start | bytes 688132
where the time goes:
time: 465 us; the launch traced here: 464 us
  waiting for transfers between devices  202 us (43%)
  blocking collectives  178 us (38%)
  matrix products  42.9 us (9%)
  starting transfers between devices  17.1 us (4%)
  local copies, waits for them, and re-layouts  16.7 us (4%)
  other arithmetic  6.6 us (1%)
    all_to_all x1, waiting for transfers between devices, on_device(): lax.all_to_all(wide_feat, ('group', 'local'), split_axis=0, concat_axis=0...  193 us
    all_to_all x1, blocking collectives, on_device(): lax.all_to_all(partial_term, ('group', 'local'), split_axis=0, concat_axi...  178 us
    dot_general x1, matrix products, on_device(): jnp.einsum('egch,eldh->glcd', gate_rows, gate_split, preferred_element_ty...  13.7 us
    dot_general x1, matrix products, on_device(): jnp.einsum('egch,eldh->glcd', up_rows, up_split, preferred_element_type=j...  13.1 us
    dot_general x1, matrix products, on_device(): jnp.einsum('glcd,ehld->egch', arrived, down_split, preferred_element_type...  12 us
    all_to_all x1, starting transfers between devices, on_device(): lax.all_to_all(wide_lane, ('group', 'local'), split_axis=0, concat_axis=0...  11.1 us
  transfers between devices with their start and end apart: 2, of which 2 were waited for; matrix products, arithmetic and copies ran while one was open for 0% of the time, Pallas kernels for 0%

commit v1 on v0

v1 whole, which is shorter than its diff:
```python
import jax
import jax.numpy as jnp
from jax import lax
from jax.experimental import pallas as pl
from jax.experimental.pallas import tpu as pltpu
from jax.sharding import PartitionSpec as P

EXP_GRP = 3
CAP = 64
LANE_ROWS = 8
Z_LAST = (0, 32)
Z_FIRST = ((32, 16), (48, 16))
Z_OFFSETS = (0, -1, 1, 2)
VMEM = 40 * 1024 * 1024
BF = jnp.bfloat16
F32 = jnp.float32
NT = (((1,), (1,)), ((), ()))
TN = (((0,), (0,)), ((), ()))


def params(limit=VMEM):
    return pltpu.CompilerParams(vmem_limit_bytes=limit)


def cost(flops, nbytes):
    return pl.CostEstimate(flops=int(flops), bytes_accessed=int(nbytes), transcendentals=0)


def routing_kernel(groups_ref, picks_ref, weights_ref, tok_ref, table_ref, out_ref):
    group_count, slots, tok_rows = table_ref.shape
    first = out_ref.shape[1] - LANE_ROWS
    groups = groups_ref[...]
    picks = picks_ref[...]
    weights = weights_ref[...]
    ids = lax.broadcasted_iota(jnp.int32, (group_count, tok_rows), 0)
    member = jnp.zeros((group_count, tok_rows), jnp.bool_)
    for q in range(groups.shape[0]):
        member = member | (ids == groups[q : q + 1, :])
    earlier = lax.broadcasted_iota(jnp.int32, (tok_rows, tok_rows), 0) < lax.broadcasted_iota(
        jnp.int32, (tok_rows, tok_rows), 1
    )
    slot = jnp.dot(
        member.astype(F32).astype(BF), earlier.astype(F32).astype(BF), preferred_element_type=F32
    ).astype(jnp.int32)
    slot = jnp.where(member, slot, -1)
    slot_ids = lax.broadcasted_iota(jnp.int32, (group_count, slots, tok_rows), 1)
    table = (slot[:, None, :] == slot_ids).astype(F32).astype(BF)
    table_ref[...] = table

    shape = (group_count, LANE_ROWS, tok_rows)
    group_ids = lax.broadcasted_iota(jnp.int32, shape, 0)
    expert_ids = lax.broadcasted_iota(jnp.int32, shape, 1)
    spread = jnp.zeros(shape, F32)
    for k in range(picks.shape[0]):
        pick = picks[k : k + 1, :]
        chosen = jnp.zeros_like(pick)
        for q in range(groups.shape[0]):
            inside = (pick >= q * EXP_GRP) & (pick < (q + 1) * EXP_GRP)
            chosen = chosen + jnp.where(inside, groups[q : q + 1, :] * EXP_GRP + pick - q * EXP_GRP, 0)
        hit = group_ids * EXP_GRP + expert_ids == chosen[:, None, :]
        hit = hit & (expert_ids < EXP_GRP)
        spread = spread + jnp.where(hit, weights[k : k + 1, :][:, None, :], 0.0)
    spread = spread.astype(BF)

    width = out_ref.shape[2]
    rows = jnp.dot(
        table[:, :first].reshape(group_count * first, tok_rows), tok_ref[...], preferred_element_type=F32
    ).astype(BF)
    out_ref[:, :first, :] = rows.reshape(group_count, first, width)
    out_ref[:, first:, :] = jnp.zeros((group_count, LANE_ROWS, width), BF)
    for g in range(group_count):
        lanes = lax.dot_general(spread[g], table[g], NT, preferred_element_type=F32)
        out_ref[g, first:, :slots] = lanes.astype(BF)


def route(token_groups, expert_pick, combine_weight, tokens, group_count):
    tok_rows, width = tokens.shape
    first = Z_LAST[1]
    return pl.pallas_call(
        routing_kernel,
        out_shape=(
            jax.ShapeDtypeStruct((group_count, CAP, tok_rows), BF),
            jax.ShapeDtypeStruct((group_count, first + LANE_ROWS, width), BF),
        ),
        compiler_params=params(),
        cost_estimate=cost(2 * group_count * first * tok_rows * width, 4e6),
        name="route",
    )(token_groups.T, expert_pick.T, combine_weight.T, tokens)


def spread_kernel(table_ref, t0, t1, t2, t3, out_ref):
    group_count, slots, tok_rows = table_ref.shape
    table = table_ref[...].reshape(group_count * slots, tok_rows)
    for z, tok in enumerate((t0, t1, t2, t3)):
        rows = jnp.dot(table, tok[...], preferred_element_type=F32).astype(BF)
        out_ref[:, z] = rows.reshape(group_count, slots, rows.shape[1])


def spread_tokens(table, tokens):
    group_count, slots, tok_rows = table.shape
    width = tokens[0].shape[1]
    return pl.pallas_call(
        spread_kernel,
        out_shape=jax.ShapeDtypeStruct((group_count, len(tokens), slots, width), BF),
        compiler_params=params(),
        cost_estimate=cost(8 * group_count * slots * tok_rows * width, 8 * group_count * slots * width),
        name="spread",
    )(table, *tokens)


def write_grads(hidden, lane_ref, gate_ref, up_ref, out_ref):
    rows = hidden.shape[0]
    units = gate_ref.shape[-1]
    lanes = lane_ref[...].reshape(rows, EXP_GRP)
    for j in range(EXP_GRP):
        scaled = hidden[:, j * units : (j + 1) * units] * lanes[:, j : j + 1]
        p = gate_ref[j].reshape(rows, units).astype(F32)
        q = up_ref[j].reshape(rows, units).astype(F32)
        sg = 1.0 / (1.0 + jnp.exp(-p))
        gate = scaled * q * sg * (1.0 + p * (1.0 - sg))
        up = scaled * p * sg
        out_ref[:, j * units : (j + 1) * units] = gate.astype(BF)
        out_ref[:, (EXP_GRP + j) * units : (EXP_GRP + j + 1) * units] = up.astype(BF)


def hidden_last_kernel(order, x_ref, down_ref, lane_ref, gate_ref, up_ref, out_ref, total):
    step = pl.program_id(0)
    part = lax.dot_general(x_ref[0], down_ref[...], NT, preferred_element_type=F32)

    @pl.when(step == 0)
    def _():
        total[...] = part

    @pl.when(step > 0)
    def _():
        total[...] += part

    @pl.when(step == pl.num_programs(0) - 1)
    def _():
        write_grads(total[...], lane_ref, gate_ref, up_ref, out_ref)


def hidden_first_kernel(order, own_ref, other_ref, down_ref, lane_ref, gate_ref, up_ref, out_ref, total):
    step = pl.program_id(0)
    rows, width = out_ref.shape[0], own_ref.shape[-1]
    half = pl.num_programs(0) // 2

    @pl.when(step == 0)
    def _():
        total[...] = jnp.zeros_like(total)

    @pl.when(step < half)
    def _():
        total[...] += lax.dot_general(
            own_ref[...].reshape(rows, width), down_ref[...], NT, preferred_element_type=F32
        )

    @pl.when(step >= half)
    def _():
        total[...] += lax.dot_general(
            other_ref[...].reshape(rows, width), down_ref[...], NT, preferred_element_type=F32
        )

    @pl.when(step == pl.num_programs(0) - 1)
    def _():
        write_grads(total[...], lane_ref, gate_ref, up_ref, out_ref)


def hidden_grads(order, rows_in, w_down, lanes, saved_gate, saved_up, slots):
    start, count = slots
    units = w_down.shape[0]
    blocks = order.shape[0]
    width = w_down.shape[1] // blocks
    group_count = lanes.shape[0]
    rows = group_count * count
    if len(rows_in) == 1:
        kernel = hidden_last_kernel
        row_specs = [pl.BlockSpec((1, rows, width), lambda i, o: (i, 0, 0))]
    else:
        kernel = hidden_first_kernel
        half = blocks // 2
        row_specs = [
            pl.BlockSpec((group_count, 1, count, width), lambda i, o: (0, jnp.minimum(i, half - 1), 0, 0)),
            pl.BlockSpec((group_count, 1, count, width), lambda i, o: (0, jnp.maximum(i - half, 0), 0, 0)),
        ]
    saved_spec = pl.BlockSpec(
        (EXP_GRP, group_count, count, units // EXP_GRP), lambda i, o: (0, 0, start // count, 0)
    )
    return pl.pallas_call(
        kernel,
        out_shape=jax.ShapeDtypeStruct((rows, 2 * units), BF),
        grid_spec=pltpu.PrefetchScalarGridSpec(
            num_scalar_prefetch=1,
            grid=(blocks,),
            in_specs=row_specs
            + [
                pl.BlockSpec((units, width), lambda i, o: (0, o[i])),
                pl.BlockSpec((group_count, count, EXP_GRP), lambda i, o: (0, start // count, 0)),
                saved_spec,
                saved_spec,
            ],
            out_specs=pl.BlockSpec((rows, 2 * units), lambda i, o: (0, 0)),
            scratch_shapes=[pltpu.VMEM((rows, units), F32)],
        ),
        compiler_params=params(),
        cost_estimate=cost(
            2 * rows * units * blocks * width, 2 * (rows + units) * blocks * width + 8 * rows * units
        ),
        name="hidden",
    )(order, *rows_in, w_down, lanes, saved_gate, saved_up)


def weights_times(grads_ref, gate_ref, up_ref):
    columns = jnp.concatenate(
        [gate_ref[j] for j in range(EXP_GRP)] + [up_ref[j] for j in range(EXP_GRP)], axis=1
    )
    return lax.dot_general(grads_ref[...], columns, NT, preferred_element_type=F32)


def back_last_kernel(order, grads_ref, gate_ref, up_ref, out_ref):
    out_ref[0] = weights_times(grads_ref, gate_ref, up_ref).astype(BF)


def back_first_kernel(order, grads_ref, gate_ref, up_ref, out_ref):
    group_count, _, count, width = out_ref.shape
    part = weights_times(grads_ref, gate_ref, up_ref)
    out_ref[...] = part.astype(BF).reshape(group_count, 1, count, width)


def back_add_kernel(order, grads_ref, gate_ref, up_ref, other_ref, out_ref):
    group_count, _, count, width = out_ref.shape
    part = weights_times(grads_ref, gate_ref, up_ref)
    part = part + other_ref[...].reshape(group_count * count, width).astype(F32)
    out_ref[...] = part.astype(BF).reshape(group_count, 1, count, width)


def back(order, grads, w_gate, w_up, group_count, other=None, last=False):
    rows, depth = grads.shape
    blocks = order.shape[0]
    width = w_gate.shape[1] // (blocks if last else 2 * blocks)
    units = w_gate.shape[2]
    weight_spec = pl.BlockSpec((EXP_GRP, width, units), lambda i, o: (0, o[i], 0))
    in_specs = [pl.BlockSpec((rows, depth), lambda i, o: (0, 0)), weight_spec, weight_spec]
    operands = [order, grads, w_gate, w_up]
    if last:
        kernel = back_last_kernel
        out_shape = (blocks, rows, width)
        out_spec = pl.BlockSpec((1, rows, width), lambda i, o: (i, 0, 0))
    else:
        kernel = back_first_kernel
        count = rows // group_count
        out_shape = (group_count, blocks, count, width)
        out_spec = pl.BlockSpec((group_count, 1, count, width), lambda i, o: (0, i, 0, 0))
        if other is not None:
            kernel = back_add_kernel
            in_specs.append(out_spec)
            operands.append(other)
    return pl.pallas_call(
        kernel,
        out_shape=jax.ShapeDtypeStruct(out_shape, BF),
        grid_spec=pltpu.PrefetchScalarGridSpec(
            num_scalar_prefetch=1, grid=(blocks,), in_specs=in_specs, out_specs=out_spec
        ),
        compiler_params=params(),
        cost_estimate=cost(
            2 * rows * depth * blocks * width, 2 * (rows + depth) * blocks * width + 2 * rows * depth
        ),
        name="back",
    )(*operands)


def collect_kernel(*refs):
    count = len(Z_FIRST)
    tables, arrived, outs = refs[:count], refs[count : 2 * count], refs[2 * count :]
    group_count, slots, tok_rows = tables[0].shape
    width = arrived[0].shape[-1]
    for z, out in enumerate(outs):
        total = jnp.zeros((tok_rows, width), F32)
        for table, rows in zip(tables, arrived):
            total = total + lax.dot_general(
                table[...].reshape(group_count * slots, tok_rows),
                rows[:, z].reshape(group_count * slots, width),
                TN,
                preferred_element_type=F32,
            )
        out[...] = total.astype(out.dtype)


def collect(tables, arrived):
    group_count, slots, tok_rows = tables[0].shape
    width = arrived[0].shape[-1]
    return pl.pallas_call(
        collect_kernel,
        out_shape=tuple(
            jax.ShapeDtypeStruct((tok_rows, width), F32 if z == 0 else BF) for z in range(len(Z_OFFSETS))
        ),
        compiler_params=params(),
        cost_estimate=cost(16 * group_count * slots * tok_rows * width, 16 * group_count * slots * width),
        name="collect",
    )(*tables, *arrived)


def finish_kernel(table_ref, rows_ref, own_ref, a_ref, b_ref, c_ref, out_ref):
    group_count, slots, tok_rows = table_ref.shape
    width = rows_ref.shape[-1]
    total = lax.dot_general(
        table_ref[...].reshape(group_count * slots, tok_rows),
        rows_ref[...].reshape(group_count * slots, width),
        TN,
        preferred_element_type=F32,
    )
    total = total + own_ref[...]
    for ref in (a_ref, b_ref, c_ref):
        total = total + ref[...].astype(F32)
    out_ref[...] = total.astype(BF)


def finish(table, rows, own, others):
    tok_rows, width = own.shape
    return pl.pallas_call(
        finish_kernel,
        out_shape=jax.ShapeDtypeStruct((tok_rows, width), BF),
        compiler_params=params(),
        cost_estimate=cost(2 * table.shape[0] * table.shape[1] * tok_rows * width, 3e6),
        name="finish",
    )(table, rows, own, *others)


def on_device(
    grad_out, combine_weight, token_groups, expert_pick, saved_gate, saved_up, w_gate, w_up, w_down
):
    group_count = lax.axis_size("group")
    local_count = lax.axis_size("local")
    chips = local_count // 2
    place = lax.axis_index("local")
    z, core = place // 2, place % 2
    offsets = jnp.array(Z_OFFSETS, jnp.int32)
    own_order = ((z + offsets) % chips) * 2 + core
    other_order = ((z + offsets) % chips) * 2 + 1 - core
    all_order = jnp.arange(local_count, dtype=jnp.int32)

    def shift(value, by):
        pairs = [
            (c * 2 + k, ((c + by) % chips) * 2 + k) for c in range(chips) for k in range(2)
        ]
        return lax.ppermute(value, "local", pairs)

    def swap(value):
        return lax.ppermute(value, "local", [(i, i ^ 1) for i in range(local_count)])

    def exchange(value):
        return lax.all_to_all(value, "group", split_axis=0, concat_axis=0, tiled=True)

    units = w_gate.shape[2]
    down = w_down.reshape(EXP_GRP * units, w_down.shape[2])
    gate_slots = saved_gate.reshape(EXP_GRP, group_count, CAP, units)
    up_slots = saved_up.reshape(EXP_GRP, group_count, CAP, units)

    blocks = [grad_out] + [shift(grad_out, -by) for by in Z_OFFSETS[1:]]
    table, first_out = route(token_groups, expert_pick, combine_weight, grad_out, group_count)
    first_count = Z_LAST[1]
    first_in = exchange(first_out)
    lanes = jnp.transpose(first_in[:, first_count : first_count + EXP_GRP, :CAP], (0, 2, 1)).astype(F32)
    width = grad_out.shape[1]
    last_rows = lax.all_gather(
        first_in[:, :first_count].reshape(group_count * first_count, width), "local", axis=0, tiled=False
    )

    tables = [table[:, start : start + count] for start, count in Z_FIRST]
    own = [exchange(spread_tokens(t, blocks)) for t in tables]
    other = [swap(rows) for rows in own]

    last_grads = hidden_grads(all_order, [last_rows], down, lanes, gate_slots, up_slots, Z_LAST)
    last_part = back(all_order, last_grads, w_gate, w_up, group_count, last=True)
    last_sum = lax.psum_scatter(last_part, "local", scatter_dimension=0, tiled=False)

    returned = []
    for slots, mine, theirs in zip(Z_FIRST, own, other):
        grads = hidden_grads(
            jnp.concatenate([own_order, other_order]), [mine, theirs], down, lanes, gate_slots, up_slots, slots
        )
        away = swap(back(other_order, grads, w_gate, w_up, group_count))
        returned.append(exchange(back(own_order, grads, w_gate, w_up, group_count, other=away)))

    last_home = exchange(last_sum.reshape(group_count, first_count, width))
    pieces = collect(tables, returned)
    others = [shift(piece, by) for piece, by in zip(pieces[1:], Z_OFFSETS[1:])]
    return finish(table[:, :first_count], last_home, pieces[0], others)


def solution(mesh):
    placed = (
        P("group", "local"),
        P("group", None),
        P("group", None),
        P("group", None),
        P("group", None, "local"),
        P("group", None, "local"),
        P("group", None, "local"),
        P("group", None, "local"),
        P("group", "local", None),
    )
    return jax.shard_map(
        on_device, mesh=mesh, in_specs=placed, out_specs=P("group", "local"), check_vma=False
    )
```

time: 465 us -> 325 us (0.70)
  blocking collectives: 178 us -> 55.3 us
  waiting for transfers between devices: 202 us -> 140 us
  Pallas kernels: 0 us -> 58.1 us
  matrix products: 42.9 us -> 0 us
  between operations: 0.2 us -> 13.7 us
  local copies, waits for them, and re-layouts: 16.7 us -> 28.7 us
  starting transfers between devices: 17.1 us -> 28.1 us
  other arithmetic: 6.6 us -> 0.1 us
    all_to_all x2 -> x4, waiting for transfers between devices: 202 us -> 75.2 us  [exchange(): lax.all_to_all(value, 'group', split_axis=0, concat_axis=0, tiled=True)]
    all_to_all x1 -> x2, blocking collectives: 178 us -> 55.3 us  [exchange(): lax.all_to_all(value, 'group', split_axis=0, concat_axis=0, tiled=True)]
    pallas_call x0 -> x13, Pallas kernels: none -> 58.1 us  [the longest x5 28.7 us: back(): pl.pallas_call(kernel, out_shape=jax.ShapeDtypeStruct(out_shape, BF), gri...]
    all_gather x0 -> x1, waiting for transfers between devices: none -> 44 us  [on_device(): lax.all_gather(first_in[:, :first_count].reshape(group_count * first_coun...]
    dot_general x7 -> x0, matrix products: 42.9 us -> none  [the longest x1 13.7 us: on_device(): jnp.einsum('egch,eldh->glcd', gate_rows, gate_split, preferred_element_ty...]
    unnamed x23 -> x56, local copies, waits for them, and re-layouts: 0.15 us -> 27.4 us
    ppermute x0 -> x10, waiting for transfers between devices: none -> 20.7 us  [the longest x6 20.7 us: shift(): return lax.ppermute(value, 'local', pairs)]
    ppermute x0 -> x10, starting transfers between devices: none -> 9.16 us  [the longest x6 8.47 us: shift(): return lax.ppermute(value, 'local', pairs)]
  transfers between devices with their start and end apart: 2 -> 16, of which waited for: 2 -> 10; matrix products, arithmetic and copies ran while one was open for 0% -> 0% of each run, Pallas kernels for 0% -> 11%
where the time goes in v1:
time: 325 us; the launch traced here: 324 us
  waiting for transfers between devices  140 us (43%)
  Pallas kernels  58.1 us (18%)
  blocking collectives  55.3 us (17%)
  local copies, waits for them, and re-layouts  28.7 us (9%)
  starting transfers between devices  28.1 us (9%)
  between operations  13.7 us (4%)
    all_to_all x4, waiting for transfers between devices, exchange(): lax.all_to_all(value, 'group', split_axis=0, concat_axis=0, tiled=True)  75.2 us
    all_to_all x2, blocking collectives, exchange(): lax.all_to_all(value, 'group', split_axis=0, concat_axis=0, tiled=True)  55.3 us
    all_gather x1, waiting for transfers between devices, on_device(): lax.all_gather(first_in[:, :first_count].reshape(group_count * first_coun...  44 us
    pallas_call x5, Pallas kernels, back(): pl.pallas_call(kernel, out_shape=jax.ShapeDtypeStruct(out_shape, BF), gri...  28.7 us
    unnamed x56, local copies, waits for them, and re-layouts  27.4 us
    pallas_call x3, Pallas kernels, hidden_grads(): pl.pallas_call(kernel, out_shape=jax.ShapeDtypeStruct((rows, 2 * units),...  24.5 us
    ppermute x6, waiting for transfers between devices, shift(): return lax.ppermute(value, 'local', pairs)  20.7 us
    all_to_all x4, starting transfers between devices, exchange(): lax.all_to_all(value, 'group', split_axis=0, concat_axis=0, tiled=True)  18.9 us
  transfers between devices with their start and end apart: 16, of which 10 were waited for; matrix products, arithmetic and copies ran while one was open for 0% of the time, Pallas kernels for 11%

profile of v1, /device:TPU:0, one launch (start us, length us, event | category | flops | bytes accessed | tf_op | source)
XLA Modules:
  0.0 323.9 jit_solution(14613829456527511776)
XLA Ops:
  10.2 25.1 %all_to_all.30 = bf16[16,40,896]{2,1,0:T(8,128)(2,1)S(1)} all-to-all(bf16[16,40,896]{2,1,0:T(8,128)(2,1)S(1)} %get-tuple-element.12), channel_id=1, replica_groups=mesh['group'=16,'local'=8] {'group'}, dimensions={0} | all-to-all | bytes 2293760 | tf_op jit(solution)/shard_map/all_to_all | solution.py:352
  36.7 44.0 %all-gather.2.cloned.1.call-done.x_ref = bf16[8,512,896]{2,1,0:T(8,128)(2,1)} async-done(((bf16[1,512,896]{2,1,0:T(8,128)(2,1)}), bf16[8,512,896]{2,1,0:T(8,128)(2,1)}) %all-gather.2.cloned.1.call-update) | async-done | bytes 7340048 | tf_op jit(solution)/shard_map/all_gather | solution.py:365
  80.8 2.6 copy-done.4
  83.3 10.2 %hidden.3.grads_ref = bf16[512,768]{1,0:T(8,128)(2,1)S(1)} custom-call(s32[8]{0:T(128)S(1)} %iota.6.order, bf16[8,512,896]{2,1,0:T(8,128)(2,1)} %all-gather.2.cloned.1.call-done.x_ref, bf16[384,7168]{1,0:T(8,128)(2,1)S(1)} %bitcast.13, f32[16,64,3]{2,1,0:T(8,128)S(1)} %bitcast.16, bf16[3,16,64,128]{3,2,1,0:T(8,128)(2,1)S(1)} %bitcast.19, ...), custom_call_target="tpu_custom_call" | custom-call | flops 2818572288 | bytes 14417920 | tf_op jit(solution)/shard_map/hidden/pallas_call | solution.py:189
  93.6 2.6 copy-done.1
  96.1 10.5 %back.5 = bf16[8,512,896]{2,1,0:T(8,128)(2,1)} custom-call(s32[8]{0:T(128)S(1)} %iota.5.order, bf16[512,768]{1,0:T(8,128)(2,1)S(1)} %hidden.3.grads_ref, bf16[3,7168,128]{2,1,0:T(8,128)(2,1)S(1)} %bitcast.10, bf16[3,7168,128]{2,1,0:T(8,128)(2,1)S(1)} %copy-done.1), custom_call_target="tpu_custom_call" | custom-call | flops 5637144576 | bytes 19136512 | tf_op jit(solution)/shard_map/back/pallas_call | solution.py:258
  111.5 6.1 %collective-permute-done.2.t3 = bf16[128,896]{1,0:T(8,128)(2,1)S(1)} collective-permute-done((bf16[128,896]{1,0:T(8,128)(2,1)S(1)}, bf16[128,896]{1,0:T(8,128)(2,1)S(1)}, u32[]{:S(2)}, u32[]{:S(2)}) %collective-permute-start.2) | collective-permute-done | bytes 229408 | tf_op jit(solution)/shard_map/ppermute | solution.py:346
  117.6 3.7 %collective-permute-done.1.t2 = bf16[128,896]{1,0:T(8,128)(2,1)S(1)} collective-permute-done((bf16[128,896]{1,0:T(8,128)(2,1)S(1)}, bf16[128,896]{1,0:T(8,128)(2,1)S(1)}, u32[]{:S(2)}, u32[]{:S(2)}) %collective-permute-start.1) | collective-permute-done | bytes 229408 | tf_op jit(solution)/shard_map/ppermute | solution.py:346
  121.3 2.0 collective-permute-done.t1
  125.1 6.9 %all-to-all-start.2 = ((bf16[16,4,16,896]{3,2,1,0:T(8,128)(2,1)}), bf16[16,4,16,896]{3,2,1,0:T(8,128)(2,1)}, u32[]{:S(2)}, u32[]{:S(2)}) async-start(bf16[16,4,16,896]{3,2,1,0:T(8,128)(2,1)} %spread.2), calls=%async_computation.3 | async-start | bytes 3670016 | tf_op jit(solution)/shard_map/all_to_all | solution.py:352
  134.0 26.6 %all-to-all-done.2.own_ref = bf16[16,4,16,896]{3,2,1,0:T(8,128)(2,1)} async-done(((bf16[16,4,16,896]{3,2,1,0:T(8,128)(2,1)}), bf16[16,4,16,896]{3,2,1,0:T(8,128)(2,1)}, u32[]{:S(2)}, u32[]{:S(2)}) %all-to-all-start.2) | async-done | bytes 1835040 | tf_op jit(solution)/shard_map/all_to_all | solution.py:352
  160.6 4.5 %all-to-all-start.4 = ((bf16[16,4,16,896]{3,2,1,0:T(8,128)(2,1)}), bf16[16,4,16,896]{3,2,1,0:T(8,128)(2,1)}, u32[]{:S(2)}, u32[]{:S(2)}) async-start(bf16[16,4,16,896]{3,2,1,0:T(8,128)(2,1)} %copy-done.7), calls=%async_computation.5 | async-start | bytes 3670016 | tf_op jit(solution)/shard_map/all_to_all | solution.py:352
  165.2 26.7 %all-to-all-done.4.own_ref = bf16[16,4,16,896]{3,2,1,0:T(8,128)(2,1)} async-done(((bf16[16,4,16,896]{3,2,1,0:T(8,128)(2,1)}), bf16[16,4,16,896]{3,2,1,0:T(8,128)(2,1)}, u32[]{:S(2)}, u32[]{:S(2)}) %all-to-all-start.4) | async-done | bytes 1835040 | tf_op jit(solution)/shard_map/all_to_all | solution.py:352
  192.0 2.7 copy-done.5
  194.7 7.6 %hidden.4.grads_ref = bf16[256,768]{1,0:T(8,128)(2,1)S(1)} custom-call(s32[8]{0:T(128)S(1)} %pad_add_fusion.order, bf16[16,4,16,896]{3,2,1,0:T(8,128)(2,1)} %all-to-all-done.2.own_ref, bf16[16,4,16,896]{3,2,1,0:T(8,128)(2,1)} %collective-permute-done.3.other_ref, bf16[384,7168]{1,0:T(8,128)(2,1)S(1)} %bitcast.14, f32[16,64,3]{2,1,0:T(8,128)S(1)} %bitcast.17, ...), custom_call_target="tpu_custom_call" | custom-call | flops 1409286144 | bytes 9961472 | tf_op jit(solution)/shard_map/hidden/pallas_call | solution.py:189
  202.4 2.6 copy-done.2
  204.9 3.6 %back.6 = bf16[16,4,16,896]{3,2,1,0:T(8,128)(2,1)S(1)} custom-call(s32[4]{0:T(128)S(1)} %get-tuple-element.17.order, bf16[256,768]{1,0:T(8,128)(2,1)S(1)} %hidden.4.grads_ref, bf16[3,7168,128]{2,1,0:T(8,128)(2,1)S(1)} %bitcast.12, bf16[3,7168,128]{2,1,0:T(8,128)(2,1)S(1)} %copy-done.2), custom_call_target="tpu_custom_call" | custom-call | flops 1409286144 | bytes 7733248 | tf_op jit(solution)/shard_map/back/pallas_call | solution.py:258
  209.1 2.6 copy-done.6
  211.6 6.7 %hidden.5.grads_ref = bf16[256,768]{1,0:T(8,128)(2,1)S(1)} custom-call(s32[8]{0:T(128)S(1)} %pad_add_fusion.order, bf16[16,4,16,896]{3,2,1,0:T(8,128)(2,1)} %all-to-all-done.4.own_ref, bf16[16,4,16,896]{3,2,1,0:T(8,128)(2,1)S(1)} %collective-permute-done.5.other_ref, bf16[384,7168]{1,0:T(8,128)(2,1)S(1)} %bitcast.15, f32[16,64,3]{2,1,0:T(8,128)S(1)} %bitcast.18, ...), custom_call_target="tpu_custom_call" | custom-call | flops 1409286144 | bytes 9961472 | tf_op jit(solution)/shard_map/hidden/pallas_call | solution.py:189
  218.3 2.6 copy-done.3
  220.9 4.4 %back.8 = bf16[16,4,16,896]{3,2,1,0:T(8,128)(2,1)} custom-call(s32[4]{0:T(128)S(1)} %get-tuple-element.17.order, bf16[256,768]{1,0:T(8,128)(2,1)S(1)} %hidden.5.grads_ref, bf16[3,7168,128]{2,1,0:T(8,128)(2,1)S(1)} %bitcast.12, bf16[3,7168,128]{2,1,0:T(8,128)(2,1)S(1)} %copy-done.3), custom_call_target="tpu_custom_call" | custom-call | flops 1409286144 | bytes 7733248 | tf_op jit(solution)/shard_map/back/pallas_call | solution.py:258
  225.3 5.0 %back.7 = bf16[16,4,16,896]{3,2,1,0:T(8,128)(2,1)S(1)} custom-call(s32[4]{0:T(128)S(1)} %broadcast_add_fusion.order, bf16[256,768]{1,0:T(8,128)(2,1)S(1)} %hidden.4.grads_ref, bf16[3,7168,128]{2,1,0:T(8,128)(2,1)S(1)} %bitcast.12, bf16[3,7168,128]{2,1,0:T(8,128)(2,1)} %up_ref.9, bf16[16,4,16,896]{3,2,1,0:T(8,128)(2,1)S(1)} %collective-permute-done.4.other_ref), custom_call_target="tpu_custom_call" | custom-call | flops 1409286144 | bytes 7733248 | tf_op jit(solution)/shard_map/back/pallas_call | solution.py:258
  231.6 3.8 %all-to-all-start.3 = ((bf16[16,4,16,896]{3,2,1,0:T(8,128)(2,1)}), bf16[16,4,16,896]{3,2,1,0:T(8,128)(2,1)S(1)}, u32[]{:S(2)}, u32[]{:S(2)}) async-start(bf16[16,4,16,896]{3,2,1,0:T(8,128)(2,1)} %copy-done.9), calls=%async_computation.4 | async-start | bytes 3670016 | tf_op jit(solution)/shard_map/all_to_all | solution.py:352
  235.5 2.6 copy-done
  238.0 5.2 %back.9 = bf16[16,4,16,896]{3,2,1,0:T(8,128)(2,1)S(1)} custom-call(s32[4]{0:T(128)S(1)} %broadcast_add_fusion.order, bf16[256,768]{1,0:T(8,128)(2,1)S(1)} %copy-done.14, bf16[3,7168,128]{2,1,0:T(8,128)(2,1)S(1)} %copy-done, bf16[3,7168,128]{2,1,0:T(8,128)(2,1)} %up_ref.9, bf16[16,4,16,896]{3,2,1,0:T(8,128)(2,1)} %collective-permute-done.6.other_ref), custom_call_target="tpu_custom_call" | custom-call | flops 1409286144 | bytes 7733248 | tf_op jit(solution)/shard_map/back/pallas_call | solution.py:258
  244.5 21.9 %all-to-all-done.3.refs_2_ = bf16[16,4,16,896]{3,2,1,0:T(8,128)(2,1)S(1)} async-done(((bf16[16,4,16,896]{3,2,1,0:T(8,128)(2,1)}), bf16[16,4,16,896]{3,2,1,0:T(8,128)(2,1)S(1)}, u32[]{:S(2)}, u32[]{:S(2)}) %all-to-all-start.3) | async-done | bytes 1835040 | tf_op jit(solution)/shard_map/all_to_all | solution.py:352
  266.4 30.2 %all_to_all.31.refs_3_ = bf16[16,4,16,896]{3,2,1,0:T(8,128)(2,1)} all-to-all(bf16[16,4,16,896]{3,2,1,0:T(8,128)(2,1)} %copy-done.10), channel_id=1, replica_groups=mesh['group'=16,'local'=8] {'group'}, dimensions={0} | all-to-all | bytes 3670016 | tf_op jit(solution)/shard_map/all_to_all | solution.py:352
  296.6 3.6 %all-to-all-start.1 = ((bf16[16,32,896]{2,1,0:T(8,128)(2,1)}), bf16[16,32,896]{2,1,0:T(8,128)(2,1)S(1)}, u32[]{:S(2)}, u32[]{:S(2)}) async-start(bf16[16,32,896]{2,1,0:T(8,128)(2,1)} %bitcast.29), calls=%async_computation.2 | async-start | bytes 1835008 | tf_op jit(solution)/shard_map/all_to_all | solution.py:352
  302.6 2.0 collective-permute-start.8
  304.6 2.5 collective-permute-start.9
  307.1 4.0 %collective-permute-done.7.a_ref = bf16[128,896]{1,0:T(8,128)(2,1)S(1)} collective-permute-done((bf16[128,896]{1,0:T(8,128)(2,1)S(1)}, bf16[128,896]{1,0:T(8,128)(2,1)S(1)}, u32[]{:S(2)}, u32[]{:S(2)}) %collective-permute-start.7) | collective-permute-done | bytes 229408 | tf_op jit(solution)/shard_map/ppermute | solution.py:346
  311.7 4.3 %collective-permute-done.9.c_ref = bf16[128,896]{1,0:T(8,128)(2,1)S(1)} collective-permute-done((bf16[128,896]{1,0:T(8,128)(2,1)S(1)}, bf16[128,896]{1,0:T(8,128)(2,1)S(1)}, u32[]{:S(2)}, u32[]{:S(2)}) %collective-permute-start.9) | collective-permute-done | bytes 229408 | tf_op jit(solution)/shard_map/ppermute | solution.py:346
  (86 shorter events, 21.0 us)
Async XLA Ops:
  6.5 74.2 %all-gather.2.cloned.1.call-start = ((), (), s32[]{:S(2)}) async-start(), calls=%async_computation.7 | async-start | bytes 8257536 | tf_op jit(solution)/shard_map/all_gather | solution.py:365
  10.2 26.2 %copy-start.17 = (bf16[16,64,128]{2,1,0:T(8,128)(2,1)}, bf16[16,64,128]{2,1,0:T(8,128)(2,1)S(1)}, u32[]{:S(2)}) copy-start(bf16[16,64,128]{2,1,0:T(8,128)(2,1)S(1)} %get-tuple-element.11) | copy-start | bytes 786436
  35.3 45.5 %copy-start.11 = (bf16[3,1024,128]{2,1,0:T(8,128)(2,1)S(1)}, bf16[3,1024,128]{2,1,0:T(8,128)(2,1)}, u32[]{:S(2)}) copy-start(bf16[3,1024,128]{2,1,0:T(8,128)(2,1)} %param.14) | copy-start | bytes 2359300
  35.3 45.5 %copy-start.12 = (bf16[3,1024,128]{2,1,0:T(8,128)(2,1)S(1)}, bf16[3,1024,128]{2,1,0:T(8,128)(2,1)}, u32[]{:S(2)}) copy-start(bf16[3,1024,128]{2,1,0:T(8,128)(2,1)} %param.15) | copy-start | bytes 2359300
  36.4 260.2 %reduce-scatter.2.cloned.1.call-start = ((), (), s32[]{:S(2)}) async-start(), calls=%async_computation.8 | async-start | bytes 8257536 | tf_op jit(solution)/shard_map/reduce_scatter | solution.py:375
  36.5 57.1 %slice-start = ((s8[5505024]{0:T(1024)(128)(4,1)}), s8[1310720]{0:T(1024)(128)(4,1)S(1)}, s32[]{:S(2)}) async-start(s8[5505024]{0:T(1024)(128)(4,1)} %bitcast.9), calls=%async_computation.9 | async-start | bytes 2621440
  83.3 10.2 %slice-start.1 = ((s8[5505024]{0:T(1024)(128)(4,1)}), s8[4194304]{0:T(1024)(128)(4,1)S(1)}, s32[]{:S(2)}) async-start(s8[5505024]{0:T(1024)(128)(4,1)} %bitcast.9), calls=%async_computation.10 | async-start | bytes 8388608
  93.6 2.6 copy-start.1
  106.7 4.8 %copy-start.18 = (bf16[16,64,128]{2,1,0:T(8,128)(2,1)S(1)}, bf16[16,64,128]{2,1,0:T(8,128)(2,1)}, u32[]{:S(2)}) copy-start(bf16[16,64,128]{2,1,0:T(8,128)(2,1)} %copy-done.17) | copy-start | bytes 786436
  107.6 10.0 %collective-permute-start.2 = (bf16[128,896]{1,0:T(8,128)(2,1)S(1)}, bf16[128,896]{1,0:T(8,128)(2,1)S(1)}, u32[]{:S(2)}, u32[]{:S(2)}) collective-permute-start(bf16[128,896]{1,0:T(8,128)(2,1)S(1)} %copy-done.16), channel_id=1, source_target_pairs={{0,4},{1,5},{2,6},{3,7},{4,0},{5,1},{6,2},{7,3},{8,12},{9,13},{10,... | collective-permute-start | bytes 688136 | tf_op jit(solution)/shard_map/ppermute | solution.py:346
  109.4 11.8 %collective-permute-start.1 = (bf16[128,896]{1,0:T(8,128)(2,1)S(1)}, bf16[128,896]{1,0:T(8,128)(2,1)S(1)}, u32[]{:S(2)}, u32[]{:S(2)}) collective-permute-start(bf16[128,896]{1,0:T(8,128)(2,1)S(1)} %copy-done.16), channel_id=1, source_target_pairs={{0,6},{1,7},{2,0},{3,1},{4,2},{5,3},{6,4},{7,5},{8,14},{9,15},{10,... | collective-permute-start | bytes 688136 | tf_op jit(solution)/shard_map/ppermute | solution.py:346
  110.8 12.4 %collective-permute-start = (bf16[128,896]{1,0:T(8,128)(2,1)S(1)}, bf16[128,896]{1,0:T(8,128)(2,1)S(1)}, u32[]{:S(2)}, u32[]{:S(2)}) collective-permute-start(bf16[128,896]{1,0:T(8,128)(2,1)S(1)} %copy-done.16), channel_id=1, source_target_pairs={{0,2},{1,3},{2,4},{3,5},{4,6},{5,7},{6,0},{7,1},{8,10},{9,11},{10,... | collective-permute-start | bytes 688136 | tf_op jit(solution)/shard_map/ppermute | solution.py:346
  125.1 35.4 %all-to-all-start.2 = ((bf16[16,4,16,896]{3,2,1,0:T(8,128)(2,1)}), bf16[16,4,16,896]{3,2,1,0:T(8,128)(2,1)}, u32[]{:S(2)}, u32[]{:S(2)}) async-start(bf16[16,4,16,896]{3,2,1,0:T(8,128)(2,1)} %spread.2), calls=%async_computation.3 | async-start | bytes 3670016 | tf_op jit(solution)/shard_map/all_to_all | solution.py:352
  133.9 31.3 %copy-start.23 = (s32[4]{0:T(128)S(1)}, s32[4]{0:T(128)}, u32[]{:S(2)}) copy-start(s32[4]{0:T(128)} %constant.49.clone) | copy-start | bytes 52
  160.6 41.8 %slice-start.2 = ((s8[5505024]{0:T(1024)(128)(4,1)}), s8[1310720]{0:T(1024)(128)(4,1)S(1)}, s32[]{:S(2)}) async-start(s8[5505024]{0:T(1024)(128)(4,1)} %bitcast.11), calls=%async_computation.11 | async-start | bytes 2621440
  160.6 31.4 %all-to-all-start.4 = ((bf16[16,4,16,896]{3,2,1,0:T(8,128)(2,1)}), bf16[16,4,16,896]{3,2,1,0:T(8,128)(2,1)}, u32[]{:S(2)}, u32[]{:S(2)}) async-start(bf16[16,4,16,896]{3,2,1,0:T(8,128)(2,1)} %copy-done.7), calls=%async_computation.5 | async-start | bytes 3670016 | tf_op jit(solution)/shard_map/all_to_all | solution.py:352
  165.1 26.9 %collective-permute-start.3 = (bf16[16,4,16,896]{3,2,1,0:T(8,128)(2,1)}, bf16[16,4,16,896]{3,2,1,0:T(8,128)(2,1)}, u32[]{:S(2)}, u32[]{:S(2)}) collective-permute-start(bf16[16,4,16,896]{3,2,1,0:T(8,128)(2,1)} %all-to-all-done.2.own_ref), channel_id=1, source_target_pairs={{0,1},{1,0},{2,3},{3,2},{4,5},{5,4},{6,7},{7,6},{8,9},{9,8},{10,11... | collective-permute-start | bytes 5505032 | tf_op jit(solution)/shard_map/ppermute | solution.py:349
  191.9 17.2 %collective-permute-start.5 = (bf16[16,4,16,896]{3,2,1,0:T(8,128)(2,1)}, bf16[16,4,16,896]{3,2,1,0:T(8,128)(2,1)S(1)}, u32[]{:S(2)}, u32[]{:S(2)}) collective-permute-start(bf16[16,4,16,896]{3,2,1,0:T(8,128)(2,1)} %all-to-all-done.4.own_ref), channel_id=1, source_target_pairs={{0,1},{1,0},{2,3},{3,2},{4,5},{5,4},{6,7},{7,6},{8,9},{9,8},{10,11... | collective-permute-start | bytes 5505032 | tf_op jit(solution)/shard_map/ppermute | solution.py:349
  192.0 10.3 %slice-start.3 = ((s8[5505024]{0:T(1024)(128)(4,1)}), s8[4194304]{0:T(1024)(128)(4,1)S(1)}, s32[]{:S(2)}) async-start(s8[5505024]{0:T(1024)(128)(4,1)} %bitcast.11), calls=%async_computation.12 | async-start | bytes 8388608
  192.0 2.7 copy-start.5
  202.4 2.6 copy-start.2
  208.5 16.8 %collective-permute-start.4 = (bf16[16,4,16,896]{3,2,1,0:T(8,128)(2,1)S(1)}, bf16[16,4,16,896]{3,2,1,0:T(8,128)(2,1)S(1)}, u32[]{:S(2)}, u32[]{:S(2)}) collective-permute-start(bf16[16,4,16,896]{3,2,1,0:T(8,128)(2,1)S(1)} %back.6), channel_id=1, source_target_pairs={{0,1},{1,0},{2,3},{3,2},{4,5},{5,4},{6,7},{7,6},{8,9},{9,8},{10,11... | collective-permute-start | bytes 5505032 | tf_op jit(solution)/shard_map/ppermute | solution.py:349
  218.3 2.6 copy-start.3
  220.9 4.4 %copy-start.13 = (bf16[256,768]{1,0:T(8,128)(2,1)}, bf16[256,768]{1,0:T(8,128)(2,1)S(1)}, u32[]{:S(2)}) copy-start(bf16[256,768]{1,0:T(8,128)(2,1)S(1)} %hidden.5.grads_ref) | copy-start | bytes 1179652
  225.3 10.2 %collective-permute-start.6 = (bf16[16,4,16,896]{3,2,1,0:T(8,128)(2,1)}, bf16[16,4,16,896]{3,2,1,0:T(8,128)(2,1)}, u32[]{:S(2)}, u32[]{:S(2)}) collective-permute-start(bf16[16,4,16,896]{3,2,1,0:T(8,128)(2,1)} %back.8), channel_id=1, source_target_pairs={{0,1},{1,0},{2,3},{3,2},{4,5},{5,4},{6,7},{7,6},{8,9},{9,8},{10,11... | collective-permute-start | bytes 5505032 | tf_op jit(solution)/shard_map/ppermute | solution.py:349
  231.6 3.9 %copy-start.14 = (bf16[256,768]{1,0:T(8,128)(2,1)S(1)}, bf16[256,768]{1,0:T(8,128)(2,1)}, u32[]{:S(2)}) copy-start(bf16[256,768]{1,0:T(8,128)(2,1)} %copy-done.13) | copy-start | bytes 1179652
  231.6 34.8 %all-to-all-start.3 = ((bf16[16,4,16,896]{3,2,1,0:T(8,128)(2,1)}), bf16[16,4,16,896]{3,2,1,0:T(8,128)(2,1)S(1)}, u32[]{:S(2)}, u32[]{:S(2)}) async-start(bf16[16,4,16,896]{3,2,1,0:T(8,128)(2,1)} %copy-done.9), calls=%async_computation.4 | async-start | bytes 3670016 | tf_op jit(solution)/shard_map/all_to_all | solution.py:352
  296.6 19.5 %all-to-all-start.1 = ((bf16[16,32,896]{2,1,0:T(8,128)(2,1)}), bf16[16,32,896]{2,1,0:T(8,128)(2,1)S(1)}, u32[]{:S(2)}, u32[]{:S(2)}) async-start(bf16[16,32,896]{2,1,0:T(8,128)(2,1)} %bitcast.29), calls=%async_computation.2 | async-start | bytes 1835008 | tf_op jit(solution)/shard_map/all_to_all | solution.py:352
  301.7 5.3 %copy-start.19 = (bf16[16,64,128]{2,1,0:T(8,128)(2,1)S(1)}, bf16[16,64,128]{2,1,0:T(8,128)(2,1)}, u32[]{:S(2)}) copy-start(bf16[16,64,128]{2,1,0:T(8,128)(2,1)} %copy-done.17) | copy-start | bytes 786436
  302.5 8.6 %collective-permute-start.7 = (bf16[128,896]{1,0:T(8,128)(2,1)S(1)}, bf16[128,896]{1,0:T(8,128)(2,1)S(1)}, u32[]{:S(2)}, u32[]{:S(2)}) collective-permute-start(bf16[128,896]{1,0:T(8,128)(2,1)S(1)} %get-tuple-element.14), channel_id=1, source_target_pairs={{0,6},{1,7},{2,0},{3,1},{4,2},{5,3},{6,4},{7,5},{8,14},{9,15},{10,... | collective-permute-start | bytes 688136 | tf_op jit(solution)/shard_map/ppermute | solution.py:346
  302.6 9.2 %collective-permute-start.8 = (bf16[128,896]{1,0:T(8,128)(2,1)S(1)}, bf16[128,896]{1,0:T(8,128)(2,1)S(1)}, u32[]{:S(2)}, u32[]{:S(2)}) collective-permute-start(bf16[128,896]{1,0:T(8,128)(2,1)S(1)} %get-tuple-element.15), channel_id=1, source_target_pairs={{0,2},{1,3},{2,4},{3,5},{4,6},{5,7},{6,0},{7,1},{8,10},{9,11},{10,... | collective-permute-start | bytes 688136 | tf_op jit(solution)/shard_map/ppermute | solution.py:346
  304.6 11.5 %collective-permute-start.9 = (bf16[128,896]{1,0:T(8,128)(2,1)S(1)}, bf16[128,896]{1,0:T(8,128)(2,1)S(1)}, u32[]{:S(2)}, u32[]{:S(2)}) collective-permute-start(bf16[128,896]{1,0:T(8,128)(2,1)S(1)} %get-tuple-element.16), channel_id=1, source_target_pairs={{0,4},{1,5},{2,6},{3,7},{4,0},{5,1},{6,2},{7,3},{8,12},{9,13},{10,... | collective-permute-start | bytes 688136 | tf_op jit(solution)/shard_map/ppermute | solution.py:346
  (12 other events, 17.0 us)
Sparse Core Ops, SparseCore 0:
  36.5 44.1 all-gather.1
  106.8 50.6 reduce-scatter.1

commit v2 on v1

v2 whole, which is shorter than its diff:
```python
import functools

import jax
import jax.numpy as jnp
from jax import lax
from jax.experimental import pallas as pl
from jax.experimental.pallas import tpu as pltpu
from jax.sharding import PartitionSpec as P

EXP_GRP = 3
CAP = 64
LANE_ROWS = 8
Z_LAST = (0, 32)
Z_FIRST = ((32, 16), (48, 16))
Z_OFFSETS = (0, -1, 1, 2)
VMEM = 60 * 1024 * 1024
BF = jnp.bfloat16
F32 = jnp.float32
NT = (((1,), (1,)), ((), ()))
TN = (((0,), (0,)), ((), ()))


def params():
    return pltpu.CompilerParams(vmem_limit_bytes=VMEM)


COST = pl.CostEstimate(flops=1000, bytes_accessed=1000, transcendentals=0)


def after(value, *earlier):
    return lax.optimization_barrier((value, *earlier))[0]


def routing_kernel(groups_ref, picks_ref, weights_ref, tok_ref, table_ref, out_ref):
    group_count, slots, tok_rows = table_ref.shape
    first = out_ref.shape[1] - LANE_ROWS
    groups = groups_ref[...]
    picks = picks_ref[...]
    weights = weights_ref[...]
    ids = lax.broadcasted_iota(jnp.int32, (group_count, tok_rows), 0)
    member = jnp.zeros((group_count, tok_rows), jnp.bool_)
    for q in range(groups.shape[0]):
        member = member | (ids == groups[q : q + 1, :])
    earlier = lax.broadcasted_iota(jnp.int32, (tok_rows, tok_rows), 0) < lax.broadcasted_iota(
        jnp.int32, (tok_rows, tok_rows), 1
    )
    slot = jnp.dot(
        member.astype(F32).astype(BF), earlier.astype(F32).astype(BF), preferred_element_type=F32
    ).astype(jnp.int32)
    slot = jnp.where(member, slot, -1)
    slot_ids = lax.broadcasted_iota(jnp.int32, (group_count, slots, tok_rows), 1)
    table = (slot[:, None, :] == slot_ids).astype(F32).astype(BF)
    table_ref[...] = table

    shape = (group_count, LANE_ROWS, tok_rows)
    group_ids = lax.broadcasted_iota(jnp.int32, shape, 0)
    expert_ids = lax.broadcasted_iota(jnp.int32, shape, 1)
    spread = jnp.zeros(shape, F32)
    for k in range(picks.shape[0]):
        pick = picks[k : k + 1, :]
        chosen = jnp.zeros_like(pick)
        for q in range(groups.shape[0]):
            inside = (pick >= q * EXP_GRP) & (pick < (q + 1) * EXP_GRP)
            chosen = chosen + jnp.where(inside, groups[q : q + 1, :] * EXP_GRP + pick - q * EXP_GRP, 0)
        hit = group_ids * EXP_GRP + expert_ids == chosen[:, None, :]
        hit = hit & (expert_ids < EXP_GRP)
        spread = spread + jnp.where(hit, weights[k : k + 1, :][:, None, :], 0.0)
    spread = spread.astype(BF)

    width = out_ref.shape[2]
    rows = jnp.dot(
        table[:, :first].reshape(group_count * first, tok_rows), tok_ref[...], preferred_element_type=F32
    ).astype(BF)
    out_ref[:, :first, :] = rows.reshape(group_count, first, width)
    out_ref[:, first:, :] = jnp.zeros((group_count, LANE_ROWS, width), BF)
    for g in range(group_count):
        lanes = lax.dot_general(spread[g], table[g], NT, preferred_element_type=F32)
        out_ref[g, first:, :slots] = lanes.astype(BF)


def route(token_groups, expert_pick, combine_weight, tokens, group_count):
    tok_rows, width = tokens.shape
    first = Z_LAST[1]
    return pl.pallas_call(
        routing_kernel,
        out_shape=(
            jax.ShapeDtypeStruct((group_count, CAP, tok_rows), BF),
            jax.ShapeDtypeStruct((group_count, first + LANE_ROWS, width), BF),
        ),
        compiler_params=params(),
        cost_estimate=COST,
        name="route",
    )(token_groups.T, expert_pick.T, combine_weight.T, tokens)


def spread_kernel(table_ref, t0, t1, t2, t3, out_ref):
    group_count, slots, tok_rows = table_ref.shape
    table = table_ref[...].reshape(group_count * slots, tok_rows)
    for z, tok in enumerate((t0, t1, t2, t3)):
        rows = jnp.dot(table, tok[...], preferred_element_type=F32).astype(BF)
        out_ref[:, z] = rows.reshape(group_count, slots, rows.shape[1])


def spread_tokens(table, tokens):
    group_count, slots, tok_rows = table.shape
    width = tokens[0].shape[1]
    return pl.pallas_call(
        spread_kernel,
        out_shape=jax.ShapeDtypeStruct((group_count, len(tokens), slots, width), BF),
        compiler_params=params(),
        cost_estimate=COST,
        name="spread",
    )(table, *tokens)


def write_grads(hidden, lane_ref, gate_ref, up_ref, out_ref):
    rows = hidden.shape[0]
    units = gate_ref.shape[-1]
    lanes = lane_ref[...].reshape(rows, EXP_GRP)
    for j in range(EXP_GRP):
        scaled = hidden[:, j * units : (j + 1) * units] * lanes[:, j : j + 1]
        p = gate_ref[j].reshape(rows, units).astype(F32)
        q = up_ref[j].reshape(rows, units).astype(F32)
        sg = 1.0 / (1.0 + jnp.exp(-p))
        gate = scaled * q * sg * (1.0 + p * (1.0 - sg))
        up = scaled * p * sg
        out_ref[:, j * units : (j + 1) * units] = gate.astype(BF)
        out_ref[:, (EXP_GRP + j) * units : (EXP_GRP + j + 1) * units] = up.astype(BF)


ANY = pl.BlockSpec(memory_space=pl.ANY)


def block_orders(chips):
    place = lax.axis_index("local")
    z, core = lax.div(place, 2), lax.rem(place, 2)
    starts = [lax.rem(z + by + chips, chips) * 2 for by in Z_OFFSETS]
    return [start + core for start in starts], [start + 1 - core for start in starts]


def columns_of(ref, block, width):
    return ref.at[:, pl.ds(pl.multiple_of(block * width, 128), width)]


def rows_of(ref, block, width):
    return ref.at[:, pl.ds(pl.multiple_of(block * width, 128), width)]


def copies_of(pairs, sems):
    return [pltpu.make_async_copy(src, dst, sems.at[i]) for i, (src, dst) in enumerate(pairs)]


def begin(copies):
    for copy in copies:
        copy.start()
    return copies


class Stream:
    def __init__(self, groups, depth=3):
        self.groups, self.depth, self.next = groups, depth, 0
        self.ahead(depth)

    def ahead(self, until):
        while self.next < min(until, len(self.groups)):
            begin(self.groups[self.next])
            self.next += 1

    def use(self, index):
        self.ahead(index + 1 + self.depth)
        for copy in self.groups[index]:
            copy.wait()


def saved_copies(start, count, lane_ref, gate_ref, up_ref, lane, gate, up, sems):
    slots = pl.ds(start, count)
    return copies_of(
        [(lane_ref.at[:, slots], lane), (gate_ref.at[:, :, slots], gate), (up_ref.at[:, :, slots], up)], sems
    )


def weights_times(grads, gate, up):
    columns = jnp.concatenate([gate[j] for j in range(EXP_GRP)] + [up[j] for j in range(EXP_GRP)], axis=1)
    return lax.dot_general(grads, columns, NT, preferred_element_type=F32)


def last_kernel(
    x_ref, down_ref, w_gate_ref, w_up_ref, lane_ref, gate_ref, up_ref, out_ref,
    x, down, w_gate, w_up, lane, gate, up, grads, out,
    x_sems, down_sems, w_gate_sems, w_up_sems, saved_sems, out_sems,
):
    blocks, _, width = x_ref.shape
    start, count = Z_LAST
    turns = out.shape[0]
    groups = [
        copies_of([(x_ref.at[k], x.at[k])], x_sems.at[pl.ds(k, 1)])
        + copies_of([(columns_of(down_ref, k, width), down.at[k])], down_sems.at[pl.ds(k, 1)])
        for k in range(blocks)
    ]
    groups[-1] += saved_copies(start, count, lane_ref, gate_ref, up_ref, lane, gate, up, saved_sems)
    groups += [
        copies_of([(rows_of(w_gate_ref, k, width), w_gate.at[k])], w_gate_sems.at[pl.ds(k, 1)])
        + copies_of([(rows_of(w_up_ref, k, width), w_up.at[k])], w_up_sems.at[pl.ds(k, 1)])
        for k in range(blocks)
    ]
    stream = Stream(groups)
    total = None
    for k in range(blocks):
        stream.use(k)
        part = lax.dot_general(x[k], down[k], NT, preferred_element_type=F32)
        total = part if total is None else total + part
    write_grads(total, lane, gate, up, grads)
    leaving = []
    for k in range(blocks):
        stream.use(blocks + k)
        if k >= turns:
            leaving[k - turns].wait()
        out[k % turns] = weights_times(grads[...], w_gate[k], w_up[k]).astype(BF)
        leaving += begin(copies_of([(out.at[k % turns], out_ref.at[k])], out_sems.at[pl.ds(k, 1)]))
    for copy in leaving[-turns:]:
        copy.wait()


def last_pass(rows_in, w_down, w_gate, w_up, lanes, saved_gate, saved_up):
    blocks, rows, width = rows_in.shape
    units = w_gate.shape[2]
    group_count = lanes.shape[0]
    count = Z_LAST[1]
    sems = pltpu.SemaphoreType.DMA
    return pl.pallas_call(
        last_kernel,
        out_shape=jax.ShapeDtypeStruct((blocks, rows, width), BF),
        in_specs=[ANY] * 7,
        out_specs=ANY,
        scratch_shapes=[
            pltpu.VMEM((blocks, rows, width), BF),
            pltpu.VMEM((blocks, EXP_GRP * units, width), BF),
            pltpu.VMEM((blocks, EXP_GRP, width, units), BF),
            pltpu.VMEM((blocks, EXP_GRP, width, units), BF),
            pltpu.VMEM((group_count, count, EXP_GRP), F32),
            pltpu.VMEM((EXP_GRP, group_count, count, units), BF),
            pltpu.VMEM((EXP_GRP, group_count, count, units), BF),
            pltpu.VMEM((rows, 2 * EXP_GRP * units), BF),
            pltpu.VMEM((3, rows, width), BF),
            sems((blocks,)), sems((blocks,)), sems((blocks,)), sems((blocks,)), sems((3,)), sems((blocks,)),
        ],
        compiler_params=params(),
        cost_estimate=COST,
        name="last_pass",
    )(rows_in, w_down, w_gate, w_up, lanes, saved_gate, saved_up)


def first_kernel(
    start, own_ref, other_ref, down_ref, w_gate_ref, w_up_ref, lane_ref, gate_ref, up_ref, *refs
):
    chips, width = own_ref.shape[1], own_ref.shape[3]
    grads_ref, out_refs, refs = refs[0], refs[1 : 1 + chips], refs[1 + chips :]
    own, other, down, w_gate, w_up, lane, gate, up, grads, out = refs[:10]
    own_sems, other_sems, down_sems, w_gate_sems, w_up_sems, saved_sems, out_sems, grads_sems = refs[10:]
    mine, theirs = block_orders(chips)
    order = mine + theirs
    count = own_ref.shape[2]
    rows = own_ref.shape[0] * count
    groups = []
    for k in range(2 * chips):
        src, dst, sems = (own_ref, own, own_sems) if k < chips else (other_ref, other, other_sems)
        groups.append(
            copies_of([(src.at[:, k % chips], dst.at[k % chips])], sems.at[pl.ds(k % chips, 1)])
            + copies_of([(columns_of(down_ref, order[k], width), down.at[k])], down_sems.at[pl.ds(k, 1)])
        )
    groups[-1] += saved_copies(start, count, lane_ref, gate_ref, up_ref, lane, gate, up, saved_sems)
    for k in range(chips):
        block = order[chips + k]
        groups.append(
            copies_of([(rows_of(w_gate_ref, block, width), w_gate.at[k])], w_gate_sems.at[pl.ds(k, 1)])
            + copies_of([(rows_of(w_up_ref, block, width), w_up.at[k])], w_up_sems.at[pl.ds(k, 1)])
        )
    stream = Stream(groups)
    total = None
    for k in range(2 * chips):
        stream.use(k)
        piece = own[k] if k < chips else other[k - chips]
        part = lax.dot_general(piece.reshape(rows, width), down[k], NT, preferred_element_type=F32)
        total = part if total is None else total + part
    write_grads(total, lane, gate, up, grads)
    leaving = begin(copies_of([(grads, grads_ref)], grads_sems))
    for k in range(chips):
        stream.use(2 * chips + k)
        out[k] = weights_times(grads[...], w_gate[k], w_up[k]).astype(BF)
        leaving += begin(copies_of([(out.at[k], out_refs[k])], out_sems.at[pl.ds(k, 1)]))
    for copy in leaving:
        copy.wait()


def first_pass(own, other, w_down, w_gate, w_up, lanes, saved_gate, saved_up, slots):
    start, count = slots
    group_count, chips, _, width = own.shape
    units = w_gate.shape[2]
    rows = group_count * count
    sems = pltpu.SemaphoreType.DMA
    results = pl.pallas_call(
        functools.partial(first_kernel, start),
        out_shape=(jax.ShapeDtypeStruct((rows, 2 * EXP_GRP * units), BF),)
        + tuple(jax.ShapeDtypeStruct((rows, width), BF) for _ in range(chips)),
        in_specs=[ANY] * 8,
        out_specs=(ANY,) * (1 + chips),
        scratch_shapes=[
            pltpu.VMEM((chips, group_count, count, width), BF),
            pltpu.VMEM((chips, group_count, count, width), BF),
            pltpu.VMEM((2 * chips, EXP_GRP * units, width), BF),
            pltpu.VMEM((chips, EXP_GRP, width, units), BF),
            pltpu.VMEM((chips, EXP_GRP, width, units), BF),
            pltpu.VMEM((group_count, count, EXP_GRP), F32),
            pltpu.VMEM((EXP_GRP, group_count, count, units), BF),
            pltpu.VMEM((EXP_GRP, group_count, count, units), BF),
            pltpu.VMEM((rows, 2 * EXP_GRP * units), BF),
            pltpu.VMEM((chips, rows, width), BF),
            sems((chips,)), sems((chips,)), sems((2 * chips,)), sems((chips,)), sems((chips,)), sems((3,)),
            sems((chips,)), sems((1,)),
        ],
        compiler_params=params(),
        cost_estimate=COST,
        name="first_pass",
    )(own, other, w_down, w_gate, w_up, lanes, saved_gate, saved_up)
    return results[0], list(results[1:])


def own_kernel(grads_ref, w_gate_ref, w_up_ref, *refs):
    chips = len(refs) - 11
    other_refs, out_ref, refs = refs[:chips], refs[chips], refs[chips + 1 :]
    w_gate, w_up, other, grads, out, w_gate_sems, w_up_sems, other_sems, grads_sems, out_sems = refs
    group_count, _, count, width = out_ref.shape
    order = block_orders(chips)[0]
    arriving = begin(copies_of([(grads_ref, grads)], grads_sems))
    stream = Stream(
        [
            copies_of([(rows_of(w_gate_ref, order[k], width), w_gate.at[k])], w_gate_sems.at[pl.ds(k, 1)])
            + copies_of([(rows_of(w_up_ref, order[k], width), w_up.at[k])], w_up_sems.at[pl.ds(k, 1)])
            + copies_of([(other_refs[k], other.at[k])], other_sems.at[pl.ds(k, 1)])
            for k in range(chips)
        ],
        depth=2,
    )
    leaving = []
    for k in range(chips):
        stream.use(k)
        if k == 0:
            arriving[0].wait()
        part = weights_times(grads[...], w_gate[k], w_up[k]) + other[k].astype(F32)
        out[k] = part.astype(BF).reshape(group_count, count, width)
        leaving += begin(copies_of([(out.at[k], out_ref.at[:, k])], out_sems.at[pl.ds(k, 1)]))
    for copy in leaving:
        copy.wait()


def own_pass(grads, w_gate, w_up, others, group_count):
    rows, width = others[0].shape
    chips = len(others)
    count = rows // group_count
    units = w_gate.shape[2]
    sems = pltpu.SemaphoreType.DMA
    return pl.pallas_call(
        own_kernel,
        out_shape=jax.ShapeDtypeStruct((group_count, chips, count, width), BF),
        in_specs=[ANY] * (3 + chips),
        out_specs=ANY,
        scratch_shapes=[
            pltpu.VMEM((chips, EXP_GRP, width, units), BF),
            pltpu.VMEM((chips, EXP_GRP, width, units), BF),
            pltpu.VMEM((chips, rows, width), BF),
            pltpu.VMEM((rows, grads.shape[1]), BF),
            pltpu.VMEM((chips, group_count, count, width), BF),
            sems((chips,)), sems((chips,)), sems((chips,)), sems((1,)), sems((chips,)),
        ],
        compiler_params=params(),
        cost_estimate=COST,
        name="own_pass",
    )(grads, w_gate, w_up, *others)


def collect_kernel(*refs):
    count = len(Z_FIRST)
    tables, arrived, outs = refs[:count], refs[count : 2 * count], refs[2 * count :]
    group_count, slots, tok_rows = tables[0].shape
    width = arrived[0].shape[-1]
    for z, out in enumerate(outs):
        total = jnp.zeros((tok_rows, width), F32)
        for table, rows in zip(tables, arrived):
            total = total + lax.dot_general(
                table[...].reshape(group_count * slots, tok_rows),
                rows[:, z].reshape(group_count * slots, width),
                TN,
                preferred_element_type=F32,
            )
        out[...] = total.astype(out.dtype)


def collect(tables, arrived):
    group_count, slots, tok_rows = tables[0].shape
    width = arrived[0].shape[-1]
    return pl.pallas_call(
        collect_kernel,
        out_shape=tuple(
            jax.ShapeDtypeStruct((tok_rows, width), F32 if z == 0 else BF) for z in range(len(Z_OFFSETS))
        ),
        compiler_params=params(),
        cost_estimate=COST,
        name="collect",
    )(*tables, *arrived)


def finish_kernel(table_ref, rows_ref, own_ref, a_ref, b_ref, c_ref, out_ref):
    group_count, slots, tok_rows = table_ref.shape
    width = rows_ref.shape[-1]
    total = lax.dot_general(
        table_ref[...].reshape(group_count * slots, tok_rows),
        rows_ref[...].reshape(group_count * slots, width),
        TN,
        preferred_element_type=F32,
    )
    total = total + own_ref[...]
    for ref in (a_ref, b_ref, c_ref):
        total = total + ref[...].astype(F32)
    out_ref[...] = total.astype(BF)


def finish(table, rows, own, others):
    tok_rows, width = own.shape
    return pl.pallas_call(
        finish_kernel,
        out_shape=jax.ShapeDtypeStruct((tok_rows, width), BF),
        compiler_params=params(),
        cost_estimate=COST,
        name="finish",
    )(table, rows, own, *others)


def on_device(
    grad_out, combine_weight, token_groups, expert_pick, saved_gate, saved_up, w_gate, w_up, w_down
):
    group_count = lax.axis_size("group")
    local_count = lax.axis_size("local")
    chips = local_count // 2
    def shift(value, by):
        pairs = [
            (c * 2 + k, ((c + by) % chips) * 2 + k) for c in range(chips) for k in range(2)
        ]
        return lax.ppermute(value, "local", pairs)

    def swap(value):
        return lax.ppermute(value, "local", [(i, i ^ 1) for i in range(local_count)])

    def exchange(value):
        return lax.all_to_all(value, "group", split_axis=0, concat_axis=0, tiled=True)

    units = w_gate.shape[2]
    down = w_down.reshape(EXP_GRP * units, w_down.shape[2])
    gate_slots = saved_gate.reshape(EXP_GRP, group_count, CAP, units)
    up_slots = saved_up.reshape(EXP_GRP, group_count, CAP, units)

    blocks = [grad_out] + [shift(grad_out, -by) for by in Z_OFFSETS[1:]]
    table, first_out = route(token_groups, expert_pick, combine_weight, grad_out, group_count)
    first_count = Z_LAST[1]
    first_in = exchange(first_out)
    lanes = jnp.transpose(first_in[:, first_count : first_count + EXP_GRP, :CAP], (0, 2, 1)).astype(F32)
    width = grad_out.shape[1]
    tables = [table[:, start : start + count] for start, count in Z_FIRST]
    sent = [spread_tokens(t, blocks) for t in tables]
    last_rows = lax.all_gather(
        after(first_in[:, :first_count].reshape(group_count * first_count, width), sent[0]),
        "local",
        axis=0,
        tiled=False,
    )

    own = [exchange(after(sent[0], lanes))]
    own[0], sent[1] = lax.optimization_barrier((own[0], sent[1]))
    other = [swap(own[0])]
    own.append(exchange(sent[1]))

    def first(k):
        grads, away = first_pass(own[k], other[k], down, w_gate, w_up, lanes, gate_slots, up_slots, Z_FIRST[k])
        return grads, [swap(piece) for piece in away]

    grads, others = first(0)
    last_part = last_pass(after(last_rows, grads), down, w_gate, w_up, lanes, gate_slots, up_slots)
    last_part, own[1], grads, *others = lax.optimization_barrier((last_part, own[1], grads, *others))
    last_sum = lax.psum_scatter(last_part, "local", scatter_dimension=0, tiled=False)
    ready = own_pass(grads, w_gate, w_up, others, group_count)
    first_home = exchange(ready)

    other.append(swap(own[1]))
    grads, others = first(1)
    second_home = exchange(after(own_pass(grads, w_gate, w_up, others, group_count), first_home))
    returned = [first_home, second_home]

    last_home = exchange(after(last_sum, second_home).reshape(group_count, first_count, width))
    pieces = collect(tables, returned)
    others = [shift(piece, by) for piece, by in zip(pieces[1:], Z_OFFSETS[1:])]
    return finish(table[:, :first_count], last_home, pieces[0], others)


def solution(mesh):
    placed = (
        P("group", "local"),
        P("group", None),
        P("group", None),
        P("group", None),
        P("group", None, "local"),
        P("group", None, "local"),
        P("group", None, "local"),
        P("group", None, "local"),
        P("group", "local", None),
    )
    return jax.shard_map(
        on_device, mesh=mesh, in_specs=placed, out_specs=P("group", "local"), check_vma=False
    )
```

time: 325 us -> 213 us (0.66)
  waiting for transfers between devices: 140 us -> 55.1 us
  blocking collectives: 55.3 us -> 29.8 us
  local copies, waits for them, and re-layouts: 28.7 us -> 8.5 us
  starting transfers between devices: 28.1 us -> 43.9 us
    all_gather x1, waiting for transfers between devices: 44 us -> 0.01 us  [on_device(): lax.all_gather(after(first_in[:, :first_count].reshape(group_count * firs...]
    all_to_all x4 -> x5, waiting for transfers between devices: 75.2 us -> 34.1 us  [exchange(): lax.all_to_all(value, 'group', split_axis=0, concat_axis=0, tiled=True)]
    all_to_all x2 -> x1, blocking collectives: 55.3 us -> 29.8 us  [exchange(): lax.all_to_all(value, 'group', split_axis=0, concat_axis=0, tiled=True)]
    unnamed x56 -> x38, local copies, waits for them, and re-layouts: 27.4 us -> 5.13 us
    all_to_all x4 -> x5, starting transfers between devices: 18.9 us -> 29.2 us  [exchange(): lax.all_to_all(value, 'group', split_axis=0, concat_axis=0, tiled=True)]
    pallas_call x8 -> x5, Pallas kernels: 53.1 us -> 46.1 us  [the longest x2 17.6 us: first_pass(): pl.pallas_call(functools.partial(first_kernel, start), out_shape=(jax.Sha...]
    ppermute x6, starting transfers between devices: 8.47 us -> 12.4 us  [shift(): return lax.ppermute(value, 'local', pairs)]
    pallas_call x2, Pallas kernels: 2.48 us -> 6.24 us  [spread_tokens(): pl.pallas_call(spread_kernel, out_shape=jax.ShapeDtypeStruct((group_count...]
  transfers between devices with their start and end apart: 16 -> 23, of which waited for: 10 -> 11; matrix products, arithmetic and copies ran while one was open for 0% -> 1% of each run, Pallas kernels for 11% -> 26%
where the time goes in v2:
time: 213 us; the launch traced here: 212 us
  Pallas kernels  61.3 us (29%)
  waiting for transfers between devices  55.1 us (26%)
  starting transfers between devices  43.9 us (21%)
  blocking collectives  29.8 us (14%)
  between operations  13.6 us (6%)
  local copies, waits for them, and re-layouts  8.5 us (4%)
    all_to_all x5, waiting for transfers between devices, exchange(): lax.all_to_all(value, 'group', split_axis=0, concat_axis=0, tiled=True)  34.1 us
    all_to_all x1, blocking collectives, exchange(): lax.all_to_all(value, 'group', split_axis=0, concat_axis=0, tiled=True)  29.8 us
    all_to_all x5, starting transfers between devices, exchange(): lax.all_to_all(value, 'group', split_axis=0, concat_axis=0, tiled=True)  29.2 us
    ppermute x6, waiting for transfers between devices, shift(): return lax.ppermute(value, 'local', pairs)  17.8 us
    pallas_call x2, Pallas kernels, first_pass(): pl.pallas_call(functools.partial(first_kernel, start), out_shape=(jax.Sha...  17.6 us
    pallas_call x1, Pallas kernels, last_pass(): pl.pallas_call(last_kernel, out_shape=jax.ShapeDtypeStruct((blocks, rows,...  17.1 us
    ppermute x6, starting transfers between devices, shift(): return lax.ppermute(value, 'local', pairs)  12.4 us
    pallas_call x2, Pallas kernels, own_pass(): pl.pallas_call(own_kernel, out_shape=jax.ShapeDtypeStruct((group_count, c...  11.4 us
  transfers between devices with their start and end apart: 23, of which 11 were waited for; matrix products, arithmetic and copies ran while one was open for 1% of the time, Pallas kernels for 26%

profile of v2, /device:TPU:0, one launch (start us, length us, event | category | flops | bytes accessed | tf_op | source)
XLA Modules:
  0.0 212.3 jit_solution(5245708307351987815)
XLA Ops:
  6.5 2.7 %route.1 = (bf16[16,64,128]{2,1,0:T(8,128)(2,1)}, bf16[16,40,896]{2,1,0:T(8,128)(2,1)}) custom-call(s32[4,128]{1,0:T(4,128)} %bitcast.28, s32[8,128]{1,0:T(8,128)} %bitcast.26, f32[8,128]{1,0:T(8,128)} %bitcast.27, bf16[128,896]{1,0:T(8,128)(2,1)} %t0.3), custom_call_target="tpu_custom_call" | custom-call | flops 1000 | bytes 1000 | tf_op jit(solution)/shard_map/route/pallas_call | solution.py:84
  9.3 7.2 %all-to-all-start = ((bf16[16,40,896]{2,1,0:T(8,128)(2,1)}), bf16[16,40,896]{2,1,0:T(8,128)(2,1)S(1)}, u32[]{:S(2)}, u32[]{:S(2)}) async-start(bf16[16,40,896]{2,1,0:T(8,128)(2,1)} %get-tuple-element.36), calls=%async_computation | async-start | bytes 2293760 | tf_op jit(solution)/shard_map/all_to_all | solution.py:454
  16.6 4.0 %collective-permute-start.2 = (bf16[128,896]{1,0:T(8,128)(2,1)S(1)}, bf16[128,896]{1,0:T(8,128)(2,1)S(1)}, u32[]{:S(2)}, u32[]{:S(2)}) collective-permute-start(bf16[128,896]{1,0:T(8,128)(2,1)S(1)} %copy-done.3), channel_id=1, source_target_pairs={{0,4},{1,5},{2,6},{3,7},{4,0},{5,1},{6,2},{7,3},{8,12},{9,13},{10,... | collective-permute-start | bytes 688136 | tf_op jit(solution)/shard_map/ppermute | solution.py:448
  21.3 1.3 collective-permute-start
  23.3 3.8 %collective-permute-done.2.t3 = bf16[128,896]{1,0:T(8,128)(2,1)S(1)} collective-permute-done((bf16[128,896]{1,0:T(8,128)(2,1)S(1)}, bf16[128,896]{1,0:T(8,128)(2,1)S(1)}, u32[]{:S(2)}, u32[]{:S(2)}) %collective-permute-start.2) | collective-permute-done | bytes 229408 | tf_op jit(solution)/shard_map/ppermute | solution.py:448
  27.0 4.5 %collective-permute-done.1.t2 = bf16[128,896]{1,0:T(8,128)(2,1)S(1)} collective-permute-done((bf16[128,896]{1,0:T(8,128)(2,1)S(1)}, bf16[128,896]{1,0:T(8,128)(2,1)S(1)}, u32[]{:S(2)}, u32[]{:S(2)}) %collective-permute-start.1) | collective-permute-done | bytes 229408 | tf_op jit(solution)/shard_map/ppermute | solution.py:448
  32.3 3.1 %spread.2 = bf16[16,4,16,896]{3,2,1,0:T(8,128)(2,1)} custom-call(bf16[16,16,128]{2,1,0:T(8,128)(2,1)} %get-tuple-element.66.table_ref.refs_0_, bf16[128,896]{1,0:T(8,128)(2,1)} %t0.3, bf16[128,896]{1,0:T(8,128)(2,1)} %copy-done.6, bf16[128,896]{1,0:T(8,128)(2,1)} %copy-done.5, bf16[128,896]{1,0:T(8,128)(2,1)} %copy-done.4), custom_call_target="tpu_custom_call" | custom-call | flops 1000 | bytes 1000 | tf_op jit(solution)/shard_map/spread/pallas_call | solution.py:107
  35.4 1.0 slice.20
  36.5 1.0 copy.15
  37.5 6.9 %all-to-all-start.1 = ((bf16[16,4,16,896]{3,2,1,0:T(8,128)(2,1)}), bf16[16,4,16,896]{3,2,1,0:T(8,128)(2,1)S(1)}, u32[]{:S(2)}, u32[]{:S(2)}) async-start(bf16[16,4,16,896]{3,2,1,0:T(8,128)(2,1)} %spread.2), calls=%async_computation.1 | async-start | bytes 3670016 | tf_op jit(solution)/shard_map/all_to_all | solution.py:454
  44.5 3.1 %spread.3 = bf16[16,4,16,896]{3,2,1,0:T(8,128)(2,1)} custom-call(bf16[16,16,128]{2,1,0:T(8,128)(2,1)} %get-tuple-element.65.table_ref.refs_1_, bf16[128,896]{1,0:T(8,128)(2,1)} %t0.3, bf16[128,896]{1,0:T(8,128)(2,1)} %copy-done.6, bf16[128,896]{1,0:T(8,128)(2,1)} %copy-done.5, bf16[128,896]{1,0:T(8,128)(2,1)} %copy-done.4), custom_call_target="tpu_custom_call" | custom-call | flops 1000 | bytes 1000 | tf_op jit(solution)/shard_map/spread/pallas_call | solution.py:107
  47.6 23.2 %all-to-all-done.1.own_ref = bf16[16,4,16,896]{3,2,1,0:T(8,128)(2,1)S(1)} async-done(((bf16[16,4,16,896]{3,2,1,0:T(8,128)(2,1)}), bf16[16,4,16,896]{3,2,1,0:T(8,128)(2,1)S(1)}, u32[]{:S(2)}, u32[]{:S(2)}) %all-to-all-start.1) | async-done | bytes 1835040 | tf_op jit(solution)/shard_map/all_to_all | solution.py:454
  70.9 1.3 copy-done.1
  72.1 4.4 %all-to-all-start.2 = ((bf16[16,4,16,896]{3,2,1,0:T(8,128)(2,1)}), bf16[16,4,16,896]{3,2,1,0:T(8,128)(2,1)}, u32[]{:S(2)}, u32[]{:S(2)}) async-start(bf16[16,4,16,896]{3,2,1,0:T(8,128)(2,1)} %spread.3), calls=%async_computation.2 | async-start | bytes 3670016 | tf_op jit(solution)/shard_map/all_to_all | solution.py:454
  76.6 8.8 %first_pass.2 = (bf16[256,768]{1,0:T(8,128)(2,1)}, bf16[256,896]{1,0:T(8,128)(2,1)}, bf16[256,896]{1,0:T(8,128)(2,1)}, bf16[256,896]{1,0:T(8,128)(2,1)}, bf16[256,896]{1,0:T(8,128)(2,1)}) custom-call(bf16[16,4,16,896]{3,2,1,0:T(8,128)(2,1)} %copy-done.1, bf16[16,4,16,896]{3,2,1,0:T(8,128)(2,1)} %collective-permute-done.3.other_ref, ...), custom_call_target="tpu_custom_call" | custom-call | flops 1000 | bytes 1000 | tf_op jit(solution)/shard_map/first_pass/pallas_call | solution.py:301
  86.5 17.1 %last_pass.1 = bf16[8,512,896]{2,1,0:T(8,128)(2,1)} custom-call(bf16[8,512,896]{2,1,0:T(8,128)(2,1)} %bitcast.17, bf16[384,7168]{1,0:T(8,128)(2,1)} %bitcast.12, bf16[3,7168,128]{2,1,0:T(8,128)(2,1)} %w_gate_ref.9, bf16[3,7168,128]{2,1,0:T(8,128)(2,1)} %w_up_ref.9, f32[16,64,3]{2,1,0:T(8,128)} %bitcast.15, bf16[3,16,64,128]{3,2,1,0:T(8,128)(2,1)} %bitcast.19, ...), custom_call_target="tpu_custom_call" | custom-call | flops 1000 | bytes 1000 | tf_op jit(solution)/shard_map/last_pass/pallas_call | solution.py:230
  104.0 0.7 copy-done.7
  105.2 5.6 %own_pass.3 = bf16[16,4,16,896]{3,2,1,0:T(8,128)(2,1)} custom-call(bf16[256,768]{1,0:T(8,128)(2,1)} %get-tuple-element.54.grads_ref, bf16[3,7168,128]{2,1,0:T(8,128)(2,1)} %w_gate_ref.9, bf16[3,7168,128]{2,1,0:T(8,128)(2,1)} %w_up_ref.9, bf16[256,896]{1,0:T(8,128)(2,1)} %copy-done.7, bf16[256,896]{1,0:T(8,128)(2,1)} %copy-done.8, ...), custom_call_target="tpu_custom_call" | custom-call | flops 1000 | bytes 1000 | tf_op jit(solution)/shard_map/own_pass/pallas_call | solution.py:362
  110.8 7.0 %all-to-all-start.3 = ((bf16[16,4,16,896]{3,2,1,0:T(8,128)(2,1)}), bf16[16,4,16,896]{3,2,1,0:T(8,128)(2,1)S(1)}, u32[]{:S(2)}, u32[]{:S(2)}) async-start(bf16[16,4,16,896]{3,2,1,0:T(8,128)(2,1)} %own_pass.3), calls=%async_computation.4 | async-start | bytes 3670016 | tf_op jit(solution)/shard_map/all_to_all | solution.py:454
  117.8 8.8 %first_pass.3 = (bf16[256,768]{1,0:T(8,128)(2,1)}, bf16[256,896]{1,0:T(8,128)(2,1)}, bf16[256,896]{1,0:T(8,128)(2,1)}, bf16[256,896]{1,0:T(8,128)(2,1)}, bf16[256,896]{1,0:T(8,128)(2,1)}) custom-call(bf16[16,4,16,896]{3,2,1,0:T(8,128)(2,1)} %all-to-all-done.2.own_ref, bf16[16,4,16,896]{3,2,1,0:T(8,128)(2,1)} %collective-permute-done.8.other_ref, ...), custom_call_target="tpu_custom_call" | custom-call | flops 1000 | bytes 1000 | tf_op jit(solution)/shard_map/first_pass/pallas_call | solution.py:301
  127.7 1.0 collective-permute-done.9.refs_0_
  129.4 0.8 collective-permute-done.11.refs_2_
  131.6 5.8 %own_pass.2 = bf16[16,4,16,896]{3,2,1,0:T(8,128)(2,1)} custom-call(bf16[256,768]{1,0:T(8,128)(2,1)} %get-tuple-element.49.grads_ref, bf16[3,7168,128]{2,1,0:T(8,128)(2,1)} %w_gate_ref.9, bf16[3,7168,128]{2,1,0:T(8,128)(2,1)} %w_up_ref.9, bf16[256,896]{1,0:T(8,128)(2,1)} %copy-done.11, bf16[256,896]{1,0:T(8,128)(2,1)} %copy-done.12, ...), custom_call_target="tpu_custom_call" | custom-call | flops 1000 | bytes 1000 | tf_op jit(solution)/shard_map/own_pass/pallas_call | solution.py:362
  137.4 10.7 %all-to-all-done.3.refs_2_ = bf16[16,4,16,896]{3,2,1,0:T(8,128)(2,1)S(1)} async-done(((bf16[16,4,16,896]{3,2,1,0:T(8,128)(2,1)}), bf16[16,4,16,896]{3,2,1,0:T(8,128)(2,1)S(1)}, u32[]{:S(2)}, u32[]{:S(2)}) %all-to-all-start.3) | async-done | bytes 1835040 | tf_op jit(solution)/shard_map/all_to_all | solution.py:454
  148.1 29.8 %all_to_all.30.refs_3_ = bf16[16,4,16,896]{3,2,1,0:T(8,128)(2,1)} all-to-all(bf16[16,4,16,896]{3,2,1,0:T(8,128)(2,1)} %own_pass.2), channel_id=1, replica_groups=mesh['group'=16,'local'=8] {'group'}, dimensions={0} | all-to-all | bytes 3670016 | tf_op jit(solution)/shard_map/all_to_all | solution.py:454
  177.9 3.6 %all-to-all-start.5 = ((bf16[16,32,896]{2,1,0:T(8,128)(2,1)}), bf16[16,32,896]{2,1,0:T(8,128)(2,1)S(1)}, u32[]{:S(2)}, u32[]{:S(2)}) async-start(bf16[16,32,896]{2,1,0:T(8,128)(2,1)} %bitcast.25), calls=%async_computation.6 | async-start | bytes 1835008 | tf_op jit(solution)/shard_map/all_to_all | solution.py:454
  181.6 3.6 %collect.1 = (f32[128,896]{1,0:T(8,128)}, bf16[128,896]{1,0:T(8,128)(2,1)}, bf16[128,896]{1,0:T(8,128)(2,1)}, bf16[128,896]{1,0:T(8,128)(2,1)}) custom-call(bf16[16,16,128]{2,1,0:T(8,128)(2,1)} %get-tuple-element.66.table_ref.refs_0_, bf16[16,16,128]{2,1,0:T(8,128)(2,1)} %get-tuple-element.65.table_ref.refs_1_, bf16[16,4,16,896]{3,2,1,0:T(8,128)(2,1)} %copy-done, ...), custom_call_target="tpu_custom_call" | custom-call | flops 1000 | bytes 1000 | tf_op jit(solution)/shard_map/collect/pallas_call | solution.py:401
  185.2 4.6 %collective-permute-start.13 = (bf16[128,896]{1,0:T(8,128)(2,1)}, bf16[128,896]{1,0:T(8,128)(2,1)S(1)}, u32[]{:S(2)}, u32[]{:S(2)}) collective-permute-start(bf16[128,896]{1,0:T(8,128)(2,1)} %get-tuple-element.62), channel_id=1, source_target_pairs={{0,6},{1,7},{2,0},{3,1},{4,2},{5,3},{6,4},{7,5},{8,14},{9,15},{10,... | collective-permute-start | bytes 688136 | tf_op jit(solution)/shard_map/ppermute | solution.py:448
  189.7 1.9 collective-permute-start.15
  192.3 6.2 %collective-permute-done.13.a_ref = bf16[128,896]{1,0:T(8,128)(2,1)S(1)} collective-permute-done((bf16[128,896]{1,0:T(8,128)(2,1)}, bf16[128,896]{1,0:T(8,128)(2,1)S(1)}, u32[]{:S(2)}, u32[]{:S(2)}) %collective-permute-start.13) | collective-permute-done | bytes 229408 | tf_op jit(solution)/shard_map/ppermute | solution.py:448
  198.5 3.2 %collective-permute-done.14.b_ref = bf16[128,896]{1,0:T(8,128)(2,1)S(1)} collective-permute-done((bf16[128,896]{1,0:T(8,128)(2,1)}, bf16[128,896]{1,0:T(8,128)(2,1)S(1)}, u32[]{:S(2)}, u32[]{:S(2)}) %collective-permute-start.14) | collective-permute-done | bytes 229408 | tf_op jit(solution)/shard_map/ppermute | solution.py:448
  202.8 2.6 %finish.1 = bf16[128,896]{1,0:T(8,128)(2,1)} custom-call(bf16[16,32,128]{2,1,0:T(8,128)(2,1)} %slice.15.table_ref, bf16[16,32,896]{2,1,0:T(8,128)(2,1)} %copy-done.2, f32[128,896]{1,0:T(8,128)} %get-tuple-element.61.own_ref, bf16[128,896]{1,0:T(8,128)(2,1)} %copy-done.16, bf16[128,896]{1,0:T(8,128)(2,1)} %copy-done.17, bf16[128,896]{1,0:T(8,128)(2,1)} %copy-done.18), custom_call_target="tpu_custom_call" | custom-call | flops 1000 | bytes 1000 | tf_op jit(solution)/shard_map/finish/pallas_call | solution.py:429
  (71 shorter events, 9.0 us)
Async XLA Ops:
  6.5 10.1 %copy-start.3 = (bf16[128,896]{1,0:T(8,128)(2,1)S(1)}, bf16[128,896]{1,0:T(8,128)(2,1)}, u32[]{:S(2)}) copy-start(bf16[128,896]{1,0:T(8,128)(2,1)} %t0.3) | copy-start | bytes 688132
  9.3 13.3 %copy-start.15 = (bf16[16,64,128]{2,1,0:T(8,128)(2,1)S(1)}, bf16[16,64,128]{2,1,0:T(8,128)(2,1)}, u32[]{:S(2)}) copy-start(bf16[16,64,128]{2,1,0:T(8,128)(2,1)} %get-tuple-element.35) | copy-start | bytes 786436
  9.3 26.2 %all-to-all-start = ((bf16[16,40,896]{2,1,0:T(8,128)(2,1)}), bf16[16,40,896]{2,1,0:T(8,128)(2,1)S(1)}, u32[]{:S(2)}, u32[]{:S(2)}) async-start(bf16[16,40,896]{2,1,0:T(8,128)(2,1)} %get-tuple-element.36), calls=%async_computation | async-start | bytes 2293760 | tf_op jit(solution)/shard_map/all_to_all | solution.py:454
  16.5 70.0 %all-gather.3.cloned.1.call-start = ((), (), s32[]{:S(2)}) async-start(), calls=%async_computation.8 | async-start | bytes 8257536 | tf_op jit(solution)/shard_map/all_gather | solution.py:469
  16.6 10.4 %collective-permute-start.2 = (bf16[128,896]{1,0:T(8,128)(2,1)S(1)}, bf16[128,896]{1,0:T(8,128)(2,1)S(1)}, u32[]{:S(2)}, u32[]{:S(2)}) collective-permute-start(bf16[128,896]{1,0:T(8,128)(2,1)S(1)} %copy-done.3), channel_id=1, source_target_pairs={{0,4},{1,5},{2,6},{3,7},{4,0},{5,1},{6,2},{7,3},{8,12},{9,13},{10,... | collective-permute-start | bytes 688136 | tf_op jit(solution)/shard_map/ppermute | solution.py:448
  20.6 11.0 %collective-permute-start.1 = (bf16[128,896]{1,0:T(8,128)(2,1)S(1)}, bf16[128,896]{1,0:T(8,128)(2,1)S(1)}, u32[]{:S(2)}, u32[]{:S(2)}) collective-permute-start(bf16[128,896]{1,0:T(8,128)(2,1)S(1)} %copy-done.3), channel_id=1, source_target_pairs={{0,6},{1,7},{2,0},{3,1},{4,2},{5,3},{6,4},{7,5},{8,14},{9,15},{10,... | collective-permute-start | bytes 688136 | tf_op jit(solution)/shard_map/ppermute | solution.py:448
  21.3 10.3 %collective-permute-start = (bf16[128,896]{1,0:T(8,128)(2,1)S(1)}, bf16[128,896]{1,0:T(8,128)(2,1)S(1)}, u32[]{:S(2)}, u32[]{:S(2)}) collective-permute-start(bf16[128,896]{1,0:T(8,128)(2,1)S(1)} %copy-done.3), channel_id=1, source_target_pairs={{0,2},{1,3},{2,4},{3,5},{4,6},{5,7},{6,0},{7,1},{8,10},{9,11},{10,... | collective-permute-start | bytes 688136 | tf_op jit(solution)/shard_map/ppermute | solution.py:448
  27.0 4.5 %copy-start.4 = (bf16[128,896]{1,0:T(8,128)(2,1)}, bf16[128,896]{1,0:T(8,128)(2,1)S(1)}, u32[]{:S(2)}) copy-start(bf16[128,896]{1,0:T(8,128)(2,1)S(1)} %collective-permute-done.2.t3) | copy-start | bytes 688132
  37.5 33.3 %all-to-all-start.1 = ((bf16[16,4,16,896]{3,2,1,0:T(8,128)(2,1)}), bf16[16,4,16,896]{3,2,1,0:T(8,128)(2,1)S(1)}, u32[]{:S(2)}, u32[]{:S(2)}) async-start(bf16[16,4,16,896]{3,2,1,0:T(8,128)(2,1)} %spread.2), calls=%async_computation.1 | async-start | bytes 3670016 | tf_op jit(solution)/shard_map/all_to_all | solution.py:454
  70.9 1.3 copy-start.1
  70.9 5.8 %collective-permute-start.3 = (bf16[16,4,16,896]{3,2,1,0:T(8,128)(2,1)S(1)}, bf16[16,4,16,896]{3,2,1,0:T(8,128)(2,1)}, u32[]{:S(2)}, u32[]{:S(2)}) collective-permute-start(bf16[16,4,16,896]{3,2,1,0:T(8,128)(2,1)S(1)} %all-to-all-done.1.own_ref), channel_id=1, source_target_pairs={{0,1},{1,0},{2,3},{3,2},{4,5},{5,4},{6,7},{7,6},{8,9},{9,8},{10,11... | collective-permute-start | bytes 5505032 | tf_op jit(solution)/shard_map/ppermute | solution.py:451
  72.1 31.8 %all-to-all-start.2 = ((bf16[16,4,16,896]{3,2,1,0:T(8,128)(2,1)}), bf16[16,4,16,896]{3,2,1,0:T(8,128)(2,1)}, u32[]{:S(2)}, u32[]{:S(2)}) async-start(bf16[16,4,16,896]{3,2,1,0:T(8,128)(2,1)} %spread.3), calls=%async_computation.2 | async-start | bytes 3670016 | tf_op jit(solution)/shard_map/all_to_all | solution.py:454
  76.6 101.4 %reduce-scatter.2.cloned.1.call-start = ((), (), s32[]{:S(2)}) async-start(), calls=%async_computation.7 | async-start | bytes 8257536 | tf_op jit(solution)/shard_map/reduce_scatter | solution.py:488
  85.4 18.4 %collective-permute-start.4 = (bf16[256,896]{1,0:T(8,128)(2,1)}, bf16[256,896]{1,0:T(8,128)(2,1)S(1)}, u32[]{:S(2)}, u32[]{:S(2)}) collective-permute-start(bf16[256,896]{1,0:T(8,128)(2,1)} %get-tuple-element.43), channel_id=1, source_target_pairs={{0,1},{1,0},{2,3},{3,2},{4,5},{5,4},{6,7},{7,6},{8,9},{9,8},{10,11... | collective-permute-start | bytes 1376264 | tf_op jit(solution)/shard_map/ppermute | solution.py:451
  85.5 18.4 %collective-permute-start.5 = (bf16[256,896]{1,0:T(8,128)(2,1)}, bf16[256,896]{1,0:T(8,128)(2,1)S(1)}, u32[]{:S(2)}, u32[]{:S(2)}) collective-permute-start(bf16[256,896]{1,0:T(8,128)(2,1)} %get-tuple-element.44), channel_id=1, source_target_pairs={{0,1},{1,0},{2,3},{3,2},{4,5},{5,4},{6,7},{7,6},{8,9},{9,8},{10,11... | collective-permute-start | bytes 1376264 | tf_op jit(solution)/shard_map/ppermute | solution.py:451
  86.0 17.9 %collective-permute-start.6 = (bf16[256,896]{1,0:T(8,128)(2,1)}, bf16[256,896]{1,0:T(8,128)(2,1)S(1)}, u32[]{:S(2)}, u32[]{:S(2)}) collective-permute-start(bf16[256,896]{1,0:T(8,128)(2,1)} %get-tuple-element.45), channel_id=1, source_target_pairs={{0,1},{1,0},{2,3},{3,2},{4,5},{5,4},{6,7},{7,6},{8,9},{9,8},{10,11... | collective-permute-start | bytes 1376264 | tf_op jit(solution)/shard_map/ppermute | solution.py:451
  86.1 17.8 %collective-permute-start.7 = (bf16[256,896]{1,0:T(8,128)(2,1)}, bf16[256,896]{1,0:T(8,128)(2,1)S(1)}, u32[]{:S(2)}, u32[]{:S(2)}) collective-permute-start(bf16[256,896]{1,0:T(8,128)(2,1)} %get-tuple-element.46), channel_id=1, source_target_pairs={{0,1},{1,0},{2,3},{3,2},{4,5},{5,4},{6,7},{7,6},{8,9},{9,8},{10,11... | collective-permute-start | bytes 1376264 | tf_op jit(solution)/shard_map/ppermute | solution.py:451
  103.9 1.2 copy-start.10
  105.2 12.6 %collective-permute-start.8 = (bf16[16,4,16,896]{3,2,1,0:T(8,128)(2,1)}, bf16[16,4,16,896]{3,2,1,0:T(8,128)(2,1)}, u32[]{:S(2)}, u32[]{:S(2)}) collective-permute-start(bf16[16,4,16,896]{3,2,1,0:T(8,128)(2,1)} %all-to-all-done.2.own_ref), channel_id=1, source_target_pairs={{0,1},{1,0},{2,3},{3,2},{4,5},{5,4},{6,7},{7,6},{8,9},{9,8},{10,11... | collective-permute-start | bytes 5505032 | tf_op jit(solution)/shard_map/ppermute | solution.py:451
  110.8 37.3 %all-to-all-start.3 = ((bf16[16,4,16,896]{3,2,1,0:T(8,128)(2,1)}), bf16[16,4,16,896]{3,2,1,0:T(8,128)(2,1)S(1)}, u32[]{:S(2)}, u32[]{:S(2)}) async-start(bf16[16,4,16,896]{3,2,1,0:T(8,128)(2,1)} %own_pass.3), calls=%async_computation.4 | async-start | bytes 3670016 | tf_op jit(solution)/shard_map/all_to_all | solution.py:454
  126.6 2.1 collective-permute-start.9
  126.8 2.5 %collective-permute-start.10 = (bf16[256,896]{1,0:T(8,128)(2,1)}, bf16[256,896]{1,0:T(8,128)(2,1)S(1)}, u32[]{:S(2)}, u32[]{:S(2)}) collective-permute-start(bf16[256,896]{1,0:T(8,128)(2,1)} %get-tuple-element.51), channel_id=1, source_target_pairs={{0,1},{1,0},{2,3},{3,2},{4,5},{5,4},{6,7},{7,6},{8,9},{9,8},{10,11... | collective-permute-start | bytes 1376264 | tf_op jit(solution)/shard_map/ppermute | solution.py:451
  127.2 3.0 %collective-permute-start.11 = (bf16[256,896]{1,0:T(8,128)(2,1)}, bf16[256,896]{1,0:T(8,128)(2,1)S(1)}, u32[]{:S(2)}, u32[]{:S(2)}) collective-permute-start(bf16[256,896]{1,0:T(8,128)(2,1)} %get-tuple-element.52), channel_id=1, source_target_pairs={{0,1},{1,0},{2,3},{3,2},{4,5},{5,4},{6,7},{7,6},{8,9},{9,8},{10,11... | collective-permute-start | bytes 1376264 | tf_op jit(solution)/shard_map/ppermute | solution.py:451
  127.3 3.5 %collective-permute-start.12 = (bf16[256,896]{1,0:T(8,128)(2,1)}, bf16[256,896]{1,0:T(8,128)(2,1)S(1)}, u32[]{:S(2)}, u32[]{:S(2)}) collective-permute-start(bf16[256,896]{1,0:T(8,128)(2,1)} %get-tuple-element.53), channel_id=1, source_target_pairs={{0,1},{1,0},{2,3},{3,2},{4,5},{5,4},{6,7},{7,6},{8,9},{9,8},{10,11... | collective-permute-start | bytes 1376264 | tf_op jit(solution)/shard_map/ppermute | solution.py:451
  128.7 2.1 %copy-start.11 = (bf16[256,896]{1,0:T(8,128)(2,1)}, bf16[256,896]{1,0:T(8,128)(2,1)S(1)}, u32[]{:S(2)}) copy-start(bf16[256,896]{1,0:T(8,128)(2,1)S(1)} %collective-permute-done.9.refs_0_) | copy-start | bytes 1376260
  129.4 1.5 copy-start.12
  148.1 29.8 %copy-start = (bf16[16,4,16,896]{3,2,1,0:T(8,128)(2,1)}, bf16[16,4,16,896]{3,2,1,0:T(8,128)(2,1)S(1)}, u32[]{:S(2)}) copy-start(bf16[16,4,16,896]{3,2,1,0:T(8,128)(2,1)S(1)} %all-to-all-done.3.refs_2_) | copy-start | bytes 5505028
  177.9 23.8 %all-to-all-start.5 = ((bf16[16,32,896]{2,1,0:T(8,128)(2,1)}), bf16[16,32,896]{2,1,0:T(8,128)(2,1)S(1)}, u32[]{:S(2)}, u32[]{:S(2)}) async-start(bf16[16,32,896]{2,1,0:T(8,128)(2,1)} %bitcast.25), calls=%async_computation.6 | async-start | bytes 1835008 | tf_op jit(solution)/shard_map/all_to_all | solution.py:454
  185.2 13.3 %collective-permute-start.13 = (bf16[128,896]{1,0:T(8,128)(2,1)}, bf16[128,896]{1,0:T(8,128)(2,1)S(1)}, u32[]{:S(2)}, u32[]{:S(2)}) collective-permute-start(bf16[128,896]{1,0:T(8,128)(2,1)} %get-tuple-element.62), channel_id=1, source_target_pairs={{0,6},{1,7},{2,0},{3,1},{4,2},{5,3},{6,4},{7,5},{8,14},{9,15},{10,... | collective-permute-start | bytes 688136 | tf_op jit(solution)/shard_map/ppermute | solution.py:448
  189.7 12.0 %collective-permute-start.14 = (bf16[128,896]{1,0:T(8,128)(2,1)}, bf16[128,896]{1,0:T(8,128)(2,1)S(1)}, u32[]{:S(2)}, u32[]{:S(2)}) collective-permute-start(bf16[128,896]{1,0:T(8,128)(2,1)} %get-tuple-element.63), channel_id=1, source_target_pairs={{0,2},{1,3},{2,4},{3,5},{4,6},{5,7},{6,0},{7,1},{8,10},{9,11},{10,... | collective-permute-start | bytes 688136 | tf_op jit(solution)/shard_map/ppermute | solution.py:448
  189.7 12.0 %collective-permute-start.15 = (bf16[128,896]{1,0:T(8,128)(2,1)}, bf16[128,896]{1,0:T(8,128)(2,1)S(1)}, u32[]{:S(2)}, u32[]{:S(2)}) collective-permute-start(bf16[128,896]{1,0:T(8,128)(2,1)} %get-tuple-element.64), channel_id=1, source_target_pairs={{0,4},{1,5},{2,6},{3,7},{4,0},{5,1},{6,2},{7,3},{8,12},{9,13},{10,... | collective-permute-start | bytes 688136 | tf_op jit(solution)/shard_map/ppermute | solution.py:448
  198.5 3.3 %copy-start.16 = (bf16[128,896]{1,0:T(8,128)(2,1)}, bf16[128,896]{1,0:T(8,128)(2,1)S(1)}, u32[]{:S(2)}) copy-start(bf16[128,896]{1,0:T(8,128)(2,1)S(1)} %collective-permute-done.13.a_ref) | copy-start | bytes 688132
  (10 other events, 8.5 us)
Sparse Core Ops, SparseCore 0:
  36.6 46.3 all-gather.2
  104.1 50.4 reduce-scatter.1

commit v3 on v2

--- a/solution.py
+++ b/solution.py
@@ -20,8 +20,8 @@
 TN = (((0,), (0,)), ((), ()))
 
 
-def params():
-    return pltpu.CompilerParams(vmem_limit_bytes=VMEM)
+def params(limit=VMEM):
+    return pltpu.CompilerParams(vmem_limit_bytes=limit)
 
 
 COST = pl.CostEstimate(flops=1000, bytes_accessed=1000, transcendentals=0)
@@ -403,7 +403,7 @@
         out_shape=tuple(
             jax.ShapeDtypeStruct((tok_rows, width), F32 if z == 0 else BF) for z in range(len(Z_OFFSETS))
         ),
-        compiler_params=params(),
+        compiler_params=params(16 * 1024 * 1024),
         cost_estimate=COST,
         name="collect",
     )(*tables, *arrived)
@@ -429,7 +429,7 @@
     return pl.pallas_call(
         finish_kernel,
         out_shape=jax.ShapeDtypeStruct((tok_rows, width), BF),
-        compiler_params=params(),
+        compiler_params=params(16 * 1024 * 1024),
         cost_estimate=COST,
         name="finish",
     )(table, rows, own, *others)

time: 213 us -> 209 us (0.981)
  Pallas kernels: 61.3 us -> 56.9 us
    pallas_call x1, Pallas kernels: 3.59 us -> 0.74 us  [collect(): pl.pallas_call(collect_kernel, out_shape=tuple((jax.ShapeDtypeStruct((tok...]
    unnamed x38 -> x36, local copies, waits for them, and re-layouts: 5.13 us -> 5.47 us
where the time goes in v3:
time: 209 us; the launch traced here: 208 us
  Pallas kernels  56.9 us (27%)
  waiting for transfers between devices  55.5 us (27%)
  starting transfers between devices  44.2 us (21%)
  blocking collectives  29.8 us (14%)
  between operations  13.6 us (7%)
  local copies, waits for them, and re-layouts  8.2 us (4%)
    all_to_all x5, waiting for transfers between devices, exchange(): lax.all_to_all(value, 'group', split_axis=0, concat_axis=0, tiled=True)  34.1 us
    all_to_all x1, blocking collectives, exchange(): lax.all_to_all(value, 'group', split_axis=0, concat_axis=0, tiled=True)  29.8 us
    all_to_all x5, starting transfers between devices, exchange(): lax.all_to_all(value, 'group', split_axis=0, concat_axis=0, tiled=True)  29.3 us
    ppermute x6, waiting for transfers between devices, shift(): return lax.ppermute(value, 'local', pairs)  18.2 us
    pallas_call x2, Pallas kernels, first_pass(): pl.pallas_call(functools.partial(first_kernel, start), out_shape=(jax.Sha...  17.6 us
    pallas_call x1, Pallas kernels, last_pass(): pl.pallas_call(last_kernel, out_shape=jax.ShapeDtypeStruct((blocks, rows,...  17.1 us
    ppermute x6, starting transfers between devices, shift(): return lax.ppermute(value, 'local', pairs)  12.6 us
    pallas_call x2, Pallas kernels, own_pass(): pl.pallas_call(own_kernel, out_shape=jax.ShapeDtypeStruct((group_count, c...  11.4 us
  transfers between devices with their start and end apart: 23, of which 11 were waited for; matrix products, arithmetic and copies ran while one was open for 1% of the time, Pallas kernels for 26%

profile of v3, /device:TPU:0, one launch (start us, length us, event | category | flops | bytes accessed | tf_op | source)
XLA Modules:
  0.0 208.2 jit_solution(4315031368905815618)
XLA Ops:
  6.5 2.8 %route.1 = (bf16[16,64,128]{2,1,0:T(8,128)(2,1)}, bf16[16,40,896]{2,1,0:T(8,128)(2,1)}) custom-call(s32[4,128]{1,0:T(4,128)} %bitcast.28, s32[8,128]{1,0:T(8,128)} %bitcast.26, f32[8,128]{1,0:T(8,128)} %bitcast.27, bf16[128,896]{1,0:T(8,128)(2,1)} %t0.3), custom_call_target="tpu_custom_call" | custom-call | flops 1000 | bytes 1000 | tf_op jit(solution)/shard_map/route/pallas_call | solution.py:84
  9.3 7.2 %all-to-all-start = ((bf16[16,40,896]{2,1,0:T(8,128)(2,1)}), bf16[16,40,896]{2,1,0:T(8,128)(2,1)S(1)}, u32[]{:S(2)}, u32[]{:S(2)}) async-start(bf16[16,40,896]{2,1,0:T(8,128)(2,1)} %get-tuple-element.36), calls=%async_computation | async-start | bytes 2293760 | tf_op jit(solution)/shard_map/all_to_all | solution.py:454
  16.6 4.0 %collective-permute-start.2 = (bf16[128,896]{1,0:T(8,128)(2,1)S(1)}, bf16[128,896]{1,0:T(8,128)(2,1)S(1)}, u32[]{:S(2)}, u32[]{:S(2)}) collective-permute-start(bf16[128,896]{1,0:T(8,128)(2,1)S(1)} %copy-done.4), channel_id=1, source_target_pairs={{0,4},{1,5},{2,6},{3,7},{4,0},{5,1},{6,2},{7,3},{8,12},{9,13},{10,... | collective-permute-start | bytes 688136 | tf_op jit(solution)/shard_map/ppermute | solution.py:448
  21.3 1.3 collective-permute-start
  23.3 3.8 %collective-permute-done.2.t3 = bf16[128,896]{1,0:T(8,128)(2,1)S(1)} collective-permute-done((bf16[128,896]{1,0:T(8,128)(2,1)S(1)}, bf16[128,896]{1,0:T(8,128)(2,1)S(1)}, u32[]{:S(2)}, u32[]{:S(2)}) %collective-permute-start.2) | collective-permute-done | bytes 229408 | tf_op jit(solution)/shard_map/ppermute | solution.py:448
  27.0 4.5 %collective-permute-done.1.t2 = bf16[128,896]{1,0:T(8,128)(2,1)S(1)} collective-permute-done((bf16[128,896]{1,0:T(8,128)(2,1)S(1)}, bf16[128,896]{1,0:T(8,128)(2,1)S(1)}, u32[]{:S(2)}, u32[]{:S(2)}) %collective-permute-start.1) | collective-permute-done | bytes 229408 | tf_op jit(solution)/shard_map/ppermute | solution.py:448
  32.3 3.1 %spread.2 = bf16[16,4,16,896]{3,2,1,0:T(8,128)(2,1)} custom-call(bf16[16,16,128]{2,1,0:T(8,128)(2,1)} %get-tuple-element.66.table_ref.refs_0_, bf16[128,896]{1,0:T(8,128)(2,1)} %t0.3, bf16[128,896]{1,0:T(8,128)(2,1)} %copy-done.7, bf16[128,896]{1,0:T(8,128)(2,1)} %copy-done.6, bf16[128,896]{1,0:T(8,128)(2,1)} %copy-done.5), custom_call_target="tpu_custom_call" | custom-call | flops 1000 | bytes 1000 | tf_op jit(solution)/shard_map/spread/pallas_call | solution.py:107
  35.5 1.0 slice.20
  36.5 1.1 copy.15
  37.6 6.9 %all-to-all-start.1 = ((bf16[16,4,16,896]{3,2,1,0:T(8,128)(2,1)}), bf16[16,4,16,896]{3,2,1,0:T(8,128)(2,1)S(1)}, u32[]{:S(2)}, u32[]{:S(2)}) async-start(bf16[16,4,16,896]{3,2,1,0:T(8,128)(2,1)} %spread.2), calls=%async_computation.1 | async-start | bytes 3670016 | tf_op jit(solution)/shard_map/all_to_all | solution.py:454
  44.5 3.1 %spread.3 = bf16[16,4,16,896]{3,2,1,0:T(8,128)(2,1)} custom-call(bf16[16,16,128]{2,1,0:T(8,128)(2,1)} %get-tuple-element.65.table_ref.refs_1_, bf16[128,896]{1,0:T(8,128)(2,1)} %t0.3, bf16[128,896]{1,0:T(8,128)(2,1)} %copy-done.7, bf16[128,896]{1,0:T(8,128)(2,1)} %copy-done.6, bf16[128,896]{1,0:T(8,128)(2,1)} %copy-done.5), custom_call_target="tpu_custom_call" | custom-call | flops 1000 | bytes 1000 | tf_op jit(solution)/shard_map/spread/pallas_call | solution.py:107
  47.6 23.2 %all-to-all-done.1.own_ref = bf16[16,4,16,896]{3,2,1,0:T(8,128)(2,1)S(1)} async-done(((bf16[16,4,16,896]{3,2,1,0:T(8,128)(2,1)}), bf16[16,4,16,896]{3,2,1,0:T(8,128)(2,1)S(1)}, u32[]{:S(2)}, u32[]{:S(2)}) %all-to-all-start.1) | async-done | bytes 1835040 | tf_op jit(solution)/shard_map/all_to_all | solution.py:454
  70.9 1.3 copy-done.3
  72.1 4.4 %all-to-all-start.2 = ((bf16[16,4,16,896]{3,2,1,0:T(8,128)(2,1)}), bf16[16,4,16,896]{3,2,1,0:T(8,128)(2,1)}, u32[]{:S(2)}, u32[]{:S(2)}) async-start(bf16[16,4,16,896]{3,2,1,0:T(8,128)(2,1)} %spread.3), calls=%async_computation.2 | async-start | bytes 3670016 | tf_op jit(solution)/shard_map/all_to_all | solution.py:454
  76.6 8.8 %first_pass.2 = (bf16[256,768]{1,0:T(8,128)(2,1)}, bf16[256,896]{1,0:T(8,128)(2,1)}, bf16[256,896]{1,0:T(8,128)(2,1)}, bf16[256,896]{1,0:T(8,128)(2,1)}, bf16[256,896]{1,0:T(8,128)(2,1)}) custom-call(bf16[16,4,16,896]{3,2,1,0:T(8,128)(2,1)} %copy-done.3, bf16[16,4,16,896]{3,2,1,0:T(8,128)(2,1)} %collective-permute-done.3.other_ref, ...), custom_call_target="tpu_custom_call" | custom-call | flops 1000 | bytes 1000 | tf_op jit(solution)/shard_map/first_pass/pallas_call | solution.py:301
  86.6 17.1 %last_pass.1 = bf16[8,512,896]{2,1,0:T(8,128)(2,1)} custom-call(bf16[8,512,896]{2,1,0:T(8,128)(2,1)} %bitcast.17, bf16[384,7168]{1,0:T(8,128)(2,1)} %bitcast.12, bf16[3,7168,128]{2,1,0:T(8,128)(2,1)} %w_gate_ref.9, bf16[3,7168,128]{2,1,0:T(8,128)(2,1)} %w_up_ref.9, f32[16,64,3]{2,1,0:T(8,128)} %bitcast.15, bf16[3,16,64,128]{3,2,1,0:T(8,128)(2,1)} %bitcast.19, ...), custom_call_target="tpu_custom_call" | custom-call | flops 1000 | bytes 1000 | tf_op jit(solution)/shard_map/last_pass/pallas_call | solution.py:230
  105.2 5.7 %own_pass.3 = bf16[16,4,16,896]{3,2,1,0:T(8,128)(2,1)} custom-call(bf16[256,768]{1,0:T(8,128)(2,1)} %get-tuple-element.54.grads_ref, bf16[3,7168,128]{2,1,0:T(8,128)(2,1)} %w_gate_ref.9, bf16[3,7168,128]{2,1,0:T(8,128)(2,1)} %w_up_ref.9, bf16[256,896]{1,0:T(8,128)(2,1)} %copy-done.8, bf16[256,896]{1,0:T(8,128)(2,1)} %copy-done.9, ...), custom_call_target="tpu_custom_call" | custom-call | flops 1000 | bytes 1000 | tf_op jit(solution)/shard_map/own_pass/pallas_call | solution.py:362
  110.8 6.9 %all-to-all-start.3 = ((bf16[16,4,16,896]{3,2,1,0:T(8,128)(2,1)}), bf16[16,4,16,896]{3,2,1,0:T(8,128)(2,1)S(1)}, u32[]{:S(2)}, u32[]{:S(2)}) async-start(bf16[16,4,16,896]{3,2,1,0:T(8,128)(2,1)} %own_pass.3), calls=%async_computation.4 | async-start | bytes 3670016 | tf_op jit(solution)/shard_map/all_to_all | solution.py:454
  117.8 8.8 %first_pass.3 = (bf16[256,768]{1,0:T(8,128)(2,1)}, bf16[256,896]{1,0:T(8,128)(2,1)}, bf16[256,896]{1,0:T(8,128)(2,1)}, bf16[256,896]{1,0:T(8,128)(2,1)}, bf16[256,896]{1,0:T(8,128)(2,1)}) custom-call(bf16[16,4,16,896]{3,2,1,0:T(8,128)(2,1)} %all-to-all-done.2.own_ref, bf16[16,4,16,896]{3,2,1,0:T(8,128)(2,1)} %collective-permute-done.8.other_ref, ...), custom_call_target="tpu_custom_call" | custom-call | flops 1000 | bytes 1000 | tf_op jit(solution)/shard_map/first_pass/pallas_call | solution.py:301
  127.7 1.0 collective-permute-done.9.refs_0_
  129.3 0.8 collective-permute-done.11.refs_2_
  131.6 5.8 %own_pass.2 = bf16[16,4,16,896]{3,2,1,0:T(8,128)(2,1)} custom-call(bf16[256,768]{1,0:T(8,128)(2,1)} %get-tuple-element.49.grads_ref, bf16[3,7168,128]{2,1,0:T(8,128)(2,1)} %w_gate_ref.9, bf16[3,7168,128]{2,1,0:T(8,128)(2,1)} %w_up_ref.9, bf16[256,896]{1,0:T(8,128)(2,1)} %copy-done.12, bf16[256,896]{1,0:T(8,128)(2,1)} %copy-done.13, ...), custom_call_target="tpu_custom_call" | custom-call | flops 1000 | bytes 1000 | tf_op jit(solution)/shard_map/own_pass/pallas_call | solution.py:362
  137.4 10.7 %all-to-all-done.3.refs_2_ = bf16[16,4,16,896]{3,2,1,0:T(8,128)(2,1)S(1)} async-done(((bf16[16,4,16,896]{3,2,1,0:T(8,128)(2,1)}), bf16[16,4,16,896]{3,2,1,0:T(8,128)(2,1)S(1)}, u32[]{:S(2)}, u32[]{:S(2)}) %all-to-all-start.3) | async-done | bytes 1835040 | tf_op jit(solution)/shard_map/all_to_all | solution.py:454
  148.1 29.8 %all_to_all.30.refs_3_ = bf16[16,4,16,896]{3,2,1,0:T(8,128)(2,1)} all-to-all(bf16[16,4,16,896]{3,2,1,0:T(8,128)(2,1)} %own_pass.2), channel_id=1, replica_groups=mesh['group'=16,'local'=8] {'group'}, dimensions={0} | all-to-all | bytes 3670016 | tf_op jit(solution)/shard_map/all_to_all | solution.py:454
  177.8 3.8 %all-to-all-start.5 = ((bf16[16,32,896]{2,1,0:T(8,128)(2,1)}), bf16[16,32,896]{2,1,0:T(8,128)(2,1)S(1)}, u32[]{:S(2)}, u32[]{:S(2)}) async-start(bf16[16,32,896]{2,1,0:T(8,128)(2,1)} %bitcast.25), calls=%async_computation.6 | async-start | bytes 1835008 | tf_op jit(solution)/shard_map/all_to_all | solution.py:454
  181.6 1.5 copy-done
  183.1 0.7 collect.1
  183.9 4.7 %collective-permute-start.13 = (bf16[128,896]{1,0:T(8,128)(2,1)S(1)}, bf16[128,896]{1,0:T(8,128)(2,1)S(1)}, u32[]{:S(2)}, u32[]{:S(2)}) collective-permute-start(bf16[128,896]{1,0:T(8,128)(2,1)S(1)} %get-tuple-element.62), channel_id=1, source_target_pairs={{0,6},{1,7},{2,0},{3,1},{4,2},{5,3},{6,4},{7,5},{8,14},{9,15},{10,... | collective-permute-start | bytes 688136 | tf_op jit(solution)/shard_map/ppermute | solution.py:448
  188.6 1.9 collective-permute-start.15
  190.5 6.5 %collective-permute-done.13.a_ref = bf16[128,896]{1,0:T(8,128)(2,1)S(1)} collective-permute-done((bf16[128,896]{1,0:T(8,128)(2,1)S(1)}, bf16[128,896]{1,0:T(8,128)(2,1)S(1)}, u32[]{:S(2)}, u32[]{:S(2)}) %collective-permute-start.13) | collective-permute-done | bytes 229408 | tf_op jit(solution)/shard_map/ppermute | solution.py:448
  197.0 3.3 %collective-permute-done.14.b_ref = bf16[128,896]{1,0:T(8,128)(2,1)S(1)} collective-permute-done((bf16[128,896]{1,0:T(8,128)(2,1)S(1)}, bf16[128,896]{1,0:T(8,128)(2,1)S(1)}, u32[]{:S(2)}, u32[]{:S(2)}) %collective-permute-start.14) | collective-permute-done | bytes 229408 | tf_op jit(solution)/shard_map/ppermute | solution.py:448
  200.4 1.0 finish.1
  (69 shorter events, 8.0 us)
Async XLA Ops:
  6.5 10.1 %copy-start.4 = (bf16[128,896]{1,0:T(8,128)(2,1)S(1)}, bf16[128,896]{1,0:T(8,128)(2,1)}, u32[]{:S(2)}) copy-start(bf16[128,896]{1,0:T(8,128)(2,1)} %t0.3) | copy-start | bytes 688132
  9.3 13.3 %copy-start.16 = (bf16[16,64,128]{2,1,0:T(8,128)(2,1)S(1)}, bf16[16,64,128]{2,1,0:T(8,128)(2,1)}, u32[]{:S(2)}) copy-start(bf16[16,64,128]{2,1,0:T(8,128)(2,1)} %get-tuple-element.35) | copy-start | bytes 786436
  9.3 26.2 %all-to-all-start = ((bf16[16,40,896]{2,1,0:T(8,128)(2,1)}), bf16[16,40,896]{2,1,0:T(8,128)(2,1)S(1)}, u32[]{:S(2)}, u32[]{:S(2)}) async-start(bf16[16,40,896]{2,1,0:T(8,128)(2,1)} %get-tuple-element.36), calls=%async_computation | async-start | bytes 2293760 | tf_op jit(solution)/shard_map/all_to_all | solution.py:454
  16.5 70.0 %all-gather.3.cloned.1.call-start = ((), (), s32[]{:S(2)}) async-start(), calls=%async_computation.8 | async-start | bytes 8257536 | tf_op jit(solution)/shard_map/all_gather | solution.py:469
  16.6 10.4 %collective-permute-start.2 = (bf16[128,896]{1,0:T(8,128)(2,1)S(1)}, bf16[128,896]{1,0:T(8,128)(2,1)S(1)}, u32[]{:S(2)}, u32[]{:S(2)}) collective-permute-start(bf16[128,896]{1,0:T(8,128)(2,1)S(1)} %copy-done.4), channel_id=1, source_target_pairs={{0,4},{1,5},{2,6},{3,7},{4,0},{5,1},{6,2},{7,3},{8,12},{9,13},{10,... | collective-permute-start | bytes 688136 | tf_op jit(solution)/shard_map/ppermute | solution.py:448
  20.6 11.0 %collective-permute-start.1 = (bf16[128,896]{1,0:T(8,128)(2,1)S(1)}, bf16[128,896]{1,0:T(8,128)(2,1)S(1)}, u32[]{:S(2)}, u32[]{:S(2)}) collective-permute-start(bf16[128,896]{1,0:T(8,128)(2,1)S(1)} %copy-done.4), channel_id=1, source_target_pairs={{0,6},{1,7},{2,0},{3,1},{4,2},{5,3},{6,4},{7,5},{8,14},{9,15},{10,... | collective-permute-start | bytes 688136 | tf_op jit(solution)/shard_map/ppermute | solution.py:448
  21.3 10.3 %collective-permute-start = (bf16[128,896]{1,0:T(8,128)(2,1)S(1)}, bf16[128,896]{1,0:T(8,128)(2,1)S(1)}, u32[]{:S(2)}, u32[]{:S(2)}) collective-permute-start(bf16[128,896]{1,0:T(8,128)(2,1)S(1)} %copy-done.4), channel_id=1, source_target_pairs={{0,2},{1,3},{2,4},{3,5},{4,6},{5,7},{6,0},{7,1},{8,10},{9,11},{10,... | collective-permute-start | bytes 688136 | tf_op jit(solution)/shard_map/ppermute | solution.py:448
  27.0 4.5 %copy-start.5 = (bf16[128,896]{1,0:T(8,128)(2,1)}, bf16[128,896]{1,0:T(8,128)(2,1)S(1)}, u32[]{:S(2)}) copy-start(bf16[128,896]{1,0:T(8,128)(2,1)S(1)} %collective-permute-done.2.t3) | copy-start | bytes 688132
  37.6 33.3 %all-to-all-start.1 = ((bf16[16,4,16,896]{3,2,1,0:T(8,128)(2,1)}), bf16[16,4,16,896]{3,2,1,0:T(8,128)(2,1)S(1)}, u32[]{:S(2)}, u32[]{:S(2)}) async-start(bf16[16,4,16,896]{3,2,1,0:T(8,128)(2,1)} %spread.2), calls=%async_computation.1 | async-start | bytes 3670016 | tf_op jit(solution)/shard_map/all_to_all | solution.py:454
  70.9 5.7 %collective-permute-start.3 = (bf16[16,4,16,896]{3,2,1,0:T(8,128)(2,1)S(1)}, bf16[16,4,16,896]{3,2,1,0:T(8,128)(2,1)}, u32[]{:S(2)}, u32[]{:S(2)}) collective-permute-start(bf16[16,4,16,896]{3,2,1,0:T(8,128)(2,1)S(1)} %all-to-all-done.1.own_ref), channel_id=1, source_target_pairs={{0,1},{1,0},{2,3},{3,2},{4,5},{5,4},{6,7},{7,6},{8,9},{9,8},{10,11... | collective-permute-start | bytes 5505032 | tf_op jit(solution)/shard_map/ppermute | solution.py:451
  72.1 31.8 %all-to-all-start.2 = ((bf16[16,4,16,896]{3,2,1,0:T(8,128)(2,1)}), bf16[16,4,16,896]{3,2,1,0:T(8,128)(2,1)}, u32[]{:S(2)}, u32[]{:S(2)}) async-start(bf16[16,4,16,896]{3,2,1,0:T(8,128)(2,1)} %spread.3), calls=%async_computation.2 | async-start | bytes 3670016 | tf_op jit(solution)/shard_map/all_to_all | solution.py:454
  76.6 101.3 %reduce-scatter.2.cloned.1.call-start = ((), (), s32[]{:S(2)}) async-start(), calls=%async_computation.7 | async-start | bytes 8257536 | tf_op jit(solution)/shard_map/reduce_scatter | solution.py:488
  85.5 18.5 %collective-permute-start.4 = (bf16[256,896]{1,0:T(8,128)(2,1)}, bf16[256,896]{1,0:T(8,128)(2,1)S(1)}, u32[]{:S(2)}, u32[]{:S(2)}) collective-permute-start(bf16[256,896]{1,0:T(8,128)(2,1)} %get-tuple-element.43), channel_id=1, source_target_pairs={{0,1},{1,0},{2,3},{3,2},{4,5},{5,4},{6,7},{7,6},{8,9},{9,8},{10,11... | collective-permute-start | bytes 1376264 | tf_op jit(solution)/shard_map/ppermute | solution.py:451
  85.5 18.4 %collective-permute-start.5 = (bf16[256,896]{1,0:T(8,128)(2,1)}, bf16[256,896]{1,0:T(8,128)(2,1)S(1)}, u32[]{:S(2)}, u32[]{:S(2)}) collective-permute-start(bf16[256,896]{1,0:T(8,128)(2,1)} %get-tuple-element.44), channel_id=1, source_target_pairs={{0,1},{1,0},{2,3},{3,2},{4,5},{5,4},{6,7},{7,6},{8,9},{9,8},{10,11... | collective-permute-start | bytes 1376264 | tf_op jit(solution)/shard_map/ppermute | solution.py:451
  86.0 17.9 %collective-permute-start.6 = (bf16[256,896]{1,0:T(8,128)(2,1)}, bf16[256,896]{1,0:T(8,128)(2,1)S(1)}, u32[]{:S(2)}, u32[]{:S(2)}) collective-permute-start(bf16[256,896]{1,0:T(8,128)(2,1)} %get-tuple-element.45), channel_id=1, source_target_pairs={{0,1},{1,0},{2,3},{3,2},{4,5},{5,4},{6,7},{7,6},{8,9},{9,8},{10,11... | collective-permute-start | bytes 1376264 | tf_op jit(solution)/shard_map/ppermute | solution.py:451
  86.1 17.8 %collective-permute-start.7 = (bf16[256,896]{1,0:T(8,128)(2,1)}, bf16[256,896]{1,0:T(8,128)(2,1)S(1)}, u32[]{:S(2)}, u32[]{:S(2)}) collective-permute-start(bf16[256,896]{1,0:T(8,128)(2,1)} %get-tuple-element.46), channel_id=1, source_target_pairs={{0,1},{1,0},{2,3},{3,2},{4,5},{5,4},{6,7},{7,6},{8,9},{9,8},{10,11... | collective-permute-start | bytes 1376264 | tf_op jit(solution)/shard_map/ppermute | solution.py:451
  105.2 12.6 %collective-permute-start.8 = (bf16[16,4,16,896]{3,2,1,0:T(8,128)(2,1)}, bf16[16,4,16,896]{3,2,1,0:T(8,128)(2,1)}, u32[]{:S(2)}, u32[]{:S(2)}) collective-permute-start(bf16[16,4,16,896]{3,2,1,0:T(8,128)(2,1)} %all-to-all-done.2.own_ref), channel_id=1, source_target_pairs={{0,1},{1,0},{2,3},{3,2},{4,5},{5,4},{6,7},{7,6},{8,9},{9,8},{10,11... | collective-permute-start | bytes 5505032 | tf_op jit(solution)/shard_map/ppermute | solution.py:451
  110.8 37.2 %all-to-all-start.3 = ((bf16[16,4,16,896]{3,2,1,0:T(8,128)(2,1)}), bf16[16,4,16,896]{3,2,1,0:T(8,128)(2,1)S(1)}, u32[]{:S(2)}, u32[]{:S(2)}) async-start(bf16[16,4,16,896]{3,2,1,0:T(8,128)(2,1)} %own_pass.3), calls=%async_computation.4 | async-start | bytes 3670016 | tf_op jit(solution)/shard_map/all_to_all | solution.py:454
  126.6 2.1 %collective-permute-start.9 = (bf16[256,896]{1,0:T(8,128)(2,1)}, bf16[256,896]{1,0:T(8,128)(2,1)S(1)}, u32[]{:S(2)}, u32[]{:S(2)}) collective-permute-start(bf16[256,896]{1,0:T(8,128)(2,1)} %get-tuple-element.50), channel_id=1, source_target_pairs={{0,1},{1,0},{2,3},{3,2},{4,5},{5,4},{6,7},{7,6},{8,9},{9,8},{10,11... | collective-permute-start | bytes 1376264 | tf_op jit(solution)/shard_map/ppermute | solution.py:451
  126.7 2.6 %collective-permute-start.10 = (bf16[256,896]{1,0:T(8,128)(2,1)}, bf16[256,896]{1,0:T(8,128)(2,1)S(1)}, u32[]{:S(2)}, u32[]{:S(2)}) collective-permute-start(bf16[256,896]{1,0:T(8,128)(2,1)} %get-tuple-element.51), channel_id=1, source_target_pairs={{0,1},{1,0},{2,3},{3,2},{4,5},{5,4},{6,7},{7,6},{8,9},{9,8},{10,11... | collective-permute-start | bytes 1376264 | tf_op jit(solution)/shard_map/ppermute | solution.py:451
  127.1 3.0 %collective-permute-start.11 = (bf16[256,896]{1,0:T(8,128)(2,1)}, bf16[256,896]{1,0:T(8,128)(2,1)S(1)}, u32[]{:S(2)}, u32[]{:S(2)}) collective-permute-start(bf16[256,896]{1,0:T(8,128)(2,1)} %get-tuple-element.52), channel_id=1, source_target_pairs={{0,1},{1,0},{2,3},{3,2},{4,5},{5,4},{6,7},{7,6},{8,9},{9,8},{10,11... | collective-permute-start | bytes 1376264 | tf_op jit(solution)/shard_map/ppermute | solution.py:451
  127.2 3.6 %collective-permute-start.12 = (bf16[256,896]{1,0:T(8,128)(2,1)}, bf16[256,896]{1,0:T(8,128)(2,1)S(1)}, u32[]{:S(2)}, u32[]{:S(2)}) collective-permute-start(bf16[256,896]{1,0:T(8,128)(2,1)} %get-tuple-element.53), channel_id=1, source_target_pairs={{0,1},{1,0},{2,3},{3,2},{4,5},{5,4},{6,7},{7,6},{8,9},{9,8},{10,11... | collective-permute-start | bytes 1376264 | tf_op jit(solution)/shard_map/ppermute | solution.py:451
  128.7 2.1 %copy-start.12 = (bf16[256,896]{1,0:T(8,128)(2,1)}, bf16[256,896]{1,0:T(8,128)(2,1)S(1)}, u32[]{:S(2)}) copy-start(bf16[256,896]{1,0:T(8,128)(2,1)S(1)} %collective-permute-done.9.refs_0_) | copy-start | bytes 1376260
  129.3 1.5 copy-start.13
  177.8 3.8 %copy-start.1 = (bf16[16,16,128]{2,1,0:T(8,128)(2,1)S(1)}, bf16[16,16,128]{2,1,0:T(8,128)(2,1)}, u32[]{:S(2)}) copy-start(bf16[16,16,128]{2,1,0:T(8,128)(2,1)} %get-tuple-element.65.table_ref.refs_1_) | copy-start | bytes 196612
  177.8 3.8 %copy-start.2 = (bf16[16,16,128]{2,1,0:T(8,128)(2,1)S(1)}, bf16[16,16,128]{2,1,0:T(8,128)(2,1)}, u32[]{:S(2)}) copy-start(bf16[16,16,128]{2,1,0:T(8,128)(2,1)} %get-tuple-element.66.table_ref.refs_0_) | copy-start | bytes 196612
  177.8 22.5 %all-to-all-start.5 = ((bf16[16,32,896]{2,1,0:T(8,128)(2,1)}), bf16[16,32,896]{2,1,0:T(8,128)(2,1)S(1)}, u32[]{:S(2)}, u32[]{:S(2)}) async-start(bf16[16,32,896]{2,1,0:T(8,128)(2,1)} %bitcast.25), calls=%async_computation.6 | async-start | bytes 1835008 | tf_op jit(solution)/shard_map/all_to_all | solution.py:454
  181.6 1.5 copy-start
  183.1 7.4 %copy-start.17 = (bf16[16,64,128]{2,1,0:T(8,128)(2,1)S(1)}, bf16[16,64,128]{2,1,0:T(8,128)(2,1)}, u32[]{:S(2)}) copy-start(bf16[16,64,128]{2,1,0:T(8,128)(2,1)} %get-tuple-element.35) | copy-start | bytes 786436
  183.9 13.1 %collective-permute-start.13 = (bf16[128,896]{1,0:T(8,128)(2,1)S(1)}, bf16[128,896]{1,0:T(8,128)(2,1)S(1)}, u32[]{:S(2)}, u32[]{:S(2)}) collective-permute-start(bf16[128,896]{1,0:T(8,128)(2,1)S(1)} %get-tuple-element.62), channel_id=1, source_target_pairs={{0,6},{1,7},{2,0},{3,1},{4,2},{5,3},{6,4},{7,5},{8,14},{9,15},{10,... | collective-permute-start | bytes 688136 | tf_op jit(solution)/shard_map/ppermute | solution.py:448
  188.6 11.8 %collective-permute-start.14 = (bf16[128,896]{1,0:T(8,128)(2,1)S(1)}, bf16[128,896]{1,0:T(8,128)(2,1)S(1)}, u32[]{:S(2)}, u32[]{:S(2)}) collective-permute-start(bf16[128,896]{1,0:T(8,128)(2,1)S(1)} %get-tuple-element.63), channel_id=1, source_target_pairs={{0,2},{1,3},{2,4},{3,5},{4,6},{5,7},{6,0},{7,1},{8,10},{9,11},{10,... | collective-permute-start | bytes 688136 | tf_op jit(solution)/shard_map/ppermute | solution.py:448
  188.6 11.8 %collective-permute-start.15 = (bf16[128,896]{1,0:T(8,128)(2,1)S(1)}, bf16[128,896]{1,0:T(8,128)(2,1)S(1)}, u32[]{:S(2)}, u32[]{:S(2)}) collective-permute-start(bf16[128,896]{1,0:T(8,128)(2,1)S(1)} %get-tuple-element.64), channel_id=1, source_target_pairs={{0,4},{1,5},{2,6},{3,7},{4,0},{5,1},{6,2},{7,3},{8,12},{9,13},{10,... | collective-permute-start | bytes 688136 | tf_op jit(solution)/shard_map/ppermute | solution.py:448
  (9 other events, 8.2 us)
Sparse Core Ops, SparseCore 0:
  36.6 46.3 all-gather.2
  104.1 50.4 reduce-scatter.1

commit v4 on v3

--- a/solution.py
+++ b/solution.py
@@ -13,6 +13,7 @@
 Z_LAST = (0, 32)
 Z_FIRST = ((32, 16), (48, 16))
 Z_OFFSETS = (0, -1, 1, 2)
+CHIPS = len(Z_OFFSETS)
 VMEM = 60 * 1024 * 1024
 BF = jnp.bfloat16
 F32 = jnp.float32
@@ -25,6 +26,7 @@
 
 
 COST = pl.CostEstimate(flops=1000, bytes_accessed=1000, transcendentals=0)
+SLOW = pl.CostEstimate(flops=150_000_000_000, bytes_accessed=1000, transcendentals=0)
 
 
 def after(value, *earlier):
@@ -184,25 +186,18 @@
     return lax.dot_general(grads, columns, NT, preferred_element_type=F32)
 
 
-def last_kernel(
-    x_ref, down_ref, w_gate_ref, w_up_ref, lane_ref, gate_ref, up_ref, out_ref,
-    x, down, w_gate, w_up, lane, gate, up, grads, out,
-    x_sems, down_sems, w_gate_sems, w_up_sems, saved_sems, out_sems,
+def hidden_last_kernel(
+    x_ref, down_ref, lane_ref, gate_ref, up_ref, out_ref, x, down, lane, gate, up, grads, x_sems, down_sems,
+    saved_sems, out_sems,
 ):
     blocks, _, width = x_ref.shape
     start, count = Z_LAST
-    turns = out.shape[0]
     groups = [
         copies_of([(x_ref.at[k], x.at[k])], x_sems.at[pl.ds(k, 1)])
         + copies_of([(columns_of(down_ref, k, width), down.at[k])], down_sems.at[pl.ds(k, 1)])
         for k in range(blocks)
     ]
     groups[-1] += saved_copies(start, count, lane_ref, gate_ref, up_ref, lane, gate, up, saved_sems)
-    groups += [
-        copies_of([(rows_of(w_gate_ref, k, width), w_gate.at[k])], w_gate_sems.at[pl.ds(k, 1)])
-        + copies_of([(rows_of(w_up_ref, k, width), w_up.at[k])], w_up_sems.at[pl.ds(k, 1)])
-        for k in range(blocks)
-    ]
     stream = Stream(groups)
     total = None
     for k in range(blocks):
@@ -210,9 +205,53 @@
         part = lax.dot_general(x[k], down[k], NT, preferred_element_type=F32)
         total = part if total is None else total + part
     write_grads(total, lane, gate, up, grads)
+    for copy in begin(copies_of([(grads, out_ref)], out_sems)):
+        copy.wait()
+
+
+def hidden_last(rows_in, w_down, lanes, saved_gate, saved_up):
+    blocks, rows, width = rows_in.shape
+    units = saved_gate.shape[3]
+    group_count = lanes.shape[0]
+    count = Z_LAST[1]
+    sems = pltpu.SemaphoreType.DMA
+    return pl.pallas_call(
+        hidden_last_kernel,
+        out_shape=jax.ShapeDtypeStruct((rows, 2 * EXP_GRP * units), BF),
+        in_specs=[ANY] * 5,
+        out_specs=ANY,
+        scratch_shapes=[
+            pltpu.VMEM((blocks, rows, width), BF),
+            pltpu.VMEM((blocks, EXP_GRP * units, width), BF),
+            pltpu.VMEM((group_count, count, EXP_GRP), F32),
+            pltpu.VMEM((EXP_GRP, group_count, count, units), BF),
+            pltpu.VMEM((EXP_GRP, group_count, count, units), BF),
+            pltpu.VMEM((rows, 2 * EXP_GRP * units), BF),
+            sems((blocks,)), sems((blocks,)), sems((3,)), sems((1,)),
+        ],
+        compiler_params=params(),
+        cost_estimate=COST,
+        name="hidden_last",
+    )(rows_in, w_down, lanes, saved_gate, saved_up)
+
+
+def back_last_kernel(
+    grads_ref, w_gate_ref, w_up_ref, out_ref, grads, w_gate, w_up, out, grads_sems, w_gate_sems, w_up_sems, out_sems
+):
+    blocks, _, width = out_ref.shape
+    turns = out.shape[0]
+    arriving = begin(copies_of([(grads_ref, grads)], grads_sems))
+    stream = Stream(
+        [
+            copies_of([(rows_of(w_gate_ref, k, width), w_gate.at[k])], w_gate_sems.at[pl.ds(k, 1)])
+            + copies_of([(rows_of(w_up_ref, k, width), w_up.at[k])], w_up_sems.at[pl.ds(k, 1)])
+            for k in range(blocks)
+        ]
+    )
+    arriving[0].wait()
     leaving = []
     for k in range(blocks):
-        stream.use(blocks + k)
+        stream.use(k)
         if k >= turns:
             leaving[k - turns].wait()
         out[k % turns] = weights_times(grads[...], w_gate[k], w_up[k]).astype(BF)
@@ -221,33 +260,27 @@
         copy.wait()
 
 
-def last_pass(rows_in, w_down, w_gate, w_up, lanes, saved_gate, saved_up):
-    blocks, rows, width = rows_in.shape
+def back_last(grads, w_gate, w_up, blocks):
+    rows, depth = grads.shape
+    width = w_gate.shape[1] // blocks
     units = w_gate.shape[2]
-    group_count = lanes.shape[0]
-    count = Z_LAST[1]
     sems = pltpu.SemaphoreType.DMA
     return pl.pallas_call(
-        last_kernel,
+        back_last_kernel,
         out_shape=jax.ShapeDtypeStruct((blocks, rows, width), BF),
-        in_specs=[ANY] * 7,
+        in_specs=[ANY] * 3,
         out_specs=ANY,
         scratch_shapes=[
-            pltpu.VMEM((blocks, rows, width), BF),
-            pltpu.VMEM((blocks, EXP_GRP * units, width), BF),
+            pltpu.VMEM((rows, depth), BF),
             pltpu.VMEM((blocks, EXP_GRP, width, units), BF),
             pltpu.VMEM((blocks, EXP_GRP, width, units), BF),
-            pltpu.VMEM((group_count, count, EXP_GRP), F32),
-            pltpu.VMEM((EXP_GRP, group_count, count, units), BF),
-            pltpu.VMEM((EXP_GRP, group_count, count, units), BF),
-            pltpu.VMEM((rows, 2 * EXP_GRP * units), BF),
             pltpu.VMEM((3, rows, width), BF),
-            sems((blocks,)), sems((blocks,)), sems((blocks,)), sems((blocks,)), sems((3,)), sems((blocks,)),
+            sems((1,)), sems((blocks,)), sems((blocks,)), sems((blocks,)),
         ],
         compiler_params=params(),
         cost_estimate=COST,
-        name="last_pass",
-    )(rows_in, w_down, w_gate, w_up, lanes, saved_gate, saved_up)
+        name="back_last",
+    )(grads, w_gate, w_up)
 
 
 def first_kernel(
@@ -378,6 +411,24 @@
     )(grads, w_gate, w_up, *others)
 
 
+def cut_kernel(table_ref, *out_refs):
+    for (start, count), out_ref in zip((Z_LAST, *Z_FIRST), out_refs):
+        out_ref[...] = table_ref[:, start : start + count]
+
+
+def cut(table):
+    group_count, _, tok_rows = table.shape
+    return pl.pallas_call(
+        cut_kernel,
+        out_shape=tuple(
+            jax.ShapeDtypeStruct((group_count, count, tok_rows), BF) for _, count in (Z_LAST, *Z_FIRST)
+        ),
+        compiler_params=params(16 * 1024 * 1024),
+        cost_estimate=SLOW,
+        name="cut",
+    )(table)
+
+
 def collect_kernel(*refs):
     count = len(Z_FIRST)
     tables, arrived, outs = refs[:count], refs[count : 2 * count], refs[2 * count :]
@@ -473,8 +524,8 @@
         tiled=False,
     )
 
-    own = [exchange(after(sent[0], lanes))]
-    own[0], sent[1] = lax.optimization_barrier((own[0], sent[1]))
+    own = [exchange(after(sent[0], first_in))]
+    own[0], sent[1], lanes = lax.optimization_barrier((own[0], sent[1], lanes))
     other = [swap(own[0])]
     own.append(exchange(sent[1]))
 
@@ -483,21 +534,27 @@
         return grads, [swap(piece) for piece in away]
 
     grads, others = first(0)
-    last_part = last_pass(after(last_rows, grads), down, w_gate, w_up, lanes, gate_slots, up_slots)
-    last_part, own[1], grads, *others = lax.optimization_barrier((last_part, own[1], grads, *others))
+    last_grads = hidden_last(after(last_rows, grads), down, lanes, gate_slots, up_slots)
+    last_grads, grads, *others = lax.optimization_barrier((last_grads, grads, *others))
+    ready = own_pass(grads, w_gate, w_up, others, group_count)
+    ready, last_grads, own[1] = lax.optimization_barrier((ready, last_grads, own[1]))
+    first_home = exchange(ready)
+    last_part = back_last(last_grads, w_gate, w_up, local_count)
     last_sum = lax.psum_scatter(last_part, "local", scatter_dimension=0, tiled=False)
+
+    other.append(swap(own[1]))
+    own[1] = after(own[1], last_part)
+    grads, others = first(1)
     ready = own_pass(grads, w_gate, w_up, others, group_count)
-    first_home = exchange(ready)
-
-    other.append(swap(own[1]))
-    grads, others = first(1)
-    second_home = exchange(after(own_pass(grads, w_gate, w_up, others, group_count), first_home))
+    ready, first_home, table = lax.optimization_barrier((ready, first_home, table))
+    last_table, *tables = cut(table)
+    second_home = exchange(after(ready, first_home, last_table))
     returned = [first_home, second_home]
 
     last_home = exchange(after(last_sum, second_home).reshape(group_count, first_count, width))
     pieces = collect(tables, returned)
     others = [shift(piece, by) for piece, by in zip(pieces[1:], Z_OFFSETS[1:])]
-    return finish(table[:, :first_count], last_home, pieces[0], others)
+    return finish(last_table, last_home, pieces[0], others)
 
 
 def solution(mesh):

time: 209 us -> 213 us (1.019)
  blocking collectives: 29.8 us -> 33 us
  Pallas kernels: 56.9 us -> 59.4 us
    all_to_all x5, waiting for transfers between devices: 34.1 us -> 23.6 us  [exchange(): lax.all_to_all(value, 'group', split_axis=0, concat_axis=0, tiled=True)]
    reduce_scatter x1, waiting for transfers between devices: 0.01 us -> 7.11 us  [on_device(): lax.psum_scatter(last_part, 'local', scatter_dimension=0, tiled=False)]
    ppermute x6, starting transfers between devices: 12.6 us -> 8.75 us  [shift(): return lax.ppermute(value, 'local', pairs)]
    all_to_all x1, blocking collectives: 29.8 us -> 33 us  [exchange(): lax.all_to_all(value, 'group', split_axis=0, concat_axis=0, tiled=True)]
    pallas_call x1 -> x3, Pallas kernels: 17.1 us -> 19.8 us  [the longest x1 11.3 us: back_last(): pl.pallas_call(back_last_kernel, out_shape=jax.ShapeDtypeStruct((blocks,...]
    unnamed x36 -> x30, local copies, waits for them, and re-layouts: 5.47 us -> 7.4 us
where the time goes in v4:
time: 213 us; the launch traced here: 212 us
  Pallas kernels  59.4 us (28%)
  waiting for transfers between devices  53.9 us (25%)
  starting transfers between devices  42.4 us (20%)
  blocking collectives  33 us (15%)
  between operations  13.7 us (6%)
  local copies, waits for them, and re-layouts  10.2 us (5%)
    all_to_all x1, blocking collectives, exchange(): lax.all_to_all(value, 'group', split_axis=0, concat_axis=0, tiled=True)  33 us
    all_to_all x5, starting transfers between devices, exchange(): lax.all_to_all(value, 'group', split_axis=0, concat_axis=0, tiled=True)  31.2 us
    all_to_all x5, waiting for transfers between devices, exchange(): lax.all_to_all(value, 'group', split_axis=0, concat_axis=0, tiled=True)  23.6 us
    ppermute x6, waiting for transfers between devices, shift(): return lax.ppermute(value, 'local', pairs)  20 us
    pallas_call x2, Pallas kernels, first_pass(): pl.pallas_call(functools.partial(first_kernel, start), out_shape=(jax.Sha...  17.3 us
    pallas_call x2, Pallas kernels, own_pass(): pl.pallas_call(own_kernel, out_shape=jax.ShapeDtypeStruct((group_count, c...  11.3 us
    pallas_call x1, Pallas kernels, back_last(): pl.pallas_call(back_last_kernel, out_shape=jax.ShapeDtypeStruct((blocks,...  11.3 us
    ppermute x6, starting transfers between devices, shift(): return lax.ppermute(value, 'local', pairs)  8.75 us
  transfers between devices with their start and end apart: 23, of which 11 were waited for; matrix products, arithmetic and copies ran while one was open for 1% of the time, Pallas kernels for 26%

profile of v4, /device:TPU:0, one launch (start us, length us, event | category | flops | bytes accessed | tf_op | source)
XLA Modules:
  0.0 212.5 jit_solution(12074534199687379468)
XLA Ops:
  6.5 2.7 %route.1 = (bf16[16,64,128]{2,1,0:T(8,128)(2,1)}, bf16[16,40,896]{2,1,0:T(8,128)(2,1)}) custom-call(s32[4,128]{1,0:T(4,128)} %bitcast.28, s32[8,128]{1,0:T(8,128)} %bitcast.26, f32[8,128]{1,0:T(8,128)} %bitcast.27, bf16[128,896]{1,0:T(8,128)(2,1)} %t0.3), custom_call_target="tpu_custom_call" | custom-call | flops 1000 | bytes 1000 | tf_op jit(solution)/shard_map/route/pallas_call | solution.py:86
  9.3 7.2 %all-to-all-start = ((bf16[16,40,896]{2,1,0:T(8,128)(2,1)}), bf16[16,40,896]{2,1,0:T(8,128)(2,1)S(1)}, u32[]{:S(2)}, u32[]{:S(2)}) async-start(bf16[16,40,896]{2,1,0:T(8,128)(2,1)} %get-tuple-element.45), calls=%async_computation | async-start | bytes 2293760 | tf_op jit(solution)/shard_map/all_to_all | solution.py:505
  16.6 4.0 %collective-permute-start.2 = (bf16[128,896]{1,0:T(8,128)(2,1)S(1)}, bf16[128,896]{1,0:T(8,128)(2,1)S(1)}, u32[]{:S(2)}, u32[]{:S(2)}) collective-permute-start(bf16[128,896]{1,0:T(8,128)(2,1)S(1)} %copy-done.4), channel_id=1, source_target_pairs={{0,4},{1,5},{2,6},{3,7},{4,0},{5,1},{6,2},{7,3},{8,12},{9,13},{10,... | collective-permute-start | bytes 688136 | tf_op jit(solution)/shard_map/ppermute | solution.py:499
  21.3 1.3 collective-permute-start
  23.2 3.8 %collective-permute-done.2.t3 = bf16[128,896]{1,0:T(8,128)(2,1)S(1)} collective-permute-done((bf16[128,896]{1,0:T(8,128)(2,1)S(1)}, bf16[128,896]{1,0:T(8,128)(2,1)S(1)}, u32[]{:S(2)}, u32[]{:S(2)}) %collective-permute-start.2) | collective-permute-done | bytes 229408 | tf_op jit(solution)/shard_map/ppermute | solution.py:499
  27.0 4.5 %collective-permute-done.1.t2 = bf16[128,896]{1,0:T(8,128)(2,1)S(1)} collective-permute-done((bf16[128,896]{1,0:T(8,128)(2,1)S(1)}, bf16[128,896]{1,0:T(8,128)(2,1)S(1)}, u32[]{:S(2)}, u32[]{:S(2)}) %collective-permute-start.1) | collective-permute-done | bytes 229408 | tf_op jit(solution)/shard_map/ppermute | solution.py:499
  32.3 3.2 %spread.2 = bf16[16,4,16,896]{3,2,1,0:T(8,128)(2,1)} custom-call(bf16[16,16,128]{2,1,0:T(8,128)(2,1)} %get-tuple-element.86.table_ref, bf16[128,896]{1,0:T(8,128)(2,1)} %t0.3, bf16[128,896]{1,0:T(8,128)(2,1)} %copy-done.7, bf16[128,896]{1,0:T(8,128)(2,1)} %copy-done.6, bf16[128,896]{1,0:T(8,128)(2,1)} %copy-done.5), custom_call_target="tpu_custom_call" | custom-call | flops 1000 | bytes 1000 | tf_op jit(solution)/shard_map/spread/pallas_call | solution.py:109
  35.5 1.0 slice.16
  36.6 6.9 %all-to-all-start.1 = ((bf16[16,4,16,896]{3,2,1,0:T(8,128)(2,1)}), bf16[16,4,16,896]{3,2,1,0:T(8,128)(2,1)S(1)}, u32[]{:S(2)}, u32[]{:S(2)}) async-start(bf16[16,4,16,896]{3,2,1,0:T(8,128)(2,1)} %spread.2), calls=%async_computation.1 | async-start | bytes 3670016 | tf_op jit(solution)/shard_map/all_to_all | solution.py:505
  43.6 3.2 %spread.3 = bf16[16,4,16,896]{3,2,1,0:T(8,128)(2,1)} custom-call(bf16[16,16,128]{2,1,0:T(8,128)(2,1)} %get-tuple-element.85.table_ref, bf16[128,896]{1,0:T(8,128)(2,1)} %t0.3, bf16[128,896]{1,0:T(8,128)(2,1)} %copy-done.7, bf16[128,896]{1,0:T(8,128)(2,1)} %copy-done.6, bf16[128,896]{1,0:T(8,128)(2,1)} %copy-done.5), custom_call_target="tpu_custom_call" | custom-call | flops 1000 | bytes 1000 | tf_op jit(solution)/shard_map/spread/pallas_call | solution.py:109
  46.8 1.1 copy.15
  47.9 22.0 %all-to-all-done.1.own_ref = bf16[16,4,16,896]{3,2,1,0:T(8,128)(2,1)S(1)} async-done(((bf16[16,4,16,896]{3,2,1,0:T(8,128)(2,1)}), bf16[16,4,16,896]{3,2,1,0:T(8,128)(2,1)S(1)}, u32[]{:S(2)}, u32[]{:S(2)}) %all-to-all-start.1) | async-done | bytes 1835040 | tf_op jit(solution)/shard_map/all_to_all | solution.py:505
  69.9 1.2 copy-done.3
  71.2 4.4 %all-to-all-start.2 = ((bf16[16,4,16,896]{3,2,1,0:T(8,128)(2,1)}), bf16[16,4,16,896]{3,2,1,0:T(8,128)(2,1)}, u32[]{:S(2)}, u32[]{:S(2)}) async-start(bf16[16,4,16,896]{3,2,1,0:T(8,128)(2,1)} %spread.3), calls=%async_computation.2 | async-start | bytes 3670016 | tf_op jit(solution)/shard_map/all_to_all | solution.py:505
  75.6 8.7 %first_pass.2 = (bf16[256,768]{1,0:T(8,128)(2,1)}, bf16[256,896]{1,0:T(8,128)(2,1)}, bf16[256,896]{1,0:T(8,128)(2,1)}, bf16[256,896]{1,0:T(8,128)(2,1)}, bf16[256,896]{1,0:T(8,128)(2,1)}) custom-call(bf16[16,4,16,896]{3,2,1,0:T(8,128)(2,1)} %copy-done.3, bf16[16,4,16,896]{3,2,1,0:T(8,128)(2,1)} %collective-permute-done.3.other_ref, ...), custom_call_target="tpu_custom_call" | custom-call | flops 1000 | bytes 1000 | tf_op jit(solution)/shard_map/first_pass/pallas_call | solution.py:334
  85.4 8.5 %hidden_last.1.grads_ref = bf16[512,768]{1,0:T(8,128)(2,1)} custom-call(bf16[8,512,896]{2,1,0:T(8,128)(2,1)} %bitcast.17, bf16[384,7168]{1,0:T(8,128)(2,1)} %bitcast.12, f32[16,64,3]{2,1,0:T(8,128)} %bitcast.15, bf16[3,16,64,128]{3,2,1,0:T(8,128)(2,1)} %bitcast.19, bf16[3,16,64,128]{3,2,1,0:T(8,128)(2,1)} %bitcast.22), custom_call_target="tpu_custom_call" | custom-call | flops 1000 | bytes 1000 | tf_op jit(solution)/shard_map/hidden_last/pallas_call | solution.py:218
  95.8 5.6 %own_pass.2 = bf16[16,4,16,896]{3,2,1,0:T(8,128)(2,1)} custom-call(bf16[256,768]{1,0:T(8,128)(2,1)} %get-tuple-element.57.grads_ref, bf16[3,7168,128]{2,1,0:T(8,128)(2,1)} %w_gate_ref.9, bf16[3,7168,128]{2,1,0:T(8,128)(2,1)} %w_up_ref.9, bf16[256,896]{1,0:T(8,128)(2,1)} %copy-done.8, bf16[256,896]{1,0:T(8,128)(2,1)} %copy-done.10, ...), custom_call_target="tpu_custom_call" | custom-call | flops 1000 | bytes 1000 | tf_op jit(solution)/shard_map/own_pass/pallas_call | solution.py:395
  101.4 1.6 all-to-all-done.2.own_ref
  103.0 5.7 %all-to-all-start.3 = ((bf16[16,4,16,896]{3,2,1,0:T(8,128)(2,1)}), bf16[16,4,16,896]{3,2,1,0:T(8,128)(2,1)S(1)}, u32[]{:S(2)}, u32[]{:S(2)}) async-start(bf16[16,4,16,896]{3,2,1,0:T(8,128)(2,1)} %own_pass.2), calls=%async_computation.3 | async-start | bytes 3670016 | tf_op jit(solution)/shard_map/all_to_all | solution.py:505
  109.0 11.3 %back_last.1 = bf16[8,512,896]{2,1,0:T(8,128)(2,1)} custom-call(bf16[512,768]{1,0:T(8,128)(2,1)} %hidden_last.1.grads_ref, bf16[3,7168,128]{2,1,0:T(8,128)(2,1)} %w_gate_ref.9, bf16[3,7168,128]{2,1,0:T(8,128)(2,1)} %w_up_ref.9), custom_call_target="tpu_custom_call" | custom-call | flops 1000 | bytes 1000 | tf_op jit(solution)/shard_map/back_last/pallas_call | solution.py:268
  120.3 8.7 %first_pass.3 = (bf16[256,768]{1,0:T(8,128)(2,1)}, bf16[256,896]{1,0:T(8,128)(2,1)}, bf16[256,896]{1,0:T(8,128)(2,1)}, bf16[256,896]{1,0:T(8,128)(2,1)}, bf16[256,896]{1,0:T(8,128)(2,1)}) custom-call(bf16[16,4,16,896]{3,2,1,0:T(8,128)(2,1)} %all-to-all-done.2.own_ref, bf16[16,4,16,896]{3,2,1,0:T(8,128)(2,1)} %collective-permute-done.8.other_ref, ...), custom_call_target="tpu_custom_call" | custom-call | flops 1000 | bytes 1000 | tf_op jit(solution)/shard_map/first_pass/pallas_call | solution.py:334
  131.7 1.3 collective-permute-done.11.refs_2_
  133.8 5.7 %own_pass.3 = bf16[16,4,16,896]{3,2,1,0:T(8,128)(2,1)} custom-call(bf16[256,768]{1,0:T(8,128)(2,1)} %get-tuple-element.67.grads_ref, bf16[3,7168,128]{2,1,0:T(8,128)(2,1)} %w_gate_ref.9, bf16[3,7168,128]{2,1,0:T(8,128)(2,1)} %w_up_ref.9, bf16[256,896]{1,0:T(8,128)(2,1)} %copy-done.9, bf16[256,896]{1,0:T(8,128)(2,1)} %copy-done.11, ...), custom_call_target="tpu_custom_call" | custom-call | flops 1000 | bytes 1000 | tf_op jit(solution)/shard_map/own_pass/pallas_call | solution.py:395
  139.5 1.5 copy-done.2
  141.0 33.0 %all_to_all.30.refs_3_ = bf16[16,4,16,896]{3,2,1,0:T(8,128)(2,1)} all-to-all(bf16[16,4,16,896]{3,2,1,0:T(8,128)(2,1)S(1)} %copy-done.2), channel_id=1, replica_groups=mesh['group'=16,'local'=8] {'group'}, dimensions={0} | all-to-all | bytes 3670016 | tf_op jit(solution)/shard_map/all_to_all | solution.py:505
  173.9 7.1 %reduce-scatter.2.cloned.1.call-done = bf16[1,512,896]{2,1,0:T(8,128)(2,1)} async-done(((bf16[8,512,896]{2,1,0:T(8,128)(2,1)}), bf16[1,512,896]{2,1,0:T(8,128)(2,1)}) %reduce-scatter.2.cloned.1.call-update) | async-done | bytes 917520 | tf_op jit(solution)/shard_map/reduce_scatter | solution.py:543
  181.1 6.8 %all-to-all-start.5 = ((bf16[16,32,896]{2,1,0:T(8,128)(2,1)}), bf16[16,32,896]{2,1,0:T(8,128)(2,1)S(1)}, u32[]{:S(2)}, u32[]{:S(2)}) async-start(bf16[16,32,896]{2,1,0:T(8,128)(2,1)} %bitcast.25), calls=%async_computation.6 | async-start | bytes 1835008 | tf_op jit(solution)/shard_map/all_to_all | solution.py:505
  187.9 1.5 copy-done
  191.0 1.3 collective-permute-start.14
  192.9 8.3 %collective-permute-done.13.a_ref = bf16[128,896]{1,0:T(8,128)(2,1)S(1)} collective-permute-done((bf16[128,896]{1,0:T(8,128)(2,1)S(1)}, bf16[128,896]{1,0:T(8,128)(2,1)S(1)}, u32[]{:S(2)}, u32[]{:S(2)}) %collective-permute-start.13) | collective-permute-done | bytes 229408 | tf_op jit(solution)/shard_map/ppermute | solution.py:499
  201.2 3.4 %collective-permute-done.14.b_ref = bf16[128,896]{1,0:T(8,128)(2,1)S(1)} collective-permute-done((bf16[128,896]{1,0:T(8,128)(2,1)S(1)}, bf16[128,896]{1,0:T(8,128)(2,1)S(1)}, u32[]{:S(2)}, u32[]{:S(2)}) %collective-permute-start.14) | collective-permute-done | bytes 229408 | tf_op jit(solution)/shard_map/ppermute | solution.py:499
  204.6 1.0 finish.1
  (64 shorter events, 11.2 us)
Async XLA Ops:
  6.5 10.0 %copy-start.4 = (bf16[128,896]{1,0:T(8,128)(2,1)S(1)}, bf16[128,896]{1,0:T(8,128)(2,1)}, u32[]{:S(2)}) copy-start(bf16[128,896]{1,0:T(8,128)(2,1)} %t0.3) | copy-start | bytes 688132
  9.3 13.3 %copy-start.1 = (bf16[16,64,128]{2,1,0:T(8,128)(2,1)S(1)}, bf16[16,64,128]{2,1,0:T(8,128)(2,1)}, u32[]{:S(2)}) copy-start(bf16[16,64,128]{2,1,0:T(8,128)(2,1)} %get-tuple-element.73.table_ref) | copy-start | bytes 786436
  9.3 26.3 %all-to-all-start = ((bf16[16,40,896]{2,1,0:T(8,128)(2,1)}), bf16[16,40,896]{2,1,0:T(8,128)(2,1)S(1)}, u32[]{:S(2)}, u32[]{:S(2)}) async-start(bf16[16,40,896]{2,1,0:T(8,128)(2,1)} %get-tuple-element.45), calls=%async_computation | async-start | bytes 2293760 | tf_op jit(solution)/shard_map/all_to_all | solution.py:505
  16.5 68.8 %all-gather.3.cloned.1.call-start = ((), (), s32[]{:S(2)}) async-start(), calls=%async_computation.8 | async-start | bytes 8257536 | tf_op jit(solution)/shard_map/all_gather | solution.py:520
  16.6 10.4 %collective-permute-start.2 = (bf16[128,896]{1,0:T(8,128)(2,1)S(1)}, bf16[128,896]{1,0:T(8,128)(2,1)S(1)}, u32[]{:S(2)}, u32[]{:S(2)}) collective-permute-start(bf16[128,896]{1,0:T(8,128)(2,1)S(1)} %copy-done.4), channel_id=1, source_target_pairs={{0,4},{1,5},{2,6},{3,7},{4,0},{5,1},{6,2},{7,3},{8,12},{9,13},{10,... | collective-permute-start | bytes 688136 | tf_op jit(solution)/shard_map/ppermute | solution.py:499
  20.5 11.0 %collective-permute-start.1 = (bf16[128,896]{1,0:T(8,128)(2,1)S(1)}, bf16[128,896]{1,0:T(8,128)(2,1)S(1)}, u32[]{:S(2)}, u32[]{:S(2)}) collective-permute-start(bf16[128,896]{1,0:T(8,128)(2,1)S(1)} %copy-done.4), channel_id=1, source_target_pairs={{0,6},{1,7},{2,0},{3,1},{4,2},{5,3},{6,4},{7,5},{8,14},{9,15},{10,... | collective-permute-start | bytes 688136 | tf_op jit(solution)/shard_map/ppermute | solution.py:499
  21.3 10.3 %collective-permute-start = (bf16[128,896]{1,0:T(8,128)(2,1)S(1)}, bf16[128,896]{1,0:T(8,128)(2,1)S(1)}, u32[]{:S(2)}, u32[]{:S(2)}) collective-permute-start(bf16[128,896]{1,0:T(8,128)(2,1)S(1)} %copy-done.4), channel_id=1, source_target_pairs={{0,2},{1,3},{2,4},{3,5},{4,6},{5,7},{6,0},{7,1},{8,10},{9,11},{10,... | collective-permute-start | bytes 688136 | tf_op jit(solution)/shard_map/ppermute | solution.py:499
  27.0 4.5 %copy-start.5 = (bf16[128,896]{1,0:T(8,128)(2,1)}, bf16[128,896]{1,0:T(8,128)(2,1)S(1)}, u32[]{:S(2)}) copy-start(bf16[128,896]{1,0:T(8,128)(2,1)S(1)} %collective-permute-done.2.t3) | copy-start | bytes 688132
  36.6 33.3 %all-to-all-start.1 = ((bf16[16,4,16,896]{3,2,1,0:T(8,128)(2,1)}), bf16[16,4,16,896]{3,2,1,0:T(8,128)(2,1)S(1)}, u32[]{:S(2)}, u32[]{:S(2)}) async-start(bf16[16,4,16,896]{3,2,1,0:T(8,128)(2,1)} %spread.2), calls=%async_computation.1 | async-start | bytes 3670016 | tf_op jit(solution)/shard_map/all_to_all | solution.py:505
  69.9 1.2 copy-start.3
  69.9 5.7 %collective-permute-start.3 = (bf16[16,4,16,896]{3,2,1,0:T(8,128)(2,1)S(1)}, bf16[16,4,16,896]{3,2,1,0:T(8,128)(2,1)}, u32[]{:S(2)}, u32[]{:S(2)}) collective-permute-start(bf16[16,4,16,896]{3,2,1,0:T(8,128)(2,1)S(1)} %all-to-all-done.1.own_ref), channel_id=1, source_target_pairs={{0,1},{1,0},{2,3},{3,2},{4,5},{5,4},{6,7},{7,6},{8,9},{9,8},{10,11... | collective-permute-start | bytes 5505032 | tf_op jit(solution)/shard_map/ppermute | solution.py:502
  71.2 31.8 %all-to-all-start.2 = ((bf16[16,4,16,896]{3,2,1,0:T(8,128)(2,1)}), bf16[16,4,16,896]{3,2,1,0:T(8,128)(2,1)}, u32[]{:S(2)}, u32[]{:S(2)}) async-start(bf16[16,4,16,896]{3,2,1,0:T(8,128)(2,1)} %spread.3), calls=%async_computation.2 | async-start | bytes 3670016 | tf_op jit(solution)/shard_map/all_to_all | solution.py:505
  84.3 9.6 %collective-permute-start.4 = (bf16[256,896]{1,0:T(8,128)(2,1)}, bf16[256,896]{1,0:T(8,128)(2,1)S(1)}, u32[]{:S(2)}, u32[]{:S(2)}) collective-permute-start(bf16[256,896]{1,0:T(8,128)(2,1)} %get-tuple-element.53), channel_id=1, source_target_pairs={{0,1},{1,0},{2,3},{3,2},{4,5},{5,4},{6,7},{7,6},{8,9},{9,8},{10,11... | collective-permute-start | bytes 1376264 | tf_op jit(solution)/shard_map/ppermute | solution.py:502
  84.4 9.6 %collective-permute-start.5 = (bf16[256,896]{1,0:T(8,128)(2,1)}, bf16[256,896]{1,0:T(8,128)(2,1)S(1)}, u32[]{:S(2)}, u32[]{:S(2)}) collective-permute-start(bf16[256,896]{1,0:T(8,128)(2,1)} %get-tuple-element.54), channel_id=1, source_target_pairs={{0,1},{1,0},{2,3},{3,2},{4,5},{5,4},{6,7},{7,6},{8,9},{9,8},{10,11... | collective-permute-start | bytes 1376264 | tf_op jit(solution)/shard_map/ppermute | solution.py:502
  84.9 9.1 %collective-permute-start.6 = (bf16[256,896]{1,0:T(8,128)(2,1)}, bf16[256,896]{1,0:T(8,128)(2,1)S(1)}, u32[]{:S(2)}, u32[]{:S(2)}) collective-permute-start(bf16[256,896]{1,0:T(8,128)(2,1)} %get-tuple-element.55), channel_id=1, source_target_pairs={{0,1},{1,0},{2,3},{3,2},{4,5},{5,4},{6,7},{7,6},{8,9},{9,8},{10,11... | collective-permute-start | bytes 1376264 | tf_op jit(solution)/shard_map/ppermute | solution.py:502
  84.9 9.0 %collective-permute-start.7 = (bf16[256,896]{1,0:T(8,128)(2,1)}, bf16[256,896]{1,0:T(8,128)(2,1)S(1)}, u32[]{:S(2)}, u32[]{:S(2)}) collective-permute-start(bf16[256,896]{1,0:T(8,128)(2,1)} %get-tuple-element.56), channel_id=1, source_target_pairs={{0,1},{1,0},{2,3},{3,2},{4,5},{5,4},{6,7},{7,6},{8,9},{9,8},{10,11... | collective-permute-start | bytes 1376264 | tf_op jit(solution)/shard_map/ppermute | solution.py:502
  93.9 1.1 copy-start.12
  103.0 17.3 %collective-permute-start.8 = (bf16[16,4,16,896]{3,2,1,0:T(8,128)(2,1)}, bf16[16,4,16,896]{3,2,1,0:T(8,128)(2,1)}, u32[]{:S(2)}, u32[]{:S(2)}) collective-permute-start(bf16[16,4,16,896]{3,2,1,0:T(8,128)(2,1)} %all-to-all-done.2.own_ref), channel_id=1, source_target_pairs={{0,1},{1,0},{2,3},{3,2},{4,5},{5,4},{6,7},{7,6},{8,9},{9,8},{10,11... | collective-permute-start | bytes 5505032 | tf_op jit(solution)/shard_map/ppermute | solution.py:502
  103.0 36.5 %all-to-all-start.3 = ((bf16[16,4,16,896]{3,2,1,0:T(8,128)(2,1)}), bf16[16,4,16,896]{3,2,1,0:T(8,128)(2,1)S(1)}, u32[]{:S(2)}, u32[]{:S(2)}) async-start(bf16[16,4,16,896]{3,2,1,0:T(8,128)(2,1)} %own_pass.2), calls=%async_computation.3 | async-start | bytes 3670016 | tf_op jit(solution)/shard_map/all_to_all | solution.py:505
  108.7 72.4 %reduce-scatter.2.cloned.1.call-start = ((), (), s32[]{:S(2)}) async-start(), calls=%async_computation.7 | async-start | bytes 8257536 | tf_op jit(solution)/shard_map/reduce_scatter | solution.py:543
  128.9 2.1 collective-permute-start.9
  129.2 2.5 %collective-permute-start.10 = (bf16[256,896]{1,0:T(8,128)(2,1)}, bf16[256,896]{1,0:T(8,128)(2,1)S(1)}, u32[]{:S(2)}, u32[]{:S(2)}) collective-permute-start(bf16[256,896]{1,0:T(8,128)(2,1)} %get-tuple-element.69), channel_id=1, source_target_pairs={{0,1},{1,0},{2,3},{3,2},{4,5},{5,4},{6,7},{7,6},{8,9},{9,8},{10,11... | collective-permute-start | bytes 1376264 | tf_op jit(solution)/shard_map/ppermute | solution.py:502
  129.5 3.5 %collective-permute-start.11 = (bf16[256,896]{1,0:T(8,128)(2,1)}, bf16[256,896]{1,0:T(8,128)(2,1)S(1)}, u32[]{:S(2)}, u32[]{:S(2)}) collective-permute-start(bf16[256,896]{1,0:T(8,128)(2,1)} %get-tuple-element.70), channel_id=1, source_target_pairs={{0,1},{1,0},{2,3},{3,2},{4,5},{5,4},{6,7},{7,6},{8,9},{9,8},{10,11... | collective-permute-start | bytes 1376264 | tf_op jit(solution)/shard_map/ppermute | solution.py:502
  129.7 3.5 %collective-permute-start.12 = (bf16[256,896]{1,0:T(8,128)(2,1)}, bf16[256,896]{1,0:T(8,128)(2,1)}, u32[]{:S(2)}, u32[]{:S(2)}) collective-permute-start(bf16[256,896]{1,0:T(8,128)(2,1)} %get-tuple-element.71), channel_id=1, source_target_pairs={{0,1},{1,0},{2,3},{3,2},{4,5},{5,4},{6,7},{7,6},{8,9},{9,8},{10,11... | collective-permute-start | bytes 1376264 | tf_op jit(solution)/shard_map/ppermute | solution.py:502
  131.0 2.1 copy-start.9
  131.7 1.4 copy-start.11
  139.5 1.5 copy-start.2
  181.1 23.6 %all-to-all-start.5 = ((bf16[16,32,896]{2,1,0:T(8,128)(2,1)}), bf16[16,32,896]{2,1,0:T(8,128)(2,1)S(1)}, u32[]{:S(2)}, u32[]{:S(2)}) async-start(bf16[16,32,896]{2,1,0:T(8,128)(2,1)} %bitcast.25), calls=%async_computation.6 | async-start | bytes 1835008 | tf_op jit(solution)/shard_map/all_to_all | solution.py:505
  187.9 1.5 copy-start
  190.1 11.1 %collective-permute-start.13 = (bf16[128,896]{1,0:T(8,128)(2,1)S(1)}, bf16[128,896]{1,0:T(8,128)(2,1)S(1)}, u32[]{:S(2)}, u32[]{:S(2)}) collective-permute-start(bf16[128,896]{1,0:T(8,128)(2,1)S(1)} %get-tuple-element.82), channel_id=1, source_target_pairs={{0,6},{1,7},{2,0},{3,1},{4,2},{5,3},{6,4},{7,5},{8,14},{9,15},{10,... | collective-permute-start | bytes 688136 | tf_op jit(solution)/shard_map/ppermute | solution.py:499
  191.0 13.6 %collective-permute-start.14 = (bf16[128,896]{1,0:T(8,128)(2,1)S(1)}, bf16[128,896]{1,0:T(8,128)(2,1)S(1)}, u32[]{:S(2)}, u32[]{:S(2)}) collective-permute-start(bf16[128,896]{1,0:T(8,128)(2,1)S(1)} %get-tuple-element.83), channel_id=1, source_target_pairs={{0,2},{1,3},{2,4},{3,5},{4,6},{5,7},{6,0},{7,1},{8,10},{9,11},{10,... | collective-permute-start | bytes 688136 | tf_op jit(solution)/shard_map/ppermute | solution.py:499
  192.2 12.4 %collective-permute-start.15 = (bf16[128,896]{1,0:T(8,128)(2,1)S(1)}, bf16[128,896]{1,0:T(8,128)(2,1)S(1)}, u32[]{:S(2)}, u32[]{:S(2)}) collective-permute-start(bf16[128,896]{1,0:T(8,128)(2,1)S(1)} %get-tuple-element.84), channel_id=1, source_target_pairs={{0,4},{1,5},{2,6},{3,7},{4,0},{5,1},{6,2},{7,3},{8,12},{9,13},{10,... | collective-permute-start | bytes 688136 | tf_op jit(solution)/shard_map/ppermute | solution.py:499
  (6 other events, 4.7 us)
Sparse Core Ops, SparseCore 0:
  36.7 46.3 all-gather.2
  130.2 50.8 reduce-scatter.1

commit v5 on v4

--- a/solution.py
+++ b/solution.py
@@ -26,7 +26,7 @@
 
 
 COST = pl.CostEstimate(flops=1000, bytes_accessed=1000, transcendentals=0)
-SLOW = pl.CostEstimate(flops=150_000_000_000, bytes_accessed=1000, transcendentals=0)
+SLOW = pl.CostEstimate(flops=127_000_000_000, bytes_accessed=1000, transcendentals=0)
 
 
 def after(value, *earlier):
@@ -546,8 +546,7 @@
     own[1] = after(own[1], last_part)
     grads, others = first(1)
     ready = own_pass(grads, w_gate, w_up, others, group_count)
-    ready, first_home, table = lax.optimization_barrier((ready, first_home, table))
-    last_table, *tables = cut(table)
+    last_table, *tables = cut(after(table, ready, first_home))
     second_home = exchange(after(ready, first_home, last_table))
     returned = [first_home, second_home]
 

time: 213 us -> 206 us (0.967)
  waiting for transfers between devices: 53.9 us -> 46 us
    reduce_scatter x1, waiting for transfers between devices: 7.11 us -> 0.01 us  [on_device(): lax.psum_scatter(last_part, 'local', scatter_dimension=0, tiled=False)]
    ppermute x6, starting transfers between devices: 8.75 us -> 12.7 us  [shift(): return lax.ppermute(value, 'local', pairs)]
    all_to_all x5, starting transfers between devices: 31.2 us -> 28 us  [exchange(): lax.all_to_all(value, 'group', split_axis=0, concat_axis=0, tiled=True)]
    unnamed x30 -> x32, local copies, waits for them, and re-layouts: 7.4 us -> 7.6 us
  transfers between devices with their start and end apart: 23 -> 23, of which waited for: 11 -> 10; matrix products, arithmetic and copies ran while one was open for 1% -> 1% of each run, Pallas kernels for 26% -> 27%
where the time goes in v5:
time: 206 us
  Pallas kernels  59.5 us (29%)
  waiting for transfers between devices  46 us (22%)
  starting transfers between devices  43.2 us (21%)
  blocking collectives  33 us (16%)
  between operations  13.7 us (7%)
  local copies, waits for them, and re-layouts  10.4 us (5%)
    all_to_all x1, blocking collectives, exchange(): lax.all_to_all(value, 'group', split_axis=0, concat_axis=0, tiled=True)  33 us
    all_to_all x5, starting transfers between devices, exchange(): lax.all_to_all(value, 'group', split_axis=0, concat_axis=0, tiled=True)  28 us
    all_to_all x5, waiting for transfers between devices, exchange(): lax.all_to_all(value, 'group', split_axis=0, concat_axis=0, tiled=True)  23.6 us
    ppermute x6, waiting for transfers between devices, shift(): return lax.ppermute(value, 'local', pairs)  18.7 us
    pallas_call x2, Pallas kernels, first_pass(): pl.pallas_call(functools.partial(first_kernel, start), out_shape=(jax.Sha...  17.4 us
    ppermute x6, starting transfers between devices, shift(): return lax.ppermute(value, 'local', pairs)  12.7 us
    pallas_call x2, Pallas kernels, own_pass(): pl.pallas_call(own_kernel, out_shape=jax.ShapeDtypeStruct((group_count, c...  11.3 us
    pallas_call x1, Pallas kernels, back_last(): pl.pallas_call(back_last_kernel, out_shape=jax.ShapeDtypeStruct((blocks,...  11.3 us
  transfers between devices with their start and end apart: 23, of which 10 were waited for; matrix products, arithmetic and copies ran while one was open for 1% of the time, Pallas kernels for 27%

profile of v5, /device:TPU:0, one launch (start us, length us, event | category | flops | bytes accessed | tf_op | source)
XLA Modules:
  0.0 205.7 jit_solution(3259900169398718432)
XLA Ops:
  6.5 2.7 %route.1 = (bf16[16,64,128]{2,1,0:T(8,128)(2,1)}, bf16[16,40,896]{2,1,0:T(8,128)(2,1)}) custom-call(s32[4,128]{1,0:T(4,128)} %bitcast.28, s32[8,128]{1,0:T(8,128)} %bitcast.26, f32[8,128]{1,0:T(8,128)} %bitcast.27, bf16[128,896]{1,0:T(8,128)(2,1)} %t0.3), custom_call_target="tpu_custom_call" | custom-call | flops 1000 | bytes 1000 | tf_op jit(solution)/shard_map/route/pallas_call | solution.py:86
  9.3 7.2 %all-to-all-start = ((bf16[16,40,896]{2,1,0:T(8,128)(2,1)}), bf16[16,40,896]{2,1,0:T(8,128)(2,1)S(1)}, u32[]{:S(2)}, u32[]{:S(2)}) async-start(bf16[16,40,896]{2,1,0:T(8,128)(2,1)} %get-tuple-element.44), calls=%async_computation | async-start | bytes 2293760 | tf_op jit(solution)/shard_map/all_to_all | solution.py:505
  16.6 4.0 %collective-permute-start.2 = (bf16[128,896]{1,0:T(8,128)(2,1)S(1)}, bf16[128,896]{1,0:T(8,128)(2,1)S(1)}, u32[]{:S(2)}, u32[]{:S(2)}) collective-permute-start(bf16[128,896]{1,0:T(8,128)(2,1)S(1)} %copy-done.4), channel_id=1, source_target_pairs={{0,4},{1,5},{2,6},{3,7},{4,0},{5,1},{6,2},{7,3},{8,12},{9,13},{10,... | collective-permute-start | bytes 688136 | tf_op jit(solution)/shard_map/ppermute | solution.py:499
  21.3 1.3 collective-permute-start
  23.2 3.8 %collective-permute-done.2.t3 = bf16[128,896]{1,0:T(8,128)(2,1)S(1)} collective-permute-done((bf16[128,896]{1,0:T(8,128)(2,1)S(1)}, bf16[128,896]{1,0:T(8,128)(2,1)S(1)}, u32[]{:S(2)}, u32[]{:S(2)}) %collective-permute-start.2) | collective-permute-done | bytes 229408 | tf_op jit(solution)/shard_map/ppermute | solution.py:499
  27.0 4.5 %collective-permute-done.1.t2 = bf16[128,896]{1,0:T(8,128)(2,1)S(1)} collective-permute-done((bf16[128,896]{1,0:T(8,128)(2,1)S(1)}, bf16[128,896]{1,0:T(8,128)(2,1)S(1)}, u32[]{:S(2)}, u32[]{:S(2)}) %collective-permute-start.1) | collective-permute-done | bytes 229408 | tf_op jit(solution)/shard_map/ppermute | solution.py:499
  32.3 3.2 %spread.2 = bf16[16,4,16,896]{3,2,1,0:T(8,128)(2,1)} custom-call(bf16[16,16,128]{2,1,0:T(8,128)(2,1)} %get-tuple-element.82.table_ref, bf16[128,896]{1,0:T(8,128)(2,1)} %t0.3, bf16[128,896]{1,0:T(8,128)(2,1)} %copy-done.7, bf16[128,896]{1,0:T(8,128)(2,1)} %copy-done.6, bf16[128,896]{1,0:T(8,128)(2,1)} %copy-done.5), custom_call_target="tpu_custom_call" | custom-call | flops 1000 | bytes 1000 | tf_op jit(solution)/shard_map/spread/pallas_call | solution.py:109
  35.6 1.0 slice.16
  36.6 6.9 %all-to-all-start.1 = ((bf16[16,4,16,896]{3,2,1,0:T(8,128)(2,1)}), bf16[16,4,16,896]{3,2,1,0:T(8,128)(2,1)S(1)}, u32[]{:S(2)}, u32[]{:S(2)}) async-start(bf16[16,4,16,896]{3,2,1,0:T(8,128)(2,1)} %spread.2), calls=%async_computation.1 | async-start | bytes 3670016 | tf_op jit(solution)/shard_map/all_to_all | solution.py:505
  43.6 3.2 %spread.3 = bf16[16,4,16,896]{3,2,1,0:T(8,128)(2,1)} custom-call(bf16[16,16,128]{2,1,0:T(8,128)(2,1)} %get-tuple-element.81.table_ref, bf16[128,896]{1,0:T(8,128)(2,1)} %t0.3, bf16[128,896]{1,0:T(8,128)(2,1)} %copy-done.7, bf16[128,896]{1,0:T(8,128)(2,1)} %copy-done.6, bf16[128,896]{1,0:T(8,128)(2,1)} %copy-done.5), custom_call_target="tpu_custom_call" | custom-call | flops 1000 | bytes 1000 | tf_op jit(solution)/shard_map/spread/pallas_call | solution.py:109
  46.8 1.1 copy.15
  47.9 22.1 %all-to-all-done.1.own_ref = bf16[16,4,16,896]{3,2,1,0:T(8,128)(2,1)S(1)} async-done(((bf16[16,4,16,896]{3,2,1,0:T(8,128)(2,1)}), bf16[16,4,16,896]{3,2,1,0:T(8,128)(2,1)S(1)}, u32[]{:S(2)}, u32[]{:S(2)}) %all-to-all-start.1) | async-done | bytes 1835040 | tf_op jit(solution)/shard_map/all_to_all | solution.py:505
  69.9 1.2 copy-done.3
  71.2 4.4 %all-to-all-start.2 = ((bf16[16,4,16,896]{3,2,1,0:T(8,128)(2,1)}), bf16[16,4,16,896]{3,2,1,0:T(8,128)(2,1)}, u32[]{:S(2)}, u32[]{:S(2)}) async-start(bf16[16,4,16,896]{3,2,1,0:T(8,128)(2,1)} %spread.3), calls=%async_computation.2 | async-start | bytes 3670016 | tf_op jit(solution)/shard_map/all_to_all | solution.py:505
  75.6 8.7 %first_pass.2 = (bf16[256,768]{1,0:T(8,128)(2,1)}, bf16[256,896]{1,0:T(8,128)(2,1)}, bf16[256,896]{1,0:T(8,128)(2,1)}, bf16[256,896]{1,0:T(8,128)(2,1)}, bf16[256,896]{1,0:T(8,128)(2,1)}) custom-call(bf16[16,4,16,896]{3,2,1,0:T(8,128)(2,1)} %copy-done.3, bf16[16,4,16,896]{3,2,1,0:T(8,128)(2,1)} %collective-permute-done.3.other_ref, ...), custom_call_target="tpu_custom_call" | custom-call | flops 1000 | bytes 1000 | tf_op jit(solution)/shard_map/first_pass/pallas_call | solution.py:334
  85.4 8.5 %hidden_last.1.grads_ref = bf16[512,768]{1,0:T(8,128)(2,1)} custom-call(bf16[8,512,896]{2,1,0:T(8,128)(2,1)} %bitcast.17, bf16[384,7168]{1,0:T(8,128)(2,1)} %bitcast.12, f32[16,64,3]{2,1,0:T(8,128)} %bitcast.15, bf16[3,16,64,128]{3,2,1,0:T(8,128)(2,1)} %bitcast.19, bf16[3,16,64,128]{3,2,1,0:T(8,128)(2,1)} %bitcast.22), custom_call_target="tpu_custom_call" | custom-call | flops 1000 | bytes 1000 | tf_op jit(solution)/shard_map/hidden_last/pallas_call | solution.py:218
  95.8 5.6 %own_pass.2 = bf16[16,4,16,896]{3,2,1,0:T(8,128)(2,1)} custom-call(bf16[256,768]{1,0:T(8,128)(2,1)} %get-tuple-element.55.grads_ref, bf16[3,7168,128]{2,1,0:T(8,128)(2,1)} %w_gate_ref.9, bf16[3,7168,128]{2,1,0:T(8,128)(2,1)} %w_up_ref.9, bf16[256,896]{1,0:T(8,128)(2,1)} %copy-done.8, bf16[256,896]{1,0:T(8,128)(2,1)} %copy-done.9, ...), custom_call_target="tpu_custom_call" | custom-call | flops 1000 | bytes 1000 | tf_op jit(solution)/shard_map/own_pass/pallas_call | solution.py:395
  101.4 1.6 all-to-all-done.2.own_ref
  103.0 5.7 %all-to-all-start.3 = ((bf16[16,4,16,896]{3,2,1,0:T(8,128)(2,1)}), bf16[16,4,16,896]{3,2,1,0:T(8,128)(2,1)S(1)}, u32[]{:S(2)}, u32[]{:S(2)}) async-start(bf16[16,4,16,896]{3,2,1,0:T(8,128)(2,1)} %own_pass.2), calls=%async_computation.3 | async-start | bytes 3670016 | tf_op jit(solution)/shard_map/all_to_all | solution.py:505
  109.0 11.3 %back_last.1 = bf16[8,512,896]{2,1,0:T(8,128)(2,1)} custom-call(bf16[512,768]{1,0:T(8,128)(2,1)} %hidden_last.1.grads_ref, bf16[3,7168,128]{2,1,0:T(8,128)(2,1)} %w_gate_ref.9, bf16[3,7168,128]{2,1,0:T(8,128)(2,1)} %w_up_ref.9), custom_call_target="tpu_custom_call" | custom-call | flops 1000 | bytes 1000 | tf_op jit(solution)/shard_map/back_last/pallas_call | solution.py:268
  120.3 8.7 %first_pass.3 = (bf16[256,768]{1,0:T(8,128)(2,1)}, bf16[256,896]{1,0:T(8,128)(2,1)}, bf16[256,896]{1,0:T(8,128)(2,1)}, bf16[256,896]{1,0:T(8,128)(2,1)}, bf16[256,896]{1,0:T(8,128)(2,1)}) custom-call(bf16[16,4,16,896]{3,2,1,0:T(8,128)(2,1)} %all-to-all-done.2.own_ref, bf16[16,4,16,896]{3,2,1,0:T(8,128)(2,1)} %collective-permute-done.8.other_ref, ...), custom_call_target="tpu_custom_call" | custom-call | flops 1000 | bytes 1000 | tf_op jit(solution)/shard_map/first_pass/pallas_call | solution.py:334
  132.4 1.3 collective-permute-done.12.refs_3_
  134.6 5.7 %own_pass.3 = bf16[16,4,16,896]{3,2,1,0:T(8,128)(2,1)} custom-call(bf16[256,768]{1,0:T(8,128)(2,1)} %get-tuple-element.65.grads_ref, bf16[3,7168,128]{2,1,0:T(8,128)(2,1)} %w_gate_ref.9, bf16[3,7168,128]{2,1,0:T(8,128)(2,1)} %w_up_ref.9, bf16[256,896]{1,0:T(8,128)(2,1)} %copy-done.11, bf16[256,896]{1,0:T(8,128)(2,1)} %copy-done.13, ...), custom_call_target="tpu_custom_call" | custom-call | flops 1000 | bytes 1000 | tf_op jit(solution)/shard_map/own_pass/pallas_call | solution.py:395
  140.3 1.5 copy-done.2
  141.8 33.0 %all_to_all.30.refs_3_ = bf16[16,4,16,896]{3,2,1,0:T(8,128)(2,1)} all-to-all(bf16[16,4,16,896]{3,2,1,0:T(8,128)(2,1)S(1)} %copy-done.2), channel_id=1, replica_groups=mesh['group'=16,'local'=8] {'group'}, dimensions={0} | all-to-all | bytes 3670016 | tf_op jit(solution)/shard_map/all_to_all | solution.py:505
  174.8 3.6 %all-to-all-start.5 = ((bf16[16,32,896]{2,1,0:T(8,128)(2,1)}), bf16[16,32,896]{2,1,0:T(8,128)(2,1)S(1)}, u32[]{:S(2)}, u32[]{:S(2)}) async-start(bf16[16,32,896]{2,1,0:T(8,128)(2,1)} %bitcast.25), calls=%async_computation.6 | async-start | bytes 1835008 | tf_op jit(solution)/shard_map/all_to_all | solution.py:505
  178.4 1.5 copy-done
  180.7 4.8 %collective-permute-start.13 = (bf16[128,896]{1,0:T(8,128)(2,1)S(1)}, bf16[128,896]{1,0:T(8,128)(2,1)S(1)}, u32[]{:S(2)}, u32[]{:S(2)}) collective-permute-start(bf16[128,896]{1,0:T(8,128)(2,1)S(1)} %get-tuple-element.78), channel_id=1, source_target_pairs={{0,6},{1,7},{2,0},{3,1},{4,2},{5,3},{6,4},{7,5},{8,14},{9,15},{10,... | collective-permute-start | bytes 688136 | tf_op jit(solution)/shard_map/ppermute | solution.py:499
  185.5 1.9 collective-permute-start.15
  187.4 7.0 %collective-permute-done.13.a_ref = bf16[128,896]{1,0:T(8,128)(2,1)S(1)} collective-permute-done((bf16[128,896]{1,0:T(8,128)(2,1)S(1)}, bf16[128,896]{1,0:T(8,128)(2,1)S(1)}, u32[]{:S(2)}, u32[]{:S(2)}) %collective-permute-start.13) | collective-permute-done | bytes 229408 | tf_op jit(solution)/shard_map/ppermute | solution.py:499
  194.4 3.4 %collective-permute-done.14.b_ref = bf16[128,896]{1,0:T(8,128)(2,1)S(1)} collective-permute-done((bf16[128,896]{1,0:T(8,128)(2,1)S(1)}, bf16[128,896]{1,0:T(8,128)(2,1)S(1)}, u32[]{:S(2)}, u32[]{:S(2)}) %collective-permute-start.14) | collective-permute-done | bytes 229408 | tf_op jit(solution)/shard_map/ppermute | solution.py:499
  197.8 1.0 finish.1
  (66 shorter events, 10.4 us)
Async XLA Ops:
  6.5 10.1 %copy-start.4 = (bf16[128,896]{1,0:T(8,128)(2,1)S(1)}, bf16[128,896]{1,0:T(8,128)(2,1)}, u32[]{:S(2)}) copy-start(bf16[128,896]{1,0:T(8,128)(2,1)} %t0.3) | copy-start | bytes 688132
  9.3 13.3 %copy-start.1 = (bf16[16,64,128]{2,1,0:T(8,128)(2,1)S(1)}, bf16[16,64,128]{2,1,0:T(8,128)(2,1)}, u32[]{:S(2)}) copy-start(bf16[16,64,128]{2,1,0:T(8,128)(2,1)} %get-tuple-element.71.table_ref) | copy-start | bytes 786436
  9.3 26.3 %all-to-all-start = ((bf16[16,40,896]{2,1,0:T(8,128)(2,1)}), bf16[16,40,896]{2,1,0:T(8,128)(2,1)S(1)}, u32[]{:S(2)}, u32[]{:S(2)}) async-start(bf16[16,40,896]{2,1,0:T(8,128)(2,1)} %get-tuple-element.44), calls=%async_computation | async-start | bytes 2293760 | tf_op jit(solution)/shard_map/all_to_all | solution.py:505
  16.5 68.9 %all-gather.3.cloned.1.call-start = ((), (), s32[]{:S(2)}) async-start(), calls=%async_computation.8 | async-start | bytes 8257536 | tf_op jit(solution)/shard_map/all_gather | solution.py:520
  16.6 10.4 %collective-permute-start.2 = (bf16[128,896]{1,0:T(8,128)(2,1)S(1)}, bf16[128,896]{1,0:T(8,128)(2,1)S(1)}, u32[]{:S(2)}, u32[]{:S(2)}) collective-permute-start(bf16[128,896]{1,0:T(8,128)(2,1)S(1)} %copy-done.4), channel_id=1, source_target_pairs={{0,4},{1,5},{2,6},{3,7},{4,0},{5,1},{6,2},{7,3},{8,12},{9,13},{10,... | collective-permute-start | bytes 688136 | tf_op jit(solution)/shard_map/ppermute | solution.py:499
  20.6 11.0 %collective-permute-start.1 = (bf16[128,896]{1,0:T(8,128)(2,1)S(1)}, bf16[128,896]{1,0:T(8,128)(2,1)S(1)}, u32[]{:S(2)}, u32[]{:S(2)}) collective-permute-start(bf16[128,896]{1,0:T(8,128)(2,1)S(1)} %copy-done.4), channel_id=1, source_target_pairs={{0,6},{1,7},{2,0},{3,1},{4,2},{5,3},{6,4},{7,5},{8,14},{9,15},{10,... | collective-permute-start | bytes 688136 | tf_op jit(solution)/shard_map/ppermute | solution.py:499
  21.3 10.3 %collective-permute-start = (bf16[128,896]{1,0:T(8,128)(2,1)S(1)}, bf16[128,896]{1,0:T(8,128)(2,1)S(1)}, u32[]{:S(2)}, u32[]{:S(2)}) collective-permute-start(bf16[128,896]{1,0:T(8,128)(2,1)S(1)} %copy-done.4), channel_id=1, source_target_pairs={{0,2},{1,3},{2,4},{3,5},{4,6},{5,7},{6,0},{7,1},{8,10},{9,11},{10,... | collective-permute-start | bytes 688136 | tf_op jit(solution)/shard_map/ppermute | solution.py:499
  27.0 4.5 %copy-start.5 = (bf16[128,896]{1,0:T(8,128)(2,1)}, bf16[128,896]{1,0:T(8,128)(2,1)S(1)}, u32[]{:S(2)}) copy-start(bf16[128,896]{1,0:T(8,128)(2,1)S(1)} %collective-permute-done.2.t3) | copy-start | bytes 688132
  36.6 33.3 %all-to-all-start.1 = ((bf16[16,4,16,896]{3,2,1,0:T(8,128)(2,1)}), bf16[16,4,16,896]{3,2,1,0:T(8,128)(2,1)S(1)}, u32[]{:S(2)}, u32[]{:S(2)}) async-start(bf16[16,4,16,896]{3,2,1,0:T(8,128)(2,1)} %spread.2), calls=%async_computation.1 | async-start | bytes 3670016 | tf_op jit(solution)/shard_map/all_to_all | solution.py:505
  69.9 1.2 copy-start.3
  69.9 5.7 %collective-permute-start.3 = (bf16[16,4,16,896]{3,2,1,0:T(8,128)(2,1)S(1)}, bf16[16,4,16,896]{3,2,1,0:T(8,128)(2,1)}, u32[]{:S(2)}, u32[]{:S(2)}) collective-permute-start(bf16[16,4,16,896]{3,2,1,0:T(8,128)(2,1)S(1)} %all-to-all-done.1.own_ref), channel_id=1, source_target_pairs={{0,1},{1,0},{2,3},{3,2},{4,5},{5,4},{6,7},{7,6},{8,9},{9,8},{10,11... | collective-permute-start | bytes 5505032 | tf_op jit(solution)/shard_map/ppermute | solution.py:502
  71.2 31.8 %all-to-all-start.2 = ((bf16[16,4,16,896]{3,2,1,0:T(8,128)(2,1)}), bf16[16,4,16,896]{3,2,1,0:T(8,128)(2,1)}, u32[]{:S(2)}, u32[]{:S(2)}) async-start(bf16[16,4,16,896]{3,2,1,0:T(8,128)(2,1)} %spread.3), calls=%async_computation.2 | async-start | bytes 3670016 | tf_op jit(solution)/shard_map/all_to_all | solution.py:505
  84.3 9.6 %collective-permute-start.4 = (bf16[256,896]{1,0:T(8,128)(2,1)}, bf16[256,896]{1,0:T(8,128)(2,1)S(1)}, u32[]{:S(2)}, u32[]{:S(2)}) collective-permute-start(bf16[256,896]{1,0:T(8,128)(2,1)} %get-tuple-element.51), channel_id=1, source_target_pairs={{0,1},{1,0},{2,3},{3,2},{4,5},{5,4},{6,7},{7,6},{8,9},{9,8},{10,11... | collective-permute-start | bytes 1376264 | tf_op jit(solution)/shard_map/ppermute | solution.py:502
  84.4 9.6 %collective-permute-start.5 = (bf16[256,896]{1,0:T(8,128)(2,1)}, bf16[256,896]{1,0:T(8,128)(2,1)S(1)}, u32[]{:S(2)}, u32[]{:S(2)}) collective-permute-start(bf16[256,896]{1,0:T(8,128)(2,1)} %get-tuple-element.52), channel_id=1, source_target_pairs={{0,1},{1,0},{2,3},{3,2},{4,5},{5,4},{6,7},{7,6},{8,9},{9,8},{10,11... | collective-permute-start | bytes 1376264 | tf_op jit(solution)/shard_map/ppermute | solution.py:502
  84.9 9.1 %collective-permute-start.6 = (bf16[256,896]{1,0:T(8,128)(2,1)}, bf16[256,896]{1,0:T(8,128)(2,1)S(1)}, u32[]{:S(2)}, u32[]{:S(2)}) collective-permute-start(bf16[256,896]{1,0:T(8,128)(2,1)} %get-tuple-element.53), channel_id=1, source_target_pairs={{0,1},{1,0},{2,3},{3,2},{4,5},{5,4},{6,7},{7,6},{8,9},{9,8},{10,11... | collective-permute-start | bytes 1376264 | tf_op jit(solution)/shard_map/ppermute | solution.py:502
  85.0 9.0 %collective-permute-start.7 = (bf16[256,896]{1,0:T(8,128)(2,1)}, bf16[256,896]{1,0:T(8,128)(2,1)S(1)}, u32[]{:S(2)}, u32[]{:S(2)}) collective-permute-start(bf16[256,896]{1,0:T(8,128)(2,1)} %get-tuple-element.54), channel_id=1, source_target_pairs={{0,1},{1,0},{2,3},{3,2},{4,5},{5,4},{6,7},{7,6},{8,9},{9,8},{10,11... | collective-permute-start | bytes 1376264 | tf_op jit(solution)/shard_map/ppermute | solution.py:502
  103.0 17.3 %collective-permute-start.8 = (bf16[16,4,16,896]{3,2,1,0:T(8,128)(2,1)}, bf16[16,4,16,896]{3,2,1,0:T(8,128)(2,1)}, u32[]{:S(2)}, u32[]{:S(2)}) collective-permute-start(bf16[16,4,16,896]{3,2,1,0:T(8,128)(2,1)} %all-to-all-done.2.own_ref), channel_id=1, source_target_pairs={{0,1},{1,0},{2,3},{3,2},{4,5},{5,4},{6,7},{7,6},{8,9},{9,8},{10,11... | collective-permute-start | bytes 5505032 | tf_op jit(solution)/shard_map/ppermute | solution.py:502
  103.0 37.2 %all-to-all-start.3 = ((bf16[16,4,16,896]{3,2,1,0:T(8,128)(2,1)}), bf16[16,4,16,896]{3,2,1,0:T(8,128)(2,1)S(1)}, u32[]{:S(2)}, u32[]{:S(2)}) async-start(bf16[16,4,16,896]{3,2,1,0:T(8,128)(2,1)} %own_pass.2), calls=%async_computation.3 | async-start | bytes 3670016 | tf_op jit(solution)/shard_map/all_to_all | solution.py:505
  108.7 66.0 %reduce-scatter.2.cloned.1.call-start = ((), (), s32[]{:S(2)}) async-start(), calls=%async_computation.7 | async-start | bytes 8257536 | tf_op jit(solution)/shard_map/reduce_scatter | solution.py:543
  129.0 2.1 %collective-permute-start.9 = (bf16[256,896]{1,0:T(8,128)(2,1)}, bf16[256,896]{1,0:T(8,128)(2,1)S(1)}, u32[]{:S(2)}, u32[]{:S(2)}) collective-permute-start(bf16[256,896]{1,0:T(8,128)(2,1)} %get-tuple-element.66), channel_id=1, source_target_pairs={{0,1},{1,0},{2,3},{3,2},{4,5},{5,4},{6,7},{7,6},{8,9},{9,8},{10,11... | collective-permute-start | bytes 1376264 | tf_op jit(solution)/shard_map/ppermute | solution.py:502
  129.3 2.5 %collective-permute-start.10 = (bf16[256,896]{1,0:T(8,128)(2,1)}, bf16[256,896]{1,0:T(8,128)(2,1)S(1)}, u32[]{:S(2)}, u32[]{:S(2)}) collective-permute-start(bf16[256,896]{1,0:T(8,128)(2,1)} %get-tuple-element.67), channel_id=1, source_target_pairs={{0,1},{1,0},{2,3},{3,2},{4,5},{5,4},{6,7},{7,6},{8,9},{9,8},{10,11... | collective-permute-start | bytes 1376264 | tf_op jit(solution)/shard_map/ppermute | solution.py:502
  129.6 2.8 %collective-permute-start.11 = (bf16[256,896]{1,0:T(8,128)(2,1)}, bf16[256,896]{1,0:T(8,128)(2,1)S(1)}, u32[]{:S(2)}, u32[]{:S(2)}) collective-permute-start(bf16[256,896]{1,0:T(8,128)(2,1)} %get-tuple-element.68), channel_id=1, source_target_pairs={{0,1},{1,0},{2,3},{3,2},{4,5},{5,4},{6,7},{7,6},{8,9},{9,8},{10,11... | collective-permute-start | bytes 1376264 | tf_op jit(solution)/shard_map/ppermute | solution.py:502
  129.8 4.0 %collective-permute-start.12 = (bf16[256,896]{1,0:T(8,128)(2,1)}, bf16[256,896]{1,0:T(8,128)(2,1)S(1)}, u32[]{:S(2)}, u32[]{:S(2)}) collective-permute-start(bf16[256,896]{1,0:T(8,128)(2,1)} %get-tuple-element.69), channel_id=1, source_target_pairs={{0,1},{1,0},{2,3},{3,2},{4,5},{5,4},{6,7},{7,6},{8,9},{9,8},{10,11... | collective-permute-start | bytes 1376264 | tf_op jit(solution)/shard_map/ppermute | solution.py:502
  131.1 2.6 %copy-start.11 = (bf16[256,896]{1,0:T(8,128)(2,1)}, bf16[256,896]{1,0:T(8,128)(2,1)S(1)}, u32[]{:S(2)}) copy-start(bf16[256,896]{1,0:T(8,128)(2,1)S(1)} %collective-permute-done.9.refs_0_) | copy-start | bytes 1376260
  131.8 2.0 copy-start.13
  132.4 1.3 copy-start.14
  140.2 1.5 copy-start.2
  174.8 23.0 %all-to-all-start.5 = ((bf16[16,32,896]{2,1,0:T(8,128)(2,1)}), bf16[16,32,896]{2,1,0:T(8,128)(2,1)S(1)}, u32[]{:S(2)}, u32[]{:S(2)}) async-start(bf16[16,32,896]{2,1,0:T(8,128)(2,1)} %bitcast.25), calls=%async_computation.6 | async-start | bytes 1835008 | tf_op jit(solution)/shard_map/all_to_all | solution.py:505
  178.4 1.5 copy-start
  180.7 13.7 %collective-permute-start.13 = (bf16[128,896]{1,0:T(8,128)(2,1)S(1)}, bf16[128,896]{1,0:T(8,128)(2,1)S(1)}, u32[]{:S(2)}, u32[]{:S(2)}) collective-permute-start(bf16[128,896]{1,0:T(8,128)(2,1)S(1)} %get-tuple-element.78), channel_id=1, source_target_pairs={{0,6},{1,7},{2,0},{3,1},{4,2},{5,3},{6,4},{7,5},{8,14},{9,15},{10,... | collective-permute-start | bytes 688136 | tf_op jit(solution)/shard_map/ppermute | solution.py:499
  185.5 12.3 %collective-permute-start.14 = (bf16[128,896]{1,0:T(8,128)(2,1)S(1)}, bf16[128,896]{1,0:T(8,128)(2,1)S(1)}, u32[]{:S(2)}, u32[]{:S(2)}) collective-permute-start(bf16[128,896]{1,0:T(8,128)(2,1)S(1)} %get-tuple-element.79), channel_id=1, source_target_pairs={{0,2},{1,3},{2,4},{3,5},{4,6},{5,7},{6,0},{7,1},{8,10},{9,11},{10,... | collective-permute-start | bytes 688136 | tf_op jit(solution)/shard_map/ppermute | solution.py:499
  185.5 12.3 %collective-permute-start.15 = (bf16[128,896]{1,0:T(8,128)(2,1)S(1)}, bf16[128,896]{1,0:T(8,128)(2,1)S(1)}, u32[]{:S(2)}, u32[]{:S(2)}) collective-permute-start(bf16[128,896]{1,0:T(8,128)(2,1)S(1)} %get-tuple-element.80), channel_id=1, source_target_pairs={{0,4},{1,5},{2,6},{3,7},{4,0},{5,1},{6,2},{7,3},{8,12},{9,13},{10,... | collective-permute-start | bytes 688136 | tf_op jit(solution)/shard_map/ppermute | solution.py:499
  (7 other events, 5.8 us)
Sparse Core Ops, SparseCore 0:
  36.7 46.3 all-gather.2
  120.4 50.8 reduce-scatter.1

commit v6 on v5

--- a/solution.py
+++ b/solution.py
@@ -109,7 +109,7 @@
     return pl.pallas_call(
         spread_kernel,
         out_shape=jax.ShapeDtypeStruct((group_count, len(tokens), slots, width), BF),
-        compiler_params=params(),
+        compiler_params=params(16 * 1024 * 1024),
         cost_estimate=COST,
         name="spread",
     )(table, *tokens)

time: 206 us -> 204 us (level)
  waiting for transfers between devices: 46 us -> 52.2 us
  starting transfers between devices: 43.2 us -> 38.9 us
  Pallas kernels: 59.5 us -> 56.8 us
    all_to_all x5, waiting for transfers between devices: 23.6 us -> 29.1 us  [exchange(): lax.all_to_all(value, 'group', split_axis=0, concat_axis=0, tiled=True)]
    all_to_all x5, starting transfers between devices: 28 us -> 24.1 us  [exchange(): lax.all_to_all(value, 'group', split_axis=0, concat_axis=0, tiled=True)]
    pallas_call x2, Pallas kernels: 6.45 us -> 3.9 us  [spread_tokens(): pl.pallas_call(spread_kernel, out_shape=jax.ShapeDtypeStruct((group_count...]
    unnamed x32 -> x26, local copies, waits for them, and re-layouts: 7.6 us -> 6.86 us
  transfers between devices with their start and end apart: 23 -> 23, of which waited for: 10 -> 11; matrix products, arithmetic and copies ran while one was open for 1% -> 1% of each run, Pallas kernels for 27% -> 26%
where the time goes in v6:
time: 204 us; the launch traced here: 203 us
  Pallas kernels  56.8 us (28%)
  waiting for transfers between devices  52.2 us (26%)
  starting transfers between devices  38.9 us (19%)
  blocking collectives  32.9 us (16%)
  between operations  13.7 us (7%)
  local copies, waits for them, and re-layouts  8.94 us (4%)
    all_to_all x1, blocking collectives, exchange(): lax.all_to_all(value, 'group', split_axis=0, concat_axis=0, tiled=True)  32.9 us
    all_to_all x5, waiting for transfers between devices, exchange(): lax.all_to_all(value, 'group', split_axis=0, concat_axis=0, tiled=True)  29.1 us
    all_to_all x5, starting transfers between devices, exchange(): lax.all_to_all(value, 'group', split_axis=0, concat_axis=0, tiled=True)  24.1 us
    ppermute x6, waiting for transfers between devices, shift(): return lax.ppermute(value, 'local', pairs)  19.4 us
    pallas_call x2, Pallas kernels, first_pass(): pl.pallas_call(functools.partial(first_kernel, start), out_shape=(jax.Sha...  17.4 us
    ppermute x6, starting transfers between devices, shift(): return lax.ppermute(value, 'local', pairs)  11.9 us
    pallas_call x2, Pallas kernels, own_pass(): pl.pallas_call(own_kernel, out_shape=jax.ShapeDtypeStruct((group_count, c...  11.3 us
    pallas_call x1, Pallas kernels, back_last(): pl.pallas_call(back_last_kernel, out_shape=jax.ShapeDtypeStruct((blocks,...  11.3 us
  transfers between devices with their start and end apart: 23, of which 11 were waited for; matrix products, arithmetic and copies ran while one was open for 1% of the time, Pallas kernels for 26%

profile of v6, /device:TPU:0, one launch (start us, length us, event | category | flops | bytes accessed | tf_op | source)
XLA Modules:
  0.0 203.5 jit_solution(12576769333420961965)
XLA Ops:
  6.5 2.7 %route.1 = (bf16[16,64,128]{2,1,0:T(8,128)(2,1)}, bf16[16,40,896]{2,1,0:T(8,128)(2,1)}) custom-call(s32[4,128]{1,0:T(4,128)} %bitcast.28, s32[8,128]{1,0:T(8,128)} %bitcast.26, f32[8,128]{1,0:T(8,128)} %bitcast.27, bf16[128,896]{1,0:T(8,128)(2,1)} %t0.3), custom_call_target="tpu_custom_call" | custom-call | flops 1000 | bytes 1000 | tf_op jit(solution)/shard_map/route/pallas_call | solution.py:86
  9.3 7.2 %all-to-all-start = ((bf16[16,40,896]{2,1,0:T(8,128)(2,1)}), bf16[16,40,896]{2,1,0:T(8,128)(2,1)S(1)}, u32[]{:S(2)}, u32[]{:S(2)}) async-start(bf16[16,40,896]{2,1,0:T(8,128)(2,1)} %get-tuple-element.44), calls=%async_computation | async-start | bytes 2293760 | tf_op jit(solution)/shard_map/all_to_all | solution.py:505
  16.6 4.0 %collective-permute-start.2 = (bf16[128,896]{1,0:T(8,128)(2,1)S(1)}, bf16[128,896]{1,0:T(8,128)(2,1)S(1)}, u32[]{:S(2)}, u32[]{:S(2)}) collective-permute-start(bf16[128,896]{1,0:T(8,128)(2,1)S(1)} %copy-done.1), channel_id=1, source_target_pairs={{0,4},{1,5},{2,6},{3,7},{4,0},{5,1},{6,2},{7,3},{8,12},{9,13},{10,... | collective-permute-start | bytes 688136 | tf_op jit(solution)/shard_map/ppermute | solution.py:499
  21.2 1.3 collective-permute-start
  22.6 4.4 %collective-permute-done.2.t3 = bf16[128,896]{1,0:T(8,128)(2,1)S(1)} collective-permute-done((bf16[128,896]{1,0:T(8,128)(2,1)S(1)}, bf16[128,896]{1,0:T(8,128)(2,1)S(1)}, u32[]{:S(2)}, u32[]{:S(2)}) %collective-permute-start.2) | collective-permute-done | bytes 229408 | tf_op jit(solution)/shard_map/ppermute | solution.py:499
  27.0 4.5 %collective-permute-done.1.t2 = bf16[128,896]{1,0:T(8,128)(2,1)S(1)} collective-permute-done((bf16[128,896]{1,0:T(8,128)(2,1)S(1)}, bf16[128,896]{1,0:T(8,128)(2,1)S(1)}, u32[]{:S(2)}, u32[]{:S(2)}) %collective-permute-start.1) | collective-permute-done | bytes 229408 | tf_op jit(solution)/shard_map/ppermute | solution.py:499
  31.5 1.9 spread.2
  33.5 1.9 all-to-all-done
  36.4 5.1 %all-to-all-start.1 = ((bf16[16,4,16,896]{3,2,1,0:T(8,128)(2,1)}), bf16[16,4,16,896]{3,2,1,0:T(8,128)(2,1)}, u32[]{:S(2)}, u32[]{:S(2)}) async-start(bf16[16,4,16,896]{3,2,1,0:T(8,128)(2,1)} %spread.2), calls=%async_computation.1 | async-start | bytes 3670016 | tf_op jit(solution)/shard_map/all_to_all | solution.py:505
  41.5 2.0 spread.3
  43.5 1.1 copy.15
  44.6 23.4 %all-to-all-done.1.own_ref = bf16[16,4,16,896]{3,2,1,0:T(8,128)(2,1)} async-done(((bf16[16,4,16,896]{3,2,1,0:T(8,128)(2,1)}), bf16[16,4,16,896]{3,2,1,0:T(8,128)(2,1)}, u32[]{:S(2)}, u32[]{:S(2)}) %all-to-all-start.1) | async-done | bytes 1835040 | tf_op jit(solution)/shard_map/all_to_all | solution.py:505
  68.0 4.4 %all-to-all-start.2 = ((bf16[16,4,16,896]{3,2,1,0:T(8,128)(2,1)}), bf16[16,4,16,896]{3,2,1,0:T(8,128)(2,1)}, u32[]{:S(2)}, u32[]{:S(2)}) async-start(bf16[16,4,16,896]{3,2,1,0:T(8,128)(2,1)} %spread.3), calls=%async_computation.2 | async-start | bytes 3670016 | tf_op jit(solution)/shard_map/all_to_all | solution.py:505
  72.4 1.2 copy-done.4
  73.6 8.7 %first_pass.2 = (bf16[256,768]{1,0:T(8,128)(2,1)}, bf16[256,896]{1,0:T(8,128)(2,1)}, bf16[256,896]{1,0:T(8,128)(2,1)}, bf16[256,896]{1,0:T(8,128)(2,1)}, bf16[256,896]{1,0:T(8,128)(2,1)}) custom-call(bf16[16,4,16,896]{3,2,1,0:T(8,128)(2,1)} %all-to-all-done.1.own_ref, bf16[16,4,16,896]{3,2,1,0:T(8,128)(2,1)} %copy-done.4, bf16[384,7168]{1,0:T(8,128)(2,1)} %bitcast.11, ...), custom_call_target="tpu_custom_call" | custom-call | flops 1000 | bytes 1000 | tf_op jit(solution)/shard_map/first_pass/pallas_call | solution.py:334
  83.6 8.5 %hidden_last.1.grads_ref = bf16[512,768]{1,0:T(8,128)(2,1)} custom-call(bf16[8,512,896]{2,1,0:T(8,128)(2,1)} %bitcast.17, bf16[384,7168]{1,0:T(8,128)(2,1)} %bitcast.12, f32[16,64,3]{2,1,0:T(8,128)} %bitcast.15, bf16[3,16,64,128]{3,2,1,0:T(8,128)(2,1)} %bitcast.19, bf16[3,16,64,128]{3,2,1,0:T(8,128)(2,1)} %bitcast.22), custom_call_target="tpu_custom_call" | custom-call | flops 1000 | bytes 1000 | tf_op jit(solution)/shard_map/hidden_last/pallas_call | solution.py:218
  94.0 5.6 %own_pass.2 = bf16[16,4,16,896]{3,2,1,0:T(8,128)(2,1)} custom-call(bf16[256,768]{1,0:T(8,128)(2,1)} %get-tuple-element.55.grads_ref, bf16[3,7168,128]{2,1,0:T(8,128)(2,1)} %w_gate_ref.9, bf16[3,7168,128]{2,1,0:T(8,128)(2,1)} %w_up_ref.9, bf16[256,896]{1,0:T(8,128)(2,1)} %copy-done.5, bf16[256,896]{1,0:T(8,128)(2,1)} %copy-done.6, ...), custom_call_target="tpu_custom_call" | custom-call | flops 1000 | bytes 1000 | tf_op jit(solution)/shard_map/own_pass/pallas_call | solution.py:395
  99.6 3.8 %all-to-all-done.2.own_ref = bf16[16,4,16,896]{3,2,1,0:T(8,128)(2,1)} async-done(((bf16[16,4,16,896]{3,2,1,0:T(8,128)(2,1)}), bf16[16,4,16,896]{3,2,1,0:T(8,128)(2,1)}, u32[]{:S(2)}, u32[]{:S(2)}) %all-to-all-start.2) | async-done | bytes 1835040 | tf_op jit(solution)/shard_map/all_to_all | solution.py:505
  103.4 3.7 %all-to-all-start.3 = ((bf16[16,4,16,896]{3,2,1,0:T(8,128)(2,1)}), bf16[16,4,16,896]{3,2,1,0:T(8,128)(2,1)S(1)}, u32[]{:S(2)}, u32[]{:S(2)}) async-start(bf16[16,4,16,896]{3,2,1,0:T(8,128)(2,1)} %own_pass.2), calls=%async_computation.3 | async-start | bytes 3670016 | tf_op jit(solution)/shard_map/all_to_all | solution.py:505
  107.4 11.3 %back_last.1 = bf16[8,512,896]{2,1,0:T(8,128)(2,1)} custom-call(bf16[512,768]{1,0:T(8,128)(2,1)} %hidden_last.1.grads_ref, bf16[3,7168,128]{2,1,0:T(8,128)(2,1)} %w_gate_ref.9, bf16[3,7168,128]{2,1,0:T(8,128)(2,1)} %w_up_ref.9), custom_call_target="tpu_custom_call" | custom-call | flops 1000 | bytes 1000 | tf_op jit(solution)/shard_map/back_last/pallas_call | solution.py:268
  118.7 8.7 %first_pass.3 = (bf16[256,768]{1,0:T(8,128)(2,1)}, bf16[256,896]{1,0:T(8,128)(2,1)}, bf16[256,896]{1,0:T(8,128)(2,1)}, bf16[256,896]{1,0:T(8,128)(2,1)}, bf16[256,896]{1,0:T(8,128)(2,1)}) custom-call(bf16[16,4,16,896]{3,2,1,0:T(8,128)(2,1)} %all-to-all-done.2.own_ref, bf16[16,4,16,896]{3,2,1,0:T(8,128)(2,1)} %collective-permute-done.8.other_ref, ...), custom_call_target="tpu_custom_call" | custom-call | flops 1000 | bytes 1000 | tf_op jit(solution)/shard_map/first_pass/pallas_call | solution.py:334
  128.6 1.1 collective-permute-done.9.refs_0_
  130.3 1.3 collective-permute-done.11.refs_2_
  133.1 5.7 %own_pass.3 = bf16[16,4,16,896]{3,2,1,0:T(8,128)(2,1)} custom-call(bf16[256,768]{1,0:T(8,128)(2,1)} %get-tuple-element.65.grads_ref, bf16[3,7168,128]{2,1,0:T(8,128)(2,1)} %w_gate_ref.9, bf16[3,7168,128]{2,1,0:T(8,128)(2,1)} %w_up_ref.9, bf16[256,896]{1,0:T(8,128)(2,1)} %copy-done.8, bf16[256,896]{1,0:T(8,128)(2,1)} %copy-done.10, ...), custom_call_target="tpu_custom_call" | custom-call | flops 1000 | bytes 1000 | tf_op jit(solution)/shard_map/own_pass/pallas_call | solution.py:395
  138.8 1.5 copy-done.3
  140.4 32.9 %all_to_all.30.refs_3_ = bf16[16,4,16,896]{3,2,1,0:T(8,128)(2,1)} all-to-all(bf16[16,4,16,896]{3,2,1,0:T(8,128)(2,1)S(1)} %copy-done.3), channel_id=1, replica_groups=mesh['group'=16,'local'=8] {'group'}, dimensions={0} | all-to-all | bytes 3670016 | tf_op jit(solution)/shard_map/all_to_all | solution.py:505
  173.3 3.6 %all-to-all-start.5 = ((bf16[16,32,896]{2,1,0:T(8,128)(2,1)}), bf16[16,32,896]{2,1,0:T(8,128)(2,1)S(1)}, u32[]{:S(2)}, u32[]{:S(2)}) async-start(bf16[16,32,896]{2,1,0:T(8,128)(2,1)} %bitcast.25), calls=%async_computation.6 | async-start | bytes 1835008 | tf_op jit(solution)/shard_map/all_to_all | solution.py:505
  177.0 1.5 copy-done
  179.2 4.0 %collective-permute-start.13 = (bf16[128,896]{1,0:T(8,128)(2,1)S(1)}, bf16[128,896]{1,0:T(8,128)(2,1)S(1)}, u32[]{:S(2)}, u32[]{:S(2)}) collective-permute-start(bf16[128,896]{1,0:T(8,128)(2,1)S(1)} %get-tuple-element.78), channel_id=1, source_target_pairs={{0,6},{1,7},{2,0},{3,1},{4,2},{5,3},{6,4},{7,5},{8,14},{9,15},{10,... | collective-permute-start | bytes 688136 | tf_op jit(solution)/shard_map/ppermute | solution.py:499
  183.2 2.0 collective-permute-start.15
  185.2 7.0 %collective-permute-done.13.a_ref = bf16[128,896]{1,0:T(8,128)(2,1)S(1)} collective-permute-done((bf16[128,896]{1,0:T(8,128)(2,1)S(1)}, bf16[128,896]{1,0:T(8,128)(2,1)S(1)}, u32[]{:S(2)}, u32[]{:S(2)}) %collective-permute-start.13) | collective-permute-done | bytes 229408 | tf_op jit(solution)/shard_map/ppermute | solution.py:499
  192.2 3.4 %collective-permute-done.14.b_ref = bf16[128,896]{1,0:T(8,128)(2,1)S(1)} collective-permute-done((bf16[128,896]{1,0:T(8,128)(2,1)S(1)}, bf16[128,896]{1,0:T(8,128)(2,1)S(1)}, u32[]{:S(2)}, u32[]{:S(2)}) %collective-permute-start.14) | collective-permute-done | bytes 229408 | tf_op jit(solution)/shard_map/ppermute | solution.py:499
  (60 shorter events, 10.4 us)
Async XLA Ops:
  6.5 10.0 %copy-start.1 = (bf16[128,896]{1,0:T(8,128)(2,1)S(1)}, bf16[128,896]{1,0:T(8,128)(2,1)}, u32[]{:S(2)}) copy-start(bf16[128,896]{1,0:T(8,128)(2,1)} %t0.3) | copy-start | bytes 688132
  9.3 13.3 %copy-start.2 = (bf16[16,64,128]{2,1,0:T(8,128)(2,1)S(1)}, bf16[16,64,128]{2,1,0:T(8,128)(2,1)}, u32[]{:S(2)}) copy-start(bf16[16,64,128]{2,1,0:T(8,128)(2,1)} %get-tuple-element.71.table_ref) | copy-start | bytes 786436
  9.3 26.1 %all-to-all-start = ((bf16[16,40,896]{2,1,0:T(8,128)(2,1)}), bf16[16,40,896]{2,1,0:T(8,128)(2,1)S(1)}, u32[]{:S(2)}, u32[]{:S(2)}) async-start(bf16[16,40,896]{2,1,0:T(8,128)(2,1)} %get-tuple-element.44), calls=%async_computation | async-start | bytes 2293760 | tf_op jit(solution)/shard_map/all_to_all | solution.py:505
  16.5 67.1 %all-gather.3.cloned.1.call-start = ((), (), s32[]{:S(2)}) async-start(), calls=%async_computation.8 | async-start | bytes 8257536 | tf_op jit(solution)/shard_map/all_gather | solution.py:520
  16.6 10.4 %collective-permute-start.2 = (bf16[128,896]{1,0:T(8,128)(2,1)S(1)}, bf16[128,896]{1,0:T(8,128)(2,1)S(1)}, u32[]{:S(2)}, u32[]{:S(2)}) collective-permute-start(bf16[128,896]{1,0:T(8,128)(2,1)S(1)} %copy-done.1), channel_id=1, source_target_pairs={{0,4},{1,5},{2,6},{3,7},{4,0},{5,1},{6,2},{7,3},{8,12},{9,13},{10,... | collective-permute-start | bytes 688136 | tf_op jit(solution)/shard_map/ppermute | solution.py:499
  20.5 11.0 %collective-permute-start.1 = (bf16[128,896]{1,0:T(8,128)(2,1)S(1)}, bf16[128,896]{1,0:T(8,128)(2,1)S(1)}, u32[]{:S(2)}, u32[]{:S(2)}) collective-permute-start(bf16[128,896]{1,0:T(8,128)(2,1)S(1)} %copy-done.1), channel_id=1, source_target_pairs={{0,6},{1,7},{2,0},{3,1},{4,2},{5,3},{6,4},{7,5},{8,14},{9,15},{10,... | collective-permute-start | bytes 688136 | tf_op jit(solution)/shard_map/ppermute | solution.py:499
  21.2 10.3 %collective-permute-start = (bf16[128,896]{1,0:T(8,128)(2,1)S(1)}, bf16[128,896]{1,0:T(8,128)(2,1)S(1)}, u32[]{:S(2)}, u32[]{:S(2)}) collective-permute-start(bf16[128,896]{1,0:T(8,128)(2,1)S(1)} %copy-done.1), channel_id=1, source_target_pairs={{0,2},{1,3},{2,4},{3,5},{4,6},{5,7},{6,0},{7,1},{8,10},{9,11},{10,... | collective-permute-start | bytes 688136 | tf_op jit(solution)/shard_map/ppermute | solution.py:499
  36.4 31.6 %all-to-all-start.1 = ((bf16[16,4,16,896]{3,2,1,0:T(8,128)(2,1)}), bf16[16,4,16,896]{3,2,1,0:T(8,128)(2,1)}, u32[]{:S(2)}, u32[]{:S(2)}) async-start(bf16[16,4,16,896]{3,2,1,0:T(8,128)(2,1)} %spread.2), calls=%async_computation.1 | async-start | bytes 3670016 | tf_op jit(solution)/shard_map/all_to_all | solution.py:505
  68.0 4.4 %collective-permute-start.3 = (bf16[16,4,16,896]{3,2,1,0:T(8,128)(2,1)}, bf16[16,4,16,896]{3,2,1,0:T(8,128)(2,1)S(1)}, u32[]{:S(2)}, u32[]{:S(2)}) collective-permute-start(bf16[16,4,16,896]{3,2,1,0:T(8,128)(2,1)} %all-to-all-done.1.own_ref), channel_id=1, source_target_pairs={{0,1},{1,0},{2,3},{3,2},{4,5},{5,4},{6,7},{7,6},{8,9},{9,8},{10,11... | collective-permute-start | bytes 5505032 | tf_op jit(solution)/shard_map/ppermute | solution.py:502
  68.0 35.5 %all-to-all-start.2 = ((bf16[16,4,16,896]{3,2,1,0:T(8,128)(2,1)}), bf16[16,4,16,896]{3,2,1,0:T(8,128)(2,1)}, u32[]{:S(2)}, u32[]{:S(2)}) async-start(bf16[16,4,16,896]{3,2,1,0:T(8,128)(2,1)} %spread.3), calls=%async_computation.2 | async-start | bytes 3670016 | tf_op jit(solution)/shard_map/all_to_all | solution.py:505
  72.4 1.2 copy-start.4
  82.3 9.8 %collective-permute-start.4 = (bf16[256,896]{1,0:T(8,128)(2,1)}, bf16[256,896]{1,0:T(8,128)(2,1)S(1)}, u32[]{:S(2)}, u32[]{:S(2)}) collective-permute-start(bf16[256,896]{1,0:T(8,128)(2,1)} %get-tuple-element.51), channel_id=1, source_target_pairs={{0,1},{1,0},{2,3},{3,2},{4,5},{5,4},{6,7},{7,6},{8,9},{9,8},{10,11... | collective-permute-start | bytes 1376264 | tf_op jit(solution)/shard_map/ppermute | solution.py:502
  83.0 9.1 %collective-permute-start.5 = (bf16[256,896]{1,0:T(8,128)(2,1)}, bf16[256,896]{1,0:T(8,128)(2,1)S(1)}, u32[]{:S(2)}, u32[]{:S(2)}) collective-permute-start(bf16[256,896]{1,0:T(8,128)(2,1)} %get-tuple-element.52), channel_id=1, source_target_pairs={{0,1},{1,0},{2,3},{3,2},{4,5},{5,4},{6,7},{7,6},{8,9},{9,8},{10,11... | collective-permute-start | bytes 1376264 | tf_op jit(solution)/shard_map/ppermute | solution.py:502
  83.1 9.1 %collective-permute-start.6 = (bf16[256,896]{1,0:T(8,128)(2,1)}, bf16[256,896]{1,0:T(8,128)(2,1)S(1)}, u32[]{:S(2)}, u32[]{:S(2)}) collective-permute-start(bf16[256,896]{1,0:T(8,128)(2,1)} %get-tuple-element.53), channel_id=1, source_target_pairs={{0,1},{1,0},{2,3},{3,2},{4,5},{5,4},{6,7},{7,6},{8,9},{9,8},{10,11... | collective-permute-start | bytes 1376264 | tf_op jit(solution)/shard_map/ppermute | solution.py:502
  83.5 8.7 %collective-permute-start.7 = (bf16[256,896]{1,0:T(8,128)(2,1)}, bf16[256,896]{1,0:T(8,128)(2,1)S(1)}, u32[]{:S(2)}, u32[]{:S(2)}) collective-permute-start(bf16[256,896]{1,0:T(8,128)(2,1)} %get-tuple-element.54), channel_id=1, source_target_pairs={{0,1},{1,0},{2,3},{3,2},{4,5},{5,4},{6,7},{7,6},{8,9},{9,8},{10,11... | collective-permute-start | bytes 1376264 | tf_op jit(solution)/shard_map/ppermute | solution.py:502
  92.1 0.9 copy-start.6
  92.2 1.0 copy-start.7
  103.4 15.3 %collective-permute-start.8 = (bf16[16,4,16,896]{3,2,1,0:T(8,128)(2,1)}, bf16[16,4,16,896]{3,2,1,0:T(8,128)(2,1)}, u32[]{:S(2)}, u32[]{:S(2)}) collective-permute-start(bf16[16,4,16,896]{3,2,1,0:T(8,128)(2,1)} %all-to-all-done.2.own_ref), channel_id=1, source_target_pairs={{0,1},{1,0},{2,3},{3,2},{4,5},{5,4},{6,7},{7,6},{8,9},{9,8},{10,11... | collective-permute-start | bytes 5505032 | tf_op jit(solution)/shard_map/ppermute | solution.py:502
  103.4 35.4 %all-to-all-start.3 = ((bf16[16,4,16,896]{3,2,1,0:T(8,128)(2,1)}), bf16[16,4,16,896]{3,2,1,0:T(8,128)(2,1)S(1)}, u32[]{:S(2)}, u32[]{:S(2)}) async-start(bf16[16,4,16,896]{3,2,1,0:T(8,128)(2,1)} %own_pass.2), calls=%async_computation.3 | async-start | bytes 3670016 | tf_op jit(solution)/shard_map/all_to_all | solution.py:505
  107.2 66.2 %reduce-scatter.2.cloned.1.call-start = ((), (), s32[]{:S(2)}) async-start(), calls=%async_computation.7 | async-start | bytes 8257536 | tf_op jit(solution)/shard_map/reduce_scatter | solution.py:543
  127.4 2.2 %collective-permute-start.9 = (bf16[256,896]{1,0:T(8,128)(2,1)}, bf16[256,896]{1,0:T(8,128)(2,1)S(1)}, u32[]{:S(2)}, u32[]{:S(2)}) collective-permute-start(bf16[256,896]{1,0:T(8,128)(2,1)} %get-tuple-element.66), channel_id=1, source_target_pairs={{0,1},{1,0},{2,3},{3,2},{4,5},{5,4},{6,7},{7,6},{8,9},{9,8},{10,11... | collective-permute-start | bytes 1376264 | tf_op jit(solution)/shard_map/ppermute | solution.py:502
  128.0 2.3 %collective-permute-start.10 = (bf16[256,896]{1,0:T(8,128)(2,1)}, bf16[256,896]{1,0:T(8,128)(2,1)S(1)}, u32[]{:S(2)}, u32[]{:S(2)}) collective-permute-start(bf16[256,896]{1,0:T(8,128)(2,1)} %get-tuple-element.67), channel_id=1, source_target_pairs={{0,1},{1,0},{2,3},{3,2},{4,5},{5,4},{6,7},{7,6},{8,9},{9,8},{10,11... | collective-permute-start | bytes 1376264 | tf_op jit(solution)/shard_map/ppermute | solution.py:502
  128.1 3.5 %collective-permute-start.11 = (bf16[256,896]{1,0:T(8,128)(2,1)}, bf16[256,896]{1,0:T(8,128)(2,1)S(1)}, u32[]{:S(2)}, u32[]{:S(2)}) collective-permute-start(bf16[256,896]{1,0:T(8,128)(2,1)} %get-tuple-element.68), channel_id=1, source_target_pairs={{0,1},{1,0},{2,3},{3,2},{4,5},{5,4},{6,7},{7,6},{8,9},{9,8},{10,11... | collective-permute-start | bytes 1376264 | tf_op jit(solution)/shard_map/ppermute | solution.py:502
  128.5 3.8 %collective-permute-start.12 = (bf16[256,896]{1,0:T(8,128)(2,1)}, bf16[256,896]{1,0:T(8,128)(2,1)S(1)}, u32[]{:S(2)}, u32[]{:S(2)}) collective-permute-start(bf16[256,896]{1,0:T(8,128)(2,1)} %get-tuple-element.69), channel_id=1, source_target_pairs={{0,1},{1,0},{2,3},{3,2},{4,5},{5,4},{6,7},{7,6},{8,9},{9,8},{10,11... | collective-permute-start | bytes 1376264 | tf_op jit(solution)/shard_map/ppermute | solution.py:502
  129.7 2.6 %copy-start.8 = (bf16[256,896]{1,0:T(8,128)(2,1)}, bf16[256,896]{1,0:T(8,128)(2,1)S(1)}, u32[]{:S(2)}) copy-start(bf16[256,896]{1,0:T(8,128)(2,1)S(1)} %collective-permute-done.9.refs_0_) | copy-start | bytes 1376260
  130.3 2.0 copy-start.10
  138.8 1.6 copy-start.3
  173.3 22.3 %all-to-all-start.5 = ((bf16[16,32,896]{2,1,0:T(8,128)(2,1)}), bf16[16,32,896]{2,1,0:T(8,128)(2,1)S(1)}, u32[]{:S(2)}, u32[]{:S(2)}) async-start(bf16[16,32,896]{2,1,0:T(8,128)(2,1)} %bitcast.25), calls=%async_computation.6 | async-start | bytes 1835008 | tf_op jit(solution)/shard_map/all_to_all | solution.py:505
  176.9 1.5 copy-start
  179.2 13.0 %collective-permute-start.13 = (bf16[128,896]{1,0:T(8,128)(2,1)S(1)}, bf16[128,896]{1,0:T(8,128)(2,1)S(1)}, u32[]{:S(2)}, u32[]{:S(2)}) collective-permute-start(bf16[128,896]{1,0:T(8,128)(2,1)S(1)} %get-tuple-element.78), channel_id=1, source_target_pairs={{0,6},{1,7},{2,0},{3,1},{4,2},{5,3},{6,4},{7,5},{8,14},{9,15},{10,... | collective-permute-start | bytes 688136 | tf_op jit(solution)/shard_map/ppermute | solution.py:499
  183.2 12.4 %collective-permute-start.14 = (bf16[128,896]{1,0:T(8,128)(2,1)S(1)}, bf16[128,896]{1,0:T(8,128)(2,1)S(1)}, u32[]{:S(2)}, u32[]{:S(2)}) collective-permute-start(bf16[128,896]{1,0:T(8,128)(2,1)S(1)} %get-tuple-element.79), channel_id=1, source_target_pairs={{0,2},{1,3},{2,4},{3,5},{4,6},{5,7},{6,0},{7,1},{8,10},{9,11},{10,... | collective-permute-start | bytes 688136 | tf_op jit(solution)/shard_map/ppermute | solution.py:499
  183.2 12.4 %collective-permute-start.15 = (bf16[128,896]{1,0:T(8,128)(2,1)S(1)}, bf16[128,896]{1,0:T(8,128)(2,1)S(1)}, u32[]{:S(2)}, u32[]{:S(2)}) collective-permute-start(bf16[128,896]{1,0:T(8,128)(2,1)S(1)} %get-tuple-element.80), channel_id=1, source_target_pairs={{0,4},{1,5},{2,6},{3,7},{4,0},{5,1},{6,2},{7,3},{8,12},{9,13},{10,... | collective-permute-start | bytes 688136 | tf_op jit(solution)/shard_map/ppermute | solution.py:499
  (4 other events, 3.1 us)
Sparse Core Ops, SparseCore 0:
  36.5 44.5 all-gather.2
  118.8 50.0 reduce-scatter.1
